TPU v7x, 32 devices: a whole 2x2x4 slice. The times are simulated.
32 devices in a mesh: group: 4 (over y, core), wide: 8 (over z, x).
Axes of the slice: x: 2, y: 2, z: 4, core: 2. Of those that a mesh axis runs over, the one named last changes fastest.
Arguments:
- tokens: bfloat16 [32768, 1024], P(('group', 'wide')), may hold values from -6 to 6
- cotangent: bfloat16 [32768, 1024], P(('group', 'wide')), may hold values from -6 to 6
- noise_index: int32 [256], P(('group', 'wide')), may hold values from 0 to 255
- time_embed: bfloat16 [256, 1024], replicated, may hold values from -6 to 6
- ln1_gain: bfloat16 [1024], P('wide'), may hold values from 0.5 to 1.5
- ln1_shift: bfloat16 [1024], P('wide'), may hold values from -1.75 to 1.75
- w_qkv: bfloat16 [1024, 3072], P('wide'), may hold values from -0.1875 to 0.1875
- w_out: bfloat16 [1024, 1024], P('wide'), may hold values from -2 to 2
- ln2_gain: bfloat16 [1024], P('wide'), may hold values from 0.5 to 1.5
- ln2_shift: bfloat16 [1024], P('wide'), may hold values from -1.75 to 1.75
- w_time: bfloat16 [1024, 1024], P('wide'), may hold values from -0.1875 to 0.1875
- w_up: bfloat16 [1024, 4096], P('wide'), may hold values from -0.1875 to 0.1875
- up_bias: bfloat16 [4096], P('wide'), may hold values from -1.75 to 1.75
- w_down: bfloat16 [4096, 1024], P('wide'), may hold values from -0.09375 to 0.09375
- down_bias: bfloat16 [1024], P('wide'), may hold values from -1.75 to 1.75
Outputs:
- output: bfloat16 [32768, 1024], P(('group', 'wide'))
- grad_tokens: float32 [32768, 1024], P(('group', 'wide'))
- grad_ln1_gain: float32 [1024], P('wide')
- grad_ln1_shift: float32 [1024], P('wide')
- grad_w_qkv: float32 [1024, 3072], P('wide')
- grad_w_out: float32 [1024, 1024], P('wide')
- grad_ln2_gain: float32 [1024], P('wide')
- grad_ln2_shift: float32 [1024], P('wide')
- grad_w_time: float32 [1024, 1024], P('wide')
- grad_w_up: float32 [1024, 4096], P('wide')
- grad_up_bias: float32 [4096], P('wide')
- grad_w_down: float32 [4096, 1024], P('wide')
- grad_down_bias: float32 [1024], P('wide')
Inputs may be any that keep to these rules, and one draw needn't show every extreme that they name: `noise_index`: the row of time_embed that each sequence uses.
All inputs are finite; a program needn't handle non-finite values.
Results may differ from a plain program's by a relative error of at most 0.015.
Values may be sent and summed in bfloat16 or wider, within the bound.
No kernel may reach another device: no remote copies, remote signals or barrier semaphores. Data moves between devices by JAX's collectives and lax.ppermute only.
A program may use at most 256 MiB of HBM per device.

v0:
```python
import math

import jax
import jax.numpy as jnp
from jax import lax
from jax.sharding import PartitionSpec as P

HEAD_DIM = 64


EPSILON = 1e-05


def layer_norm(values, gain_vec, shift_vec):
    average = jnp.mean(values, axis=-1, keepdims=True)
    centered = values - average
    variance = jnp.mean(centered * centered, axis=-1, keepdims=True)
    return centered * lax.rsqrt(variance + EPSILON) * gain_vec + shift_vec


def rotary_tables(length, head_size):
    half_dim = head_size // 2
    frequency = jnp.exp(
        jnp.arange(half_dim, dtype=jnp.float32) * (-2.0 * math.log(10000.0) / head_size)
    )
    angles = jnp.arange(length, dtype=jnp.float32)[:, None] * frequency[None, :]
    angles = jnp.concatenate([angles, angles], axis=1)
    return (jnp.cos(angles), jnp.sin(angles))


def rotate_half(values):
    half_dim = values.shape[-1] // 2
    return jnp.concatenate([-values[..., half_dim:], values[..., :half_dim]], axis=-1)


def rotate(values, cosine, sine_table):
    return values * cosine + rotate_half(values) * sine_table


def rotate_back(values, cosine, sine_table):
    return values * cosine - rotate_half(values * sine_table)


def exact_gelu(values):
    return jax.nn.gelu(values, approximate=False)


def attention_scores(queries, key_rows, factor):
    return (
        jnp.einsum("bqhd,bkhd->bhqk", queries, key_rows, preferred_element_type=jnp.float32)
        * factor
    )


def shards(
    tokens,
    cotangent,
    noise_index,
    time_embed,
    ln1_gain,
    ln1_shift,
    w_qkv,
    w_out,
    ln2_gain,
    ln2_shift,
    w_time,
    w_up,
    up_bias,
    w_down,
    down_bias,
):
    row_count, model_width = tokens.shape
    seq_count = noise_index.shape[0]
    length = row_count // seq_count
    head_count = model_width // HEAD_DIM
    factor = HEAD_DIM ** (-0.5)
    attn_full = (
        lax.all_gather(ln1_gain, "wide", axis=0, tiled=True),
        lax.all_gather(ln1_shift, "wide", axis=0, tiled=True),
        lax.all_gather(w_qkv, "wide", axis=0, tiled=True),
        lax.all_gather(w_out, "wide", axis=0, tiled=True),
    )
    gain_one = attn_full[0].astype(jnp.float32)
    shift_one = attn_full[1].astype(jnp.float32)
    inputs = tokens.astype(jnp.float32)
    normed_one = layer_norm(inputs, gain_one, shift_one)
    act_one = normed_one.astype(jnp.bfloat16)
    projected = jnp.dot(act_one, attn_full[2], preferred_element_type=jnp.float32)
    projected = projected.reshape(seq_count, length, 3, head_count, HEAD_DIM)
    cosine, sine_table = rotary_tables(length, HEAD_DIM)
    cosine = cosine[None, :, None, :]
    sine_table = sine_table[None, :, None, :]
    queries = rotate(projected[:, :, 0], cosine, sine_table).astype(jnp.bfloat16)
    key_rows = rotate(projected[:, :, 1], cosine, sine_table).astype(jnp.bfloat16)
    value_rows = projected[:, :, 2].astype(jnp.bfloat16)
    scores = attention_scores(queries, key_rows, factor)
    row_max = jnp.max(scores, axis=-1, keepdims=True)
    log_total = row_max + jnp.log(jnp.sum(jnp.exp(scores - row_max), axis=-1, keepdims=True))
    probs_low = jnp.exp(scores - log_total).astype(jnp.bfloat16)
    attended = jnp.einsum(
        "bhqk,bkhd->bqhd", probs_low, value_rows, preferred_element_type=jnp.float32
    )
    attended = attended.reshape(row_count, model_width).astype(jnp.bfloat16)
    middle = inputs + jnp.dot(attended, attn_full[3], preferred_element_type=jnp.float32)
    mlp_full = (
        lax.all_gather(ln2_gain, "wide", axis=0, tiled=True),
        lax.all_gather(ln2_shift, "wide", axis=0, tiled=True),
        lax.all_gather(w_time, "wide", axis=0, tiled=True),
        lax.all_gather(w_up, "wide", axis=0, tiled=True),
        lax.all_gather(up_bias, "wide", axis=0, tiled=True),
        lax.all_gather(w_down, "wide", axis=0, tiled=True),
        lax.all_gather(down_bias, "wide", axis=0, tiled=True),
    )
    gain_two = mlp_full[0].astype(jnp.float32)
    shift_two = mlp_full[1].astype(jnp.float32)
    normed_two = layer_norm(middle, gain_two, shift_two)
    level_count = time_embed.shape[0]
    selector = (noise_index[:, None] == jnp.arange(level_count, dtype=jnp.int32)[None, :]).astype(
        jnp.bfloat16
    )
    embedded = jnp.dot(selector, time_embed, preferred_element_type=jnp.float32).astype(
        jnp.bfloat16
    )
    channel_scale = 1.0 + jnp.dot(embedded, mlp_full[2], preferred_element_type=jnp.float32)
    normed_seq = normed_two.reshape(seq_count, length, model_width)
    act_two = (
        (normed_seq * channel_scale[:, None, :])
        .reshape(row_count, model_width)
        .astype(jnp.bfloat16)
    )
    pre_act = jnp.dot(act_two, mlp_full[3], preferred_element_type=jnp.float32) + mlp_full[
        4
    ].astype(jnp.float32)
    hidden_low = exact_gelu(pre_act).astype(jnp.bfloat16)
    output = (
        middle
        + jnp.dot(hidden_low, mlp_full[5], preferred_element_type=jnp.float32)
        + mlp_full[6].astype(jnp.float32)
    )
    attn_back = (
        lax.all_gather(ln1_gain, "wide", axis=0, tiled=True),
        lax.all_gather(ln1_shift, "wide", axis=0, tiled=True),
        lax.all_gather(w_qkv, "wide", axis=0, tiled=True),
        lax.all_gather(w_out, "wide", axis=0, tiled=True),
    )
    mlp_back = (
        lax.all_gather(ln2_gain, "wide", axis=0, tiled=True),
        lax.all_gather(ln2_shift, "wide", axis=0, tiled=True),
        lax.all_gather(w_time, "wide", axis=0, tiled=True),
        lax.all_gather(w_up, "wide", axis=0, tiled=True),
        lax.all_gather(up_bias, "wide", axis=0, tiled=True),
        lax.all_gather(w_down, "wide", axis=0, tiled=True),
        lax.all_gather(down_bias, "wide", axis=0, tiled=True),
    )
    grad_out = cotangent.astype(jnp.float32)
    grad_out_low = grad_out.astype(jnp.bfloat16)
    grad_down_bias = jnp.sum(grad_out_low.astype(jnp.float32), axis=0)
    grad_w_down = jnp.einsum(
        "rf,rd->fd", hidden_low, grad_out_low, preferred_element_type=jnp.float32
    )
    grad_hidden = jnp.einsum(
        "rd,fd->rf", grad_out_low, mlp_back[5], preferred_element_type=jnp.float32
    )
    unused_gelu, gelu_back = jax.vjp(exact_gelu, pre_act)
    grad_pre = gelu_back(grad_hidden)[0].astype(jnp.bfloat16)
    grad_up_bias = jnp.sum(grad_pre.astype(jnp.float32), axis=0)
    grad_w_up = jnp.einsum("rd,rf->df", act_two, grad_pre, preferred_element_type=jnp.float32)
    grad_scaled = jnp.einsum("rf,df->rd", grad_pre, mlp_back[3], preferred_element_type=jnp.float32)
    grad_seq = grad_scaled.reshape(seq_count, length, model_width)
    grad_scale = jnp.sum(grad_seq * normed_seq, axis=1).astype(jnp.bfloat16)
    grad_w_time = jnp.einsum("sd,se->de", embedded, grad_scale, preferred_element_type=jnp.float32)
    grad_normed_two = (grad_seq * channel_scale[:, None, :]).reshape(row_count, model_width)
    unused_two, norm_two_back = jax.vjp(
        layer_norm, middle, mlp_back[0].astype(jnp.float32), mlp_back[1].astype(jnp.float32)
    )
    grad_mid_norm, grad_gain_two, grad_shift_two = norm_two_back(grad_normed_two)
    grad_middle = grad_out + grad_mid_norm
    mlp_shards = (
        lax.psum_scatter(grad_gain_two, "wide", scatter_dimension=0, tiled=True),
        lax.psum_scatter(grad_shift_two, "wide", scatter_dimension=0, tiled=True),
        lax.psum_scatter(grad_w_time, "wide", scatter_dimension=0, tiled=True),
        lax.psum_scatter(grad_w_up, "wide", scatter_dimension=0, tiled=True),
        lax.psum_scatter(grad_up_bias, "wide", scatter_dimension=0, tiled=True),
        lax.psum_scatter(grad_w_down, "wide", scatter_dimension=0, tiled=True),
        lax.psum_scatter(grad_down_bias, "wide", scatter_dimension=0, tiled=True),
    )
    grad_branch = grad_middle.astype(jnp.bfloat16)
    grad_w_out = jnp.einsum("rd,re->de", attended, grad_branch, preferred_element_type=jnp.float32)
    grad_attended = jnp.einsum(
        "re,de->rd", grad_branch, attn_back[3], preferred_element_type=jnp.float32
    )
    grad_attended = grad_attended.astype(jnp.bfloat16).reshape(
        seq_count, length, head_count, HEAD_DIM
    )
    scores_again = attention_scores(queries, key_rows, factor)
    probs_again = jnp.exp(scores_again - log_total)
    grad_values = jnp.einsum(
        "bhqk,bqhd->bkhd",
        probs_again.astype(jnp.bfloat16),
        grad_attended,
        preferred_element_type=jnp.float32,
    )
    grad_probs = jnp.einsum(
        "bqhd,bkhd->bhqk", grad_attended, value_rows, preferred_element_type=jnp.float32
    )
    row_inner = jnp.sum(grad_probs * probs_again, axis=-1, keepdims=True)
    grad_scores = (probs_again * (grad_probs - row_inner)).astype(jnp.bfloat16)
    grad_queries = (
        jnp.einsum("bhqk,bkhd->bqhd", grad_scores, key_rows, preferred_element_type=jnp.float32)
        * factor
    )
    grad_keys = (
        jnp.einsum("bhqk,bqhd->bkhd", grad_scores, queries, preferred_element_type=jnp.float32)
        * factor
    )
    grad_queries = rotate_back(grad_queries, cosine, sine_table)
    grad_keys = rotate_back(grad_keys, cosine, sine_table)
    grad_projected = jnp.stack([grad_queries, grad_keys, grad_values], axis=2)
    grad_projected = grad_projected.reshape(row_count, 3 * model_width).astype(jnp.bfloat16)
    grad_w_qkv = jnp.einsum(
        "rd,re->de", act_one, grad_projected, preferred_element_type=jnp.float32
    )
    grad_normed_one = jnp.einsum(
        "re,de->rd", grad_projected, attn_back[2], preferred_element_type=jnp.float32
    )
    unused_one, norm_one_back = jax.vjp(
        layer_norm, inputs, attn_back[0].astype(jnp.float32), attn_back[1].astype(jnp.float32)
    )
    grad_in_norm, grad_gain_one, grad_shift_one = norm_one_back(grad_normed_one)
    grad_tokens = grad_middle + grad_in_norm
    attn_shards = (
        lax.psum_scatter(grad_gain_one, "wide", scatter_dimension=0, tiled=True),
        lax.psum_scatter(grad_shift_one, "wide", scatter_dimension=0, tiled=True),
        lax.psum_scatter(grad_w_qkv, "wide", scatter_dimension=0, tiled=True),
        lax.psum_scatter(grad_w_out, "wide", scatter_dimension=0, tiled=True),
    )
    summed = (
        lax.psum(attn_shards[0].astype(jnp.bfloat16), "group").astype(jnp.float32),
        lax.psum(attn_shards[1].astype(jnp.bfloat16), "group").astype(jnp.float32),
        lax.psum(attn_shards[2].astype(jnp.bfloat16), "group").astype(jnp.float32),
        lax.psum(attn_shards[3].astype(jnp.bfloat16), "group").astype(jnp.float32),
        lax.psum(mlp_shards[0].astype(jnp.bfloat16), "group").astype(jnp.float32),
        lax.psum(mlp_shards[1].astype(jnp.bfloat16), "group").astype(jnp.float32),
        lax.psum(mlp_shards[2].astype(jnp.bfloat16), "group").astype(jnp.float32),
        lax.psum(mlp_shards[3].astype(jnp.bfloat16), "group").astype(jnp.float32),
        lax.psum(mlp_shards[4].astype(jnp.bfloat16), "group").astype(jnp.float32),
        lax.psum(mlp_shards[5].astype(jnp.bfloat16), "group").astype(jnp.float32),
        lax.psum(mlp_shards[6].astype(jnp.bfloat16), "group").astype(jnp.float32),
    )
    return (
        output.astype(jnp.bfloat16),
        grad_tokens,
        summed[0],
        summed[1],
        summed[2],
        summed[3],
        summed[4],
        summed[5],
        summed[6],
        summed[7],
        summed[8],
        summed[9],
        summed[10],
    )


def solution(mesh):
    in_specs = (
        P(("group", "wide"), None),
        P(("group", "wide"), None),
        P(("group", "wide")),
        P(),
        P("wide"),
        P("wide"),
        P("wide", None),
        P("wide", None),
        P("wide"),
        P("wide"),
        P("wide", None),
        P("wide", None),
        P("wide"),
        P("wide", None),
        P("wide"),
    )
    out_specs = (
        P(("group", "wide"), None),
        P(("group", "wide"), None),
        P("wide"),
        P("wide"),
        P("wide", None),
        P("wide", None),
        P("wide"),
        P("wide"),
        P("wide", None),
        P("wide", None),
        P("wide"),
        P("wide", None),
        P("wide"),
    )
    return jax.shard_map(shards, mesh=mesh, in_specs=in_specs, out_specs=out_specs, check_vma=False)
```

profile of v0, /device:TPU:9, one launch (start us, length us, event | category | flops | bytes accessed | tf_op | source)
XLA Modules:
  0.0 1590.8 jit_solution(17770523573740564435)
XLA Ops:
  11.3 14.9 all-gather
  26.2 12.3 all-gather.1
  38.6 15.1 all-gather.2
  53.7 12.7 all-gather.3
  66.5 23.8 %all-gather.4 = bf16[8,1,512]{2,1,0:T(2,128)(2,1)S(1)} all-gather(bf16[1,1,512]{2,1,0:T(2,128)(2,1)S(1)} %reshape.176), channel_id=1, replica_groups=mesh['group'=4,'wide'=8] {'wide'}, dimensions={0}, use_global_device_ids=true | all-gather | bytes 9216 | tf_op jit(solution)/shard_map/all_gather | solution.py:110
  95.0 63.4 %all-gather.12.cloned.1.call-done = bf16[1024,3072]{1,0:T(8,128)(2,1)} async-done(((bf16[128,3072]{1,0:T(8,128)(2,1)}), bf16[1024,3072]{1,0:T(8,128)(2,1)}) %all-gather.12.cloned.1.call-update) | async-done | bytes 6291472 | tf_op jit(solution)/shard_map/all_gather | solution.py:80
  158.4 13.0 convolution_bitcast_fusion
  171.5 12.3 copy.75
  186.4 7.4 slice_bitcast_fusion.1
  193.8 5.9 slice_negate_fusion.2
  223.4 110.2 %all-gather.18.cloned.1.call-done = bf16[1024,4096]{1,0:T(8,128)(2,1)} async-done(((bf16[128,4096]{1,0:T(8,128)(2,1)}), bf16[1024,4096]{1,0:T(8,128)(2,1)}) %all-gather.18.cloned.1.call-update) | async-done | bytes 8388624 | tf_op jit(solution)/shard_map/all_gather | solution.py:109
  333.6 16.2 %fusion.73 = f32[1024,4096]{1,0:T(8,128)} fusion(bf16[1024,1024]{1,0:T(8,128)(2,1)} %fusion.24, bf16[1024,4096]{1,0:T(8,128)(2,1)} %all-gather.18.cloned.1.call-done), kind=kOutput, calls=%fused_computation.140 | convolution fusion | flops 8589934592 | bytes 27262976 | tf_op jit(solution)/shard_map/dot_general | solution.py:131
  349.8 108.9 %all-gather.20.cloned.1.call-done = bf16[4096,1024]{1,0:T(8,128)(2,1)} async-done(((bf16[512,1024]{1,0:T(8,128)(2,1)}), bf16[4096,1024]{1,0:T(8,128)(2,1)}) %all-gather.20.cloned.1.call-update) | async-done | bytes 8388624 | tf_op jit(solution)/shard_map/all_gather | solution.py:111
  458.7 51.9 %convert_reduce_fusion = (f32[4096]{0:T(1024)}, bf16[1024,4096]{1,0:T(8,128)(2,1)}, f32[1024,4096]{1,0:T(8,128)}) fusion(f32[1024,4096]{1,0:T(8,128)} %fusion.73, f32[4096]{0:T(1024)S(1)} %bitcast.138, bf16[1024,1024]{1,0:T(8,128)(2,1)S(1)} %copy-done.17, bf16[4096,1024]{1,0:T(8,128)(2,1)} %all-gather.20.cloned.1.call-done), kind=kOutput, calls=%fused_computation.2 | convolution fusion | flops 8904503296 | bytes 52461568 | tf_op jit(solution)/shard_map/rd,fd->rf/dot_general | solution.py:161
  510.7 15.9 multiply_reduce_fusion.2
  553.3 5.0 copy.59
  558.3 6.8 multiply_reduce_fusion
  565.1 5.0 multiply_convert_fusion.1
  594.1 12.9 copy.66
  609.8 10.3 fusion.6
  620.2 12.3 multiply_convert_fusion
  635.7 11.5 fusion.75
  647.3 16.4 %fusion.74 = f32[1024,4096]{1,0:T(8,128)} fusion(bf16[1024,1024]{1,0:T(8,128)(2,1)} %fusion.24, bf16[1024,4096]{1,0:T(8,128)(2,1)} %get-tuple-element.38), kind=kOutput, calls=%fused_computation.141 | convolution fusion | flops 8589934592 | bytes 27262976 | tf_op jit(solution)/shard_map/rd,rf->df/dot_general | solution.py:167
  666.3 13.7 all-gather.5
  680.0 11.6 fusion.69
  698.0 28.0 %all-reduce.6 = (bf16[1024]{0:T(1024)(128)(2,1)S(1)}, bf16[1024]{0:T(1024)(128)(2,1)S(1)}, bf16[1024]{0:T(1024)(128)(2,1)S(1)}, bf16[1024]{0:T(1024)(128)(2,1)S(...) all-reduce(f32[1024]{0:T(1024)S(1)} %get-tuple-element.15, ...), channel_id=2, replica_groups=mesh['group'=4,'wide'=8] {'wide'}, use_global_device_ids=true, to_apply=%region_12.0.clone | all-reduce | flops 9216 | bytes 55296
  726.4 15.9 all-reduce.7
  749.0 177.2 %reduce-scatter.6.cloned.1.call-done = f32[128,3072]{1,0:T(8,128)} async-done(((f32[1024,3072]{1,0:T(8,128)}), f32[128,3072]{1,0:T(8,128)}) %reduce-scatter.6.cloned.1.call-update) | async-done | bytes 1572880 | tf_op jit(solution)/shard_map/reduce_scatter | solution.py:234
  928.6 283.2 %reduce-scatter.14.cloned.1.call-done = f32[512,1024]{1,0:T(8,128)} async-done(((f32[4096,1024]{1,0:T(8,128)}), f32[512,1024]{1,0:T(8,128)}) %reduce-scatter.14.cloned.1.call-update) | async-done | bytes 2097168 | tf_op jit(solution)/shard_map/reduce_scatter | solution.py:184
  1214.5 282.6 %reduce-scatter.12.cloned.1.call-done = f32[128,4096]{1,0:T(8,128)} async-done(((f32[1024,4096]{1,0:T(8,128)}), f32[128,4096]{1,0:T(8,128)}) %reduce-scatter.12.cloned.1.call-update) | async-done | bytes 2097168 | tf_op jit(solution)/shard_map/reduce_scatter | solution.py:182
  1499.9 15.3 add_convert_fusion.1
  1515.1 59.5 %all-reduce.11.cloned.1.call-done = (bf16[128,3072]{1,0:T(8,128)(2,1)}, bf16[128,1024]{1,0:T(8,128)(2,1)}, bf16[128,1024]{1,0:T(8,128)(2,1)}, bf16[128,4096]{1,0:T(8,128)(2,1)}, bf16[512,1024]{1,0:T(8,128)(2,1)}) async-done(((bf16[128,3072]{1,0:T(8,128)(2,1)}, bf16[128,1024]{1,0:T(8,128)(2,1)}, bf16[128,1024]{1,0:T(8,128)(2,1)}, bf16[128,4096]{1,0:T(8,128)(2,1)}, bf16[512,1024]{1,0:T(8,128)(2,1)}), ...) | async-done | bytes 3407888 | tf_op jit(solution)/shard_map/psum | solution.py:240
  (235 shorter events, 123.2 us)
Async XLA Ops:
  7.2 85.6 %copy-start = (bf16[256,1024]{1,0:T(8,128)(2,1)S(1)}, bf16[256,1024]{1,0:T(8,128)(2,1)}, u32[]{:S(2)}) copy-start(bf16[256,1024]{1,0:T(8,128)(2,1)} %param.18) | copy-start | bytes 1572868
  7.2 83.9 %copy-start.7 = (bf16[1024,1024]{1,0:T(8,128)(2,1)S(1)}, bf16[1024,1024]{1,0:T(8,128)(2,1)}, u32[]{:S(2)}) copy-start(bf16[1024,1024]{1,0:T(8,128)(2,1)} %param.15) | copy-start | bytes 6291460
  7.2 85.6 %copy-start.60 = (s32[8]{0:T(128)S(1)}, s32[8]{0:T(128)}, u32[]{:S(2)}) copy-start(s32[8]{0:T(128)} %param.17) | copy-start | bytes 100
  7.2 85.8 %all-gather.16.cloned.1.call-start = ((), (), s32[]{:S(2)}) async-start(), calls=%async_computation.7 | async-start | bytes 2359296 | tf_op jit(solution)/shard_map/all_gather | solution.py:108
  8.0 150.5 %all-gather.12.cloned.1.call-start = ((), (), s32[]{:S(2)}) async-start(), calls=%async_computation.5 | async-start | bytes 7077888 | tf_op jit(solution)/shard_map/all_gather | solution.py:80
  8.7 205.6 %all-gather.14.cloned.1.call-start = ((), (), s32[]{:S(2)}) async-start(), calls=%async_computation.6 | async-start | bytes 2359296 | tf_op jit(solution)/shard_map/all_gather | solution.py:81
  9.4 324.1 %all-gather.18.cloned.1.call-start = ((), (), s32[]{:S(2)}) async-start(), calls=%async_computation.8 | async-start | bytes 9437184 | tf_op jit(solution)/shard_map/all_gather | solution.py:109
  10.0 448.7 %all-gather.20.cloned.1.call-start = ((), (), s32[]{:S(2)}) async-start(), calls=%async_computation.9 | async-start | bytes 9437184 | tf_op jit(solution)/shard_map/all_gather | solution.py:111
  10.6 734.9 %reduce-scatter.8.cloned.1.call-start = ((), (), s32[]{:S(2)}) async-start(), calls=%async_computation.11 | async-start | bytes 4718592 | tf_op jit(solution)/shard_map/reduce_scatter | solution.py:235
  26.2 145.3 %copy-start.43 = (f32[8,1,128]{2,1,0:T(1,128)}, f32[8,1,128]{2,1,0:T(1,128)S(1)}, u32[]{:S(2)}) copy-start(f32[8,1,128]{2,1,0:T(1,128)S(1)} %convert_element_type.204) | copy-start | bytes 12292
  38.6 132.9 %copy-start.58 = (f32[8,1,128]{2,1,0:T(1,128)}, f32[8,1,128]{2,1,0:T(1,128)S(1)}, u32[]{:S(2)}) copy-start(f32[8,1,128]{2,1,0:T(1,128)S(1)} %convert_element_type.205) | copy-start | bytes 12292
  53.7 166.0 %copy-start.39 = (f32[8,1,128]{2,1,0:T(1,128)}, f32[8,1,128]{2,1,0:T(1,128)S(1)}, u32[]{:S(2)}) copy-start(f32[8,1,128]{2,1,0:T(1,128)S(1)} %convert_element_type.206) | copy-start | bytes 12292
  66.5 153.2 %copy-start.49 = (f32[8,1,128]{2,1,0:T(1,128)}, f32[8,1,128]{2,1,0:T(1,128)S(1)}, u32[]{:S(2)}) copy-start(f32[8,1,128]{2,1,0:T(1,128)S(1)} %convert_element_type.207) | copy-start | bytes 12292
  91.5 80.0 %copy-start.37 = (f32[1024]{0:T(1024)}, f32[1024]{0:T(1024)S(1)}, u32[]{:S(2)}) copy-start(f32[1024]{0:T(1024)S(1)} %broadcast_multiply_fusion.3) | copy-start | bytes 12292
  92.8 78.7 %copy-start.45 = (f32[1024]{0:T(1024)}, f32[1024]{0:T(1024)S(1)}, u32[]{:S(2)}) copy-start(f32[1024]{0:T(1024)S(1)} %fusion.62) | copy-start | bytes 12292
  93.0 78.5 %copy-start.31 = (bf16[8,1024]{1,0:T(8,128)(2,1)}, bf16[8,1024]{1,0:T(8,128)(2,1)S(1)}, u32[]{:S(2)}) copy-start(bf16[8,1024]{1,0:T(8,128)(2,1)S(1)} %convolution_convert_fusion.1) | copy-start | bytes 49156
  95.0 124.7 %copy-start.29 = (f32[8,1024]{1,0:T(8,128)}, f32[8,1024]{1,0:T(8,128)S(1)}, u32[]{:S(2)}) copy-start(f32[8,1024]{1,0:T(8,128)S(1)} %convolution_add_fusion) | copy-start | bytes 98308
  186.4 22.6 %copy-start.13 = (bf16[8,128,1,16,64]{1,0,4,3,2:T(8,128)(2,1)}, bf16[8,128,1,16,64]{1,0,4,3,2:T(8,128)(2,1)S(1)}, u32[]{:S(2)}) copy-start(bf16[8,128,1,16,64]{1,0,4,3,2:T(8,128)(2,1)S(1)} %slice.45) | copy-start | bytes 6291460
  219.7 130.1 %copy-start.53 = (f32[1024]{0:T(1024)}, f32[1024]{0:T(1024)S(1)}, u32[]{:S(2)}) copy-start(f32[1024]{0:T(1024)S(1)} %multiply_reduce_fusion.4) | copy-start | bytes 12292
  219.7 130.1 %copy-start.41 = (f32[1024]{0:T(1024)}, f32[1024]{0:T(1024)S(1)}, u32[]{:S(2)}) copy-start(f32[1024]{0:T(1024)S(1)} %fusion.63) | copy-start | bytes 12292
  223.4 235.3 %copy-start.17 = (bf16[1024,1024]{1,0:T(8,128)(2,1)S(1)}, bf16[1024,1024]{1,0:T(8,128)(2,1)}, u32[]{:S(2)}) copy-start(bf16[1024,1024]{1,0:T(8,128)(2,1)} %param.16) | copy-start | bytes 6291460
  458.7 52.0 %copy-start.4 = (f32[1024,1024]{1,0:T(8,128)S(1)}, f32[1024,1024]{1,0:T(8,128)}, u32[]{:S(2)}) copy-start(f32[1024,1024]{1,0:T(8,128)} %copy-done.3) | copy-start | bytes 12582916
  458.7 52.0 %copy-start.30 = (f32[8,1024]{1,0:T(8,128)S(1)}, f32[8,1024]{1,0:T(8,128)}, u32[]{:S(2)}) copy-start(f32[8,1024]{1,0:T(8,128)} %copy-done.29) | copy-start | bytes 98308
  458.7 52.0 %copy-start.36 = (f32[1024]{0:T(1024)S(1)}, f32[1024]{0:T(1024)}, u32[]{:S(2)}) copy-start(f32[1024]{0:T(1024)} %copy-done.35) | copy-start | bytes 12292
  458.7 52.0 %copy-start.40 = (f32[8,1,128]{2,1,0:T(1,128)S(1)}, f32[8,1,128]{2,1,0:T(1,128)}, u32[]{:S(2)}) copy-start(f32[8,1,128]{2,1,0:T(1,128)} %copy-done.39) | copy-start | bytes 12292
  458.7 52.0 %copy-start.42 = (f32[1024]{0:T(1024)S(1)}, f32[1024]{0:T(1024)}, u32[]{:S(2)}) copy-start(f32[1024]{0:T(1024)} %copy-done.41) | copy-start | bytes 12292
  510.7 15.9 copy-start.54
  536.4 210.8 %reduce-scatter.10.cloned.1.call-start = ((), (), s32[]{:S(2)}) async-start(), calls=%async_computation.12 | async-start | bytes 4718592 | tf_op jit(solution)/shard_map/reduce_scatter | solution.py:181
  544.5 381.8 %reduce-scatter.6.cloned.1.call-start = ((), (), s32[]{:S(2)}) async-start(), calls=%async_computation.10 | async-start | bytes 14155776 | tf_op jit(solution)/shard_map/reduce_scatter | solution.py:234
  620.1 591.7 %reduce-scatter.14.cloned.1.call-start = ((), (), s32[]{:S(2)}) async-start(), calls=%async_computation.14 | async-start | bytes 18874368 | tf_op jit(solution)/shard_map/reduce_scatter | solution.py:184
  647.3 849.9 %reduce-scatter.12.cloned.1.call-start = ((), (), s32[]{:S(2)}) async-start(), calls=%async_computation.13 | async-start | bytes 18874368 | tf_op jit(solution)/shard_map/reduce_scatter | solution.py:182
  663.8 910.9 %all-reduce.11.cloned.1.call-start = ((), (), s32[]{:S(2)}) async-start(), calls=%async_computation.15 | async-start | bytes 6815744 | tf_op jit(solution)/shard_map/psum | solution.py:240
  (47 other events, 261.0 us)
Sparse Core Ops, SparseCore 0:
  10.2 49.6 all-gather.15
  62.1 96.3 all-gather.11
  160.6 48.9 all-gather.13
  211.5 122.0 all-gather.17
  335.5 123.1 all-gather.19
  536.5 88.3 reduce-scatter.7
  629.0 88.4 reduce-scatter.9
  721.1 205.0 reduce-scatter.5
  930.0 281.7 reduce-scatter.13
  1215.9 281.1 reduce-scatter.11
  1501.0 73.6 all-reduce.10
where the time goes:
time: 1600 us; the launch traced here: 1590 us
  waiting for transfers between devices  1090 us (68%)
  matrix products  202 us (13%)
  blocking collectives  136 us (8%)
  other arithmetic  82.2 us (5%)
  local copies, waits for them, and re-layouts  65.2 us (4%)
  between operations  16.1 us (1%)
    reduce_scatter x1, waiting for transfers between devices, shards(): lax.psum_scatter(grad_w_down, 'wide', scatter_dimension=0, tiled=True)  283 us
    reduce_scatter x1, waiting for transfers between devices, shards(): lax.psum_scatter(grad_w_up, 'wide', scatter_dimension=0, tiled=True)  283 us
    reduce_scatter x1, waiting for transfers between devices, shards(): lax.psum_scatter(grad_w_qkv, 'wide', scatter_dimension=0, tiled=True)  177 us
    all_gather x1, waiting for transfers between devices, shards(): lax.all_gather(w_up, 'wide', axis=0, tiled=True)  110 us
    all_gather x1, waiting for transfers between devices, shards(): lax.all_gather(w_down, 'wide', axis=0, tiled=True)  109 us
    all_gather x1, waiting for transfers between devices, shards(): lax.all_gather(w_qkv, 'wide', axis=0, tiled=True)  63.4 us
    psum x1, waiting for transfers between devices, shards(): lax.psum(attn_shards[2].astype(jnp.bfloat16), 'group').astype(jnp.float32)  59.5 us
    dot_general x1, matrix products, shards(): jnp.einsum('rd,fd->rf', grad_out_low, mlp_back[5], preferred_element_type...  51.9 us
  transfers between devices with their start and end apart: 11, of which 7 were waited for; matrix products, arithmetic and copies ran while one was open for 15% of the time, Pallas kernels for 0%

commit v1 on v0

v1 whole, which is shorter than its diff:
```python
import functools
import math

import jax
import jax.numpy as jnp
from jax import lax
from jax.experimental import pallas as pl
from jax.experimental.pallas import tpu as pltpu
from jax.sharding import PartitionSpec as P

HEAD_DIM = 64
EPSILON = 1e-05
BOTH = ("group", "wide")
F32 = jnp.float32
BF16 = jnp.bfloat16
BLOCKS = 32
VMEM_BYTES = 58 * 2**20


def add(a, b):
    return (a.astype(F32) + b.astype(F32)).astype(BF16)


def swapped(flag, a, b):
    return jnp.where(flag == 0, a, b), jnp.where(flag == 0, b, a)


def dot(a, b):
    return jnp.dot(a, b, preferred_element_type=F32)


def dot_nt(a, b):
    return lax.dot_general(a, b, (((1,), (1,)), ((), ())), preferred_element_type=F32)


class Plan:
    def __init__(self):
        def pairs(target):
            found = []
            for index in range(32):
                group, wide = divmod(index, 8)
                y, core, z, x = target(group // 2, group % 2, wide // 2, wide % 2)
                found.append((index, (y * 2 + core) * 8 + z * 2 + x))
            return found

        self.core_pairs = pairs(lambda y, c, z, x: (y, 1 - c, z, x))
        self.y_pairs = pairs(lambda y, c, z, x: (1 - y, c, z, x))
        self.x_pairs = pairs(lambda y, c, z, x: (y, c, z, 1 - x))
        self.first_pairs = pairs(lambda y, c, z, x: (y, c, z, 1 - x) if c == 0 else (1 - y, c, z, x))
        self.second_pairs = pairs(lambda y, c, z, x: (1 - y, c, z, x) if c == 0 else (y, c, z, 1 - x))
        self.z_pairs = [pairs(lambda y, c, z, x, step=step: (y, c, (z - step) % 4, x)) for step in range(4)]
        self.wide_pairs = [
            [(g * 8 + w, g * 8 + (w - step) % 8) for g in range(4) for w in range(8)] for step in range(8)
        ]

    def enter(self):
        self.group = lax.axis_index("group")
        self.wide = lax.axis_index("wide")
        y, core = self.group // 2, self.group % 2
        z, x = self.wide // 2, self.wide % 2
        self.core, self.y = core, y
        slot = jnp.arange(BLOCKS, dtype=jnp.int32)
        holder = core ^ (slot // 16)
        second, first, step = (slot // 8) % 2, (slot // 4) % 2, slot % 4
        across = jnp.where(holder == 0, first, second)
        along = jnp.where(holder == 0, second, first)
        places = (((z + step) % 4) * 2 + (x ^ across)) * 4 + (y ^ along) * 2 + holder
        block_z, block_x, block_y, block_core = slot // 8, (slot // 4) % 2, (slot // 2) % 2, slot % 2
        off_x, off_y = block_x ^ x, block_y ^ y
        first = jnp.where(block_core == 0, off_x, off_y)
        second = jnp.where(block_core == 0, off_y, off_x)
        slots = (((block_core ^ core) * 2 + second) * 2 + first) * 4 + (block_z - z) % 4
        return places.astype(jnp.int32), slots.astype(jnp.int32)

    def move(self, value, pairs):
        return lax.ppermute(value, BOTH, pairs)

    def gather(self, shard):
        rows = shard.shape[0] // 4
        own = lax.dynamic_slice_in_dim(shard, self.group * rows, rows, 0)
        own4 = jnp.stack([own] + [self.move(own, self.z_pairs[step]) for step in (1, 2, 3)])
        first = self.move(own4, self.first_pairs)
        second = self.move(own4, self.second_pairs)
        both = self.move(first, self.second_pairs)
        half = [own4, first, second, both]
        return half + [self.move(piece, self.core_pairs) for piece in half]

    def scatter(self, send, keep):
        got = self.move(send, self.first_pairs)
        got = self.move(add(keep[1], got[1]), self.second_pairs), got[0]
        kept = keep[0]
        total = kept[0].astype(F32) + got[1][0].astype(F32) + got[0][0].astype(F32)
        for step in (1, 2, 3):
            part = (kept[step].astype(F32) + got[1][step].astype(F32) + got[0][step].astype(F32)).astype(BF16)
            total = total + self.move(part, self.z_pairs[4 - step]).astype(F32)
        own = total.astype(BF16)
        along = self.move(own, self.y_pairs)
        across = self.move(own, self.core_pairs)
        both = self.move(along, self.core_pairs)
        low, high = swapped(self.core, own, across), swapped(self.core, along, both)
        even, odd = swapped(self.y, low[0], high[0]), swapped(self.y, low[1], high[1])
        return jnp.concatenate([even[0], odd[0], even[1], odd[1]]).astype(F32)

    def gather_small(self, small):
        return jnp.stack([small] + [self.move(small, self.wide_pairs[step]) for step in range(1, 8)])

    def in_order(self, parts):
        return lax.dynamic_slice_in_dim(jnp.concatenate([parts, parts]), (8 - self.wide) % 8, 8, 0)

    def spread_rows(self, parts):
        total = parts[0]
        for step in range(1, 8):
            total = total + self.move(parts[step], self.wide_pairs[8 - step])
        return total

    def gather_all(self, rows):
        for pairs in (self.core_pairs, self.x_pairs, self.y_pairs):
            rows = jnp.concatenate([rows, self.move(rows, pairs)])
        return jnp.concatenate([rows] + [self.move(rows, self.z_pairs[step]) for step in (1, 2, 3)])

    def sum_small(self, vectors):
        for pairs in (self.core_pairs, self.x_pairs, self.y_pairs):
            vectors = vectors + self.move(vectors, pairs)
        total = vectors
        for step in (1, 2, 3):
            total = total + self.move(vectors, self.z_pairs[step])
        return lax.dynamic_index_in_dim(total, self.wide, 0, keepdims=False)


def rotary_tables(length):
    half = HEAD_DIM // 2
    frequency = jnp.exp(jnp.arange(half, dtype=F32) * (-2.0 * math.log(10000.0) / HEAD_DIM))
    angles = jnp.arange(length, dtype=F32)[:, None] * frequency[None, :]
    sine = jnp.sin(angles)
    cosine = jnp.concatenate([jnp.cos(angles)] * 4, axis=1)
    return cosine, jnp.concatenate([-sine, sine, -sine, sine], axis=1)


def call(kernel, name, tables, grid, ins, outs, scratch=(), flops=0, moved=0):
    def spec(block, index, buffers=None):
        if buffers:
            return pl.BlockSpec(block, index, pipeline_mode=pl.Buffered(buffers))
        return pl.BlockSpec(block, index)

    return pl.pallas_call(
        kernel,
        out_shape=[jax.ShapeDtypeStruct(shape, dtype) for shape, dtype, *_ in outs],
        grid_spec=pltpu.PrefetchScalarGridSpec(
            num_scalar_prefetch=len(tables),
            grid=grid,
            in_specs=[spec(*rest) for _, *rest in ins],
            out_specs=[spec(*rest) for _, _, *rest in outs],
            scratch_shapes=list(scratch),
        ),
        compiler_params=pltpu.CompilerParams(vmem_limit_bytes=VMEM_BYTES),
        cost_estimate=pl.CostEstimate(flops=flops, bytes_accessed=moved, transcendentals=0),
        name=name,
    )(*tables, *[array for array, *_ in ins])


def whole(array, buffers=1):
    rank = array.ndim
    return (array, array.shape, lambda i, *_: (0,) * rank, buffers)


def rows_of(array, tile):
    return (array, (tile, array.shape[1]), lambda i, *_: (i, 0))


def out_rows(shape, dtype, tile):
    return (shape, dtype, (tile, shape[1]), lambda i, *_: (i, 0))


def out_whole(shape, dtype):
    return (shape, dtype, shape, lambda i, *_: (0,) * len(shape))


def put_in_order(places, pieces, held):
    for i in range(BLOCKS):
        held[places[i]] = pieces[i // 4][i % 4]


def matrix(held):
    blocks, rows, columns = held.shape
    return held[...].reshape(blocks * rows, columns)


def normalise(values):
    average = jnp.mean(values, axis=-1, keepdims=True)
    centered = values - average
    scale = lax.rsqrt(jnp.mean(centered * centered, axis=-1, keepdims=True) + EPSILON)
    return centered * scale, scale


def norm_back(grad, hat, scale, gain):
    e = grad * gain
    inner = jnp.mean(e * hat, axis=-1, keepdims=True)
    return scale * (e - jnp.mean(e, axis=-1, keepdims=True) - hat * inner)


def turned(values):
    lane = lax.broadcasted_iota(jnp.int32, values.shape, 1)
    return jnp.where(lane % 64 < 32, pltpu.roll(values, 96, 1), pltpu.roll(values, 32, 1))


def heads(values):
    lane = lax.broadcasted_iota(jnp.int32, values.shape, 1)
    zero = jnp.zeros_like(values)
    return jnp.concatenate([jnp.where(lane < 64, values, zero), jnp.where(lane < 64, zero, values)], axis=0)


def put_turned(out, slots, values):
    rows = out.shape[1]
    flipped = values.T
    for j in range(BLOCKS):
        out[slots[j]] = flipped[j * rows : (j + 1) * rows]


def attention_kernel(length, places, slots, tokens, gain, shift, cosine, sine, *refs):
    pieces, (act_turned, qkv, attended, attended_turned), held = refs[:8], refs[8:12], refs[12]
    rows, width = tokens.shape

    @pl.when(pl.program_id(0) == 0)
    def _():
        put_in_order(places, pieces, held)

    hat, _ = normalise(tokens[...].astype(F32))
    act = (hat * gain[...] + shift[...]).astype(BF16)
    put_turned(act_turned, slots, act)
    cos, sin = cosine[...], sine[...]
    for start in range(0, 3 * width, 512):
        part = dot(act, held[:, :, start : start + 512].reshape(width, 512))
        if start < 2 * width:
            for lanes in range(0, 512, 128):
                piece = part[:, lanes : lanes + 128]
                qkv[:, start + lanes : start + lanes + 128] = (piece * cos + turned(piece) * sin).astype(BF16)
        else:
            qkv[:, start : start + 512] = part.astype(BF16)
    for top in range(0, rows, length):
        for lanes in range(0, width, 128):
            q = qkv[top : top + length, lanes : lanes + 128]
            k = heads(qkv[top : top + length, width + lanes : width + lanes + 128])
            v = heads(qkv[top : top + length, 2 * width + lanes : 2 * width + lanes + 128])
            scores = dot_nt(q, k) * HEAD_DIM ** (-0.5)
            probs = []
            for head in range(2):
                own = scores[:, head * length : (head + 1) * length]
                e = jnp.exp(own - jnp.max(own, axis=-1, keepdims=True))
                probs.append((e / jnp.sum(e, axis=-1, keepdims=True)).astype(BF16))
            out = dot(jnp.concatenate(probs, axis=1), v)
            attended[top : top + length, lanes : lanes + 128] = out.astype(BF16)
    put_turned(attended_turned, slots, attended[...])


def middle_kernel(length, places, slots, tokens, attended, scales, gain, shift, *refs):
    pieces, (middle, act, act_turned), held = refs[:8], refs[8:11], refs[11]
    rows = tokens.shape[0]

    @pl.when(pl.program_id(0) == 0)
    def _():
        put_in_order(places, pieces, held)

    values = tokens[...].astype(F32) + dot(attended[...], matrix(held))
    middle[...] = values
    hat, _ = normalise(values)
    normed = hat * gain[...] + shift[...]
    first = pl.program_id(0) * (rows // length)
    for s in range(rows // length):
        act[s * length : (s + 1) * length, :] = (
            normed[s * length : (s + 1) * length, :] * scales[pl.ds(first + s, 1), :]
        ).astype(BF16)
    put_turned(act_turned, slots, act[...])


def up_kernel(places, act, bias, *refs):
    pieces, (hidden, slope), held = refs[:8], refs[8:10], refs[10]
    put_in_order(places, pieces, held)
    v = dot(act[...], matrix(held)) + bias[...]
    a = jnp.abs(v) * math.sqrt(0.5)
    t = 1.0 / (1.0 + 0.3275911 * a)
    bell = jnp.exp(-0.5 * v * v)
    series = ((((1.061405429 * t - 1.453152027) * t + 1.421413741) * t - 0.284496736) * t + 0.254829592) * t
    tail = 0.5 * series * bell
    area = jnp.where(v < 0, tail, 1.0 - tail)
    hidden[...] = (v * area).astype(BF16)
    slope[...] = (area + v * bell * (1.0 / math.sqrt(2.0 * math.pi))).astype(BF16)


def down_grad_kernel(with_got, places, *refs):
    blocks, cotangent = refs[:4], refs[4]
    part = jnp.concatenate([block[...] for block in blocks], axis=1)
    total = dot(part.T, cotangent[...]).reshape(4, -1, cotangent.shape[1])
    if not with_got:
        refs[5][0] = total.astype(BF16)
        return
    got, send, keep = refs[5:8]
    total = (total + got[0].astype(F32)).astype(BF16)

    @pl.when(pl.program_id(0) < 2)
    def _():
        send[0] = total

    @pl.when(pl.program_id(0) >= 2)
    def _():
        keep[0] = total


def weight_grad_kernel(with_got, turned_act, grad, *refs):
    blocks, rows = turned_act.shape[:2]
    total = dot(turned_act[...].reshape(blocks * rows, -1), grad[...]).reshape(4, 4, rows, -1)
    if not with_got:
        refs[0][...] = total.astype(BF16)
        return
    got, send, keep = refs
    total = (total + got[...].astype(F32)).astype(BF16)
    for second in range(2):
        keep[second] = total[2 * second]
        send[second] = total[2 * second + 1]


def pre_grad_kernel(places, cotangent, slope, *refs):
    pieces, (grad_pre, bias), held = refs[:8], refs[8:10], refs[10]

    @pl.when(pl.program_id(0) == 0)
    def _():
        put_in_order(places, pieces, held)

    count = slope.shape[1] // held.shape[1]
    rows = held[pl.ds(pl.program_id(0) * count, count)].reshape(slope.shape[1], -1)
    grad = (dot_nt(cotangent[...], rows) * slope[...].astype(F32)).astype(BF16)
    grad_pre[...] = grad
    bias[...] = jnp.sum(grad.astype(F32), axis=0, keepdims=True)


def output_kernel(places, hidden, middle, bias, *refs):
    pieces, output, held = refs[:8], refs[8], refs[9]

    @pl.when(pl.program_id(0) == 0)
    def _():
        put_in_order(places, pieces, held)

    output[...] = (middle[...] + dot(hidden[...], matrix(held)) + bias[...]).astype(BF16)


def middle_grad_kernel(length, places, grad_pre, middle, cotangent, scales, gain, shift, *refs):
    pieces, (grad_middle, grad_branch, grad_scale, gain_sum, shift_sum), held = refs[:8], refs[8:13], refs[13]
    rows = middle.shape[0]

    @pl.when(pl.program_id(0) == 0)
    def _():
        put_in_order(places, pieces, held)
        gain_sum[...] = jnp.zeros_like(gain_sum)
        shift_sum[...] = jnp.zeros_like(shift_sum)

    grad_scaled = dot_nt(grad_pre[...], matrix(held))
    hat, scale = normalise(middle[...])
    first = pl.program_id(0) * (rows // length)
    for s in range(rows // length):
        at = slice(s * length, (s + 1) * length)
        own, own_hat = grad_scaled[at], hat[at]
        normed = own_hat * gain[...] + shift[...]
        grad_scale[pl.ds(first + s, 1), :] = jnp.sum(own * normed, axis=0, keepdims=True)
        grad = own * scales[pl.ds(first + s, 1), :]
        gain_sum[...] += jnp.sum(grad * own_hat, axis=0, keepdims=True)
        shift_sum[...] += jnp.sum(grad, axis=0, keepdims=True)
        total = cotangent[at, :].astype(F32) + norm_back(grad, own_hat, scale[at], gain[...])
        grad_middle[at, :] = total
        grad_branch[at, :] = total.astype(BF16)


def attention_grad_kernel(length, places, grad_branch, qkv, cosine, sine, *refs):
    pieces, grad_projected, held, grad_attended = refs[:8], refs[8], refs[9], refs[10]
    rows, width = grad_branch.shape
    factor = HEAD_DIM ** (-0.5)

    @pl.when(pl.program_id(0) == 0)
    def _():
        put_in_order(places, pieces, held)

    grad_attended[...] = dot_nt(grad_branch[...], matrix(held)).astype(BF16)
    cos, sin = cosine[...], sine[...]
    for top in range(0, rows, length):
        at = slice(top, top + length)
        for lanes in range(0, width, 128):
            q = heads(qkv[at, lanes : lanes + 128])
            k = qkv[at, width + lanes : width + lanes + 128]
            v = qkv[at, 2 * width + lanes : 2 * width + lanes + 128]
            g = heads(grad_attended[at, lanes : lanes + 128])
            scores = dot_nt(k, q) * factor
            e = jnp.exp(scores - jnp.max(scores, axis=0, keepdims=True))
            probs = e / jnp.sum(e, axis=0, keepdims=True)
            grad_values = dot(probs.astype(BF16), g)
            grad_probs = dot_nt(v, g)
            inner = jnp.sum(grad_probs * probs, axis=0, keepdims=True)
            grad_scores = (probs * (grad_probs - inner)).astype(BF16)
            grad_keys = dot(grad_scores, q) * factor
            flipped = jnp.concatenate([grad_scores[:, :length].T, grad_scores[:, length:].T], axis=1)
            grad_queries = dot(flipped, heads(k)) * factor
            for start, grad in ((lanes, grad_queries), (width + lanes, grad_keys)):
                grad_projected[at, start : start + 128] = (grad * cos[at] - turned(grad) * sin[at]).astype(BF16)
            grad_projected[at, 2 * width + lanes : 2 * width + lanes + 128] = grad_values.astype(BF16)


def token_grad_kernel(places, grad_projected, tokens, grad_middle, gain, *refs):
    pieces, (grad_tokens, gain_sum, shift_sum), held = refs[:8], refs[8:11], refs[11]

    @pl.when(pl.program_id(0) == 0)
    def _():
        put_in_order(places, pieces, held)
        gain_sum[...] = jnp.zeros_like(gain_sum)
        shift_sum[...] = jnp.zeros_like(shift_sum)

    grad = dot_nt(grad_projected[...], matrix(held))
    hat, scale = normalise(tokens[...].astype(F32))
    gain_sum[...] += jnp.sum(grad * hat, axis=0, keepdims=True)
    shift_sum[...] += jnp.sum(grad, axis=0, keepdims=True)
    grad_tokens[...] = grad_middle[...] + norm_back(grad, hat, scale, gain[...])


def shards(plan, tokens, cotangent, noise_index, time_embed, ln1_gain, ln1_shift, w_qkv, w_out, ln2_gain, ln2_shift,
           w_time, w_up, up_bias, w_down, down_bias):
    rows, width = tokens.shape
    seqs = noise_index.shape[0]
    length = rows // seqs
    levels = time_embed.shape[0]
    ff = w_up.shape[1]
    tile = 2 * length
    steps = rows // tile
    per = ln1_gain.shape[0]

    def chosen(index, table):
        picks = (index[:, None] == jnp.arange(levels, dtype=jnp.int32)[None, :]).astype(BF16)
        return dot(picks, table).astype(BF16)

    if plan is not None:
        places, slots = plan.enter()
        lines = [v.reshape(-1, per) for v in (ln1_gain, ln1_shift, ln2_gain, ln2_shift, down_bias, up_bias)]
        index_line = jnp.pad(noise_index.astype(BF16), (0, per - seqs))[None]
        small = plan.gather_small(jnp.concatenate(lines + [index_line]))
        vectors = plan.in_order(small)
        gain_one, shift_one, gain_two, shift_two, bias_down = [
            vectors[:, i].reshape(1, -1).astype(F32) for i in range(5)
        ]
        bias_up = vectors[:, 5:-1].reshape(1, -1).astype(F32)
        near = small[:, -1, :seqs].reshape(-1).astype(jnp.int32)
        own_levels = lax.dynamic_slice_in_dim(time_embed, plan.wide * per, per, 1)
        partial = dot(chosen(near, own_levels), w_time).reshape(-1, seqs, width)
        scales = 1.0 + plan.spread_rows(partial)
        full = [plan.gather(w) for w in (w_qkv, w_out, w_up, w_down)]
    else:
        places = slots = jnp.arange(BLOCKS, dtype=jnp.int32)

        def gathered(v):
            return lax.all_gather(v, "wide", axis=0, tiled=True)

        gain_one, shift_one, gain_two, shift_two, bias_down, bias_up = [
            gathered(v).astype(F32)[None] for v in (ln1_gain, ln1_shift, ln2_gain, ln2_shift, down_bias, up_bias)
        ]
        embedded = chosen(noise_index, time_embed)
        scales = 1.0 + dot(embedded, gathered(w_time))
        full = []
        for w in (w_qkv, w_out, w_up, w_down):
            w = gathered(w)
            full.append(list(w.reshape(8, 4, w.shape[0] // BLOCKS, w.shape[1])))
    qkv_pieces, out_pieces, up_pieces, down_pieces = full
    cosine, sine = rotary_tables(length)
    cosine, sine = jnp.tile(cosine, (tile // length, 1)), jnp.tile(sine, (tile // length, 1))
    deep = width // BLOCKS

    def held(pieces):
        _, r, c = pieces[0].shape
        return pltpu.VMEM((BLOCKS, r, c), BF16)

    def turned_out():
        return ((BLOCKS, deep, rows), BF16, (BLOCKS, deep, tile), lambda i, *_: (0, 0, i))

    act_one_turned, qkv, attended, attended_turned = call(
        functools.partial(attention_kernel, length), "attention", (places, slots), (steps,),
        [rows_of(tokens, tile), whole(gain_one), whole(shift_one), whole(cosine), whole(sine)]
        + [whole(p) for p in qkv_pieces],
        [turned_out(), out_rows((rows, 3 * width), BF16, tile), out_rows((rows, width), BF16, tile), turned_out()],
        [held(qkv_pieces)], flops=2 * rows * width * 3 * width * 2, moved=20 * rows * width,
    )
    middle, act_two, act_two_turned = call(
        functools.partial(middle_kernel, length), "middle", (places, slots), (steps,),
        [rows_of(tokens, tile), rows_of(attended, tile), whole(scales), whole(gain_two), whole(shift_two)]
        + [whole(p) for p in out_pieces],
        [out_rows((rows, width), F32, tile), out_rows((rows, width), BF16, tile), turned_out()],
        [held(out_pieces)], flops=2 * rows * width * width * 2, moved=14 * rows * width,
    )
    strip = 512
    strips = ff // strip

    def columns_of(array, wide=strip):
        return (array, (array.shape[0], wide), lambda i, *_: (0, i))

    def piece_columns(piece):
        return (piece, piece.shape[:2] + (strip,), lambda i, *_: (0, 0, i))

    def out_columns(shape, dtype):
        return (shape, dtype, shape[:-1] + (strip,), lambda i, *_: (0,) * (len(shape) - 1) + (i,))

    hidden, slope = call(
        up_kernel, "up", (places,), (strips,),
        [whole(act_two), columns_of(bias_up)] + [piece_columns(p) for p in up_pieces],
        [out_columns((rows, ff), BF16), out_columns((rows, ff), BF16)],
        [pltpu.VMEM((BLOCKS, deep, strip), BF16)], flops=2 * rows * width * ff * 2, moved=26 * rows * width,
    )

    def down_grad(order, got):
        order = jnp.asarray(order, jnp.int32)
        table = places.reshape(8, 4)[order].reshape(-1)
        fr = ff // BLOCKS
        ins = [(hidden, (rows, fr), lambda i, t, o, j=j: (0, t[4 * i + j])) for j in range(4)] + [whole(cotangent)]
        block = (1, 4, fr, width)
        if got is None:
            outs = [((4, 4, fr, width), BF16, block, lambda i, t, o: (i, 0, 0, 0))]
        else:
            ins.append((got, block, lambda i, t, o: (o[i], 0, 0, 0)))
            outs = [
                ((2, 4, fr, width), BF16, block, lambda i, t, o: (jnp.minimum(i, 1), 0, 0, 0)),
                ((2, 4, fr, width), BF16, block, lambda i, t, o: (jnp.maximum(i - 2, 0), 0, 0, 0)),
            ]

        def kernel(t, o, *refs):
            down_grad_kernel(got is not None, t, *refs)

        return call(kernel, "down_grad", (table, order), (4,), ins, outs,
                    flops=rows * width * ff, moved=8 * rows * width)

    def weight_grad(turned_act, grad, half, got):
        ins = [
            (turned_act, (BLOCKS // 2, deep, rows), lambda i, *_: (half, 0, 0), 1),
            columns_of(grad),
        ]
        columns = grad.shape[1]
        if got is None:
            outs = [out_columns((4, 4, deep, columns), BF16)]
        else:
            ins.append((got, (4, 4, deep, strip), lambda i, *_: (0, 0, 0, i)))
            outs = [out_columns((2, 4, deep, columns), BF16)] * 2
        return call(functools.partial(weight_grad_kernel, got is not None), "weight_grad", (), (columns // strip,),
                    ins, outs, flops=rows * width * columns, moved=3 * rows * columns)

    def summed(theirs, ours):
        (sent,) = theirs()
        if plan is not None:
            return plan.scatter(*ours(plan.move(sent, plan.core_pairs)))
        send, keep = ours(jnp.zeros_like(sent))
        mine = jnp.stack([keep[0], send[0], keep[1], send[1]])
        grad = jnp.concatenate([mine, sent]).reshape(-1, sent.shape[-1])
        grad = lax.psum_scatter(grad, "wide", scatter_dimension=0, tiled=True)
        return lax.psum(grad, "group").astype(F32)

    grad_w_down = summed(lambda: down_grad((4, 5, 6, 7), None), lambda got: down_grad((1, 3, 0, 2), got))
    grad_down_bias = jnp.sum(cotangent.astype(F32), axis=0)
    grad_pre, grad_up_bias = call(
        pre_grad_kernel, "pre_grad", (places,), (strips,),
        [whole(cotangent), columns_of(slope)] + [whole(p) for p in down_pieces],
        [out_columns((rows, ff), BF16), out_columns((1, ff), F32)],
        [held(down_pieces)], flops=2 * rows * width * ff, moved=26 * rows * width,
    )
    grad_w_up = summed(
        lambda: weight_grad(act_two_turned, grad_pre, 1, None), lambda got: weight_grad(act_two_turned, grad_pre, 0, got)
    )
    (output,) = call(
        output_kernel, "output", (places,), (steps,),
        [rows_of(hidden, tile), rows_of(middle, tile), whole(bias_down)] + [whole(p) for p in down_pieces],
        [out_rows((rows, width), BF16, tile)],
        [held(down_pieces)], flops=2 * rows * width * ff, moved=22 * rows * width,
    )
    grad_middle, grad_branch, grad_scale, grad_gain_two, grad_shift_two = call(
        functools.partial(middle_grad_kernel, length), "middle_grad", (places,), (steps,),
        [rows_of(grad_pre, tile), rows_of(middle, tile), rows_of(cotangent, tile), whole(scales), whole(gain_two)]
        + [whole(shift_two)] + [whole(p) for p in up_pieces],
        [out_rows((rows, width), F32, tile), out_rows((rows, width), BF16, tile), out_whole((seqs, width), F32)]
        + [out_whole((1, width), F32)] * 2,
        [held(up_pieces)], flops=2 * rows * width * ff, moved=28 * rows * width,
    )
    grad_scale = grad_scale.astype(BF16)
    grad_w_out = summed(
        lambda: weight_grad(attended_turned, grad_branch, 1, None),
        lambda got: weight_grad(attended_turned, grad_branch, 0, got),
    )
    (grad_projected,) = call(
        functools.partial(attention_grad_kernel, length), "attention_grad", (places,), (steps,),
        [rows_of(grad_branch, tile), rows_of(qkv, tile), whole(cosine), whole(sine)] + [whole(p) for p in out_pieces],
        [out_rows((rows, 3 * width), BF16, tile)],
        [held(out_pieces), pltpu.VMEM((tile, width), BF16)],
        flops=2 * rows * width * 3 * width * 2, moved=16 * rows * width,
    )
    grad_w_qkv = summed(
        lambda: weight_grad(act_one_turned, grad_projected, 1, None),
        lambda got: weight_grad(act_one_turned, grad_projected, 0, got),
    )
    grad_tokens, grad_gain_one, grad_shift_one = call(
        token_grad_kernel, "token_grad", (places,), (steps,),
        [rows_of(grad_projected, tile), rows_of(tokens, tile), rows_of(grad_middle, tile), whole(gain_one)]
        + [whole(p) for p in qkv_pieces],
        [out_rows((rows, width), F32, tile)] + [out_whole((1, width), F32)] * 2,
        [held(qkv_pieces)], flops=2 * rows * width * 3 * width, moved=22 * rows * width,
    )
    sums = (grad_gain_one, grad_shift_one, grad_gain_two, grad_shift_two, grad_down_bias, grad_up_bias)
    if plan is not None:
        index_lanes = jnp.broadcast_to(noise_index.astype(BF16)[:, None], (seqs, 128))
        everyone = plan.gather_all(jnp.concatenate([grad_scale, index_lanes], axis=1))
        picked = chosen(everyone[:, width].astype(jnp.int32), own_levels)
        grad_w_time = lax.dot_general(
            picked, everyone[:, :width], (((0,), (0,)), ((), ())), preferred_element_type=F32
        )
        small_sum = plan.sum_small(jnp.concatenate([v.reshape(8, -1, per) for v in sums], axis=1))
        vec = [small_sum[i] for i in range(5)] + [small_sum[5:].reshape(-1)]
    else:
        grad_w_time = lax.dot_general(
            embedded, grad_scale, (((0,), (0,)), ((), ())), preferred_element_type=F32
        )
        grad_w_time = lax.psum(lax.psum_scatter(grad_w_time, "wide", scatter_dimension=0, tiled=True), "group")
        vec = [
            lax.psum(lax.psum_scatter(v.reshape(-1), "wide", scatter_dimension=0, tiled=True), "group") for v in sums
        ]
    return (output, grad_tokens, vec[0], vec[1], grad_w_qkv, grad_w_out, vec[2], vec[3], grad_w_time, grad_w_up,
            vec[5], grad_w_down, vec[4])


def solution(mesh):
    plan = Plan() if (mesh.shape["group"], mesh.shape["wide"]) == (4, 8) else None
    split, rows, line = P(BOTH, None), P("wide", None), P("wide")
    in_specs = (split, split, P(BOTH), P(), line, line, rows, rows, line, line, rows, rows, line, rows, line)
    out_specs = (split, split, line, line, rows, rows, line, line, rows, rows, line, rows, line)
    return jax.shard_map(
        functools.partial(shards, plan), mesh=mesh, in_specs=in_specs, out_specs=out_specs, check_vma=False
    )
```

time: 1600 us -> 603 us (0.38)
  waiting for transfers between devices: 1090 us -> 193 us
  Pallas kernels: 0 us -> 223 us
  matrix products: 202 us -> 3.74 us
  blocking collectives: 136 us -> 0 us
  starting transfers between devices: 0.44 us -> 118 us
  other arithmetic: 82.2 us -> 23.8 us
  local copies, waits for them, and re-layouts: 65.2 us -> 27.9 us
    reduce_scatter x5 -> x0, waiting for transfers between devices: 743 us -> none  [the longest x1 283 us: shards(): lax.psum_scatter(grad_w_down, 'wide', scatter_dimension=0, tiled=True)]
    all_gather x5 -> x0, waiting for transfers between devices: 283 us -> none  [the longest x1 110 us: shards(): lax.all_gather(w_up, 'wide', axis=0, tiled=True)]
    pallas_call x0 -> x16, Pallas kernels: none -> 223 us  [call(): pl.pallas_call(kernel, out_shape=[jax.ShapeDtypeStruct(shape, dtype) for...]
    dot_general x21 -> x2, matrix products: 202 us -> 3.74 us  [the longest x1 2.4 us: shards(): lax.dot_general(picked, everyone[:, :width], (((0,), (0,)), ((), ())), pr...]
    ppermute x0 -> x102, waiting for transfers between devices: none -> 193 us  [move(): return lax.ppermute(value, BOTH, pairs)]
    ppermute x0 -> x102, starting transfers between devices: none -> 118 us  [move(): return lax.ppermute(value, BOTH, pairs)]
    all_gather x6 -> x0, blocking collectives: 92.6 us -> none  [the longest x1 23.8 us: shards(): lax.all_gather(up_bias, 'wide', axis=0, tiled=True)]
    psum x1 -> x0, waiting for transfers between devices: 59.5 us -> none  [shards(): lax.psum(attn_shards[2].astype(jnp.bfloat16), 'group').astype(jnp.float32)]
  transfers between devices with their start and end apart: 11 -> 102, of which waited for: 7 -> 35; matrix products, arithmetic and copies ran while one was open for 15% -> 8% of each run, Pallas kernels for 0% -> 24%
where the time goes in v1:
time: 603 us; the launch traced here: 591 us
  Pallas kernels  223 us (37%)
  waiting for transfers between devices  193 us (32%)
  starting transfers between devices  118 us (20%)
  local copies, waits for them, and re-layouts  27.9 us (5%)
  other arithmetic  23.8 us (4%)
    pallas_call x16, Pallas kernels, call(): pl.pallas_call(kernel, out_shape=[jax.ShapeDtypeStruct(shape, dtype) for...  223 us
    ppermute x102, waiting for transfers between devices, move(): return lax.ppermute(value, BOTH, pairs)  193 us
    ppermute x102, starting transfers between devices, move(): return lax.ppermute(value, BOTH, pairs)  118 us
  transfers between devices with their start and end apart: 102, of which 35 were waited for; matrix products, arithmetic and copies ran while one was open for 8% of the time, Pallas kernels for 24%

profile of v1, /device:TPU:9, one launch (start us, length us, event | category | flops | bytes accessed | tf_op | source)
XLA Modules:
  0.0 591.0 jit_solution(1977001977360950574)
XLA Ops:
  26.8 5.1 collective-permute-start.25
  54.1 13.5 %collective-permute-done.19 = f32[8,1024]{1,0:T(8,128)S(1)} collective-permute-done((f32[8,1024]{1,0:T(8,128)S(1)}, f32[8,1024]{1,0:T(8,128)S(1)}, u32[]{:S(2)}, u32[]{:S(2)}) %collective-permute-start.19) | collective-permute-done | bytes 32800 | tf_op jit(solution)/shard_map/ppermute | solution.py:76
  78.8 11.5 %collective-permute-done.45 = bf16[128,1024]{1,0:T(8,128)(2,1)} collective-permute-done((bf16[128,1024]{1,0:T(8,128)(2,1)}, bf16[128,1024]{1,0:T(8,128)(2,1)}, u32[]{:S(2)}, u32[]{:S(2)}) %collective-permute-start.45) | collective-permute-done | bytes 262176 | tf_op jit(solution)/shard_map/ppermute | solution.py:76
  90.3 11.1 %collective-permute-done.44 = bf16[128,1024]{1,0:T(8,128)(2,1)} collective-permute-done((bf16[128,1024]{1,0:T(8,128)(2,1)}, bf16[128,1024]{1,0:T(8,128)(2,1)}, u32[]{:S(2)}, u32[]{:S(2)}) %collective-permute-start.44) | collective-permute-done | bytes 262176 | tf_op jit(solution)/shard_map/ppermute | solution.py:76
  132.7 27.7 %collective-permute-done.11.refs_2_ = bf16[4,32,3072]{2,1,0:T(8,128)(2,1)S(1)} collective-permute-done((bf16[4,32,3072]{2,1,0:T(8,128)(2,1)S(1)}, bf16[4,32,3072]{2,1,0:T(8,128)(2,1)S(1)}, u32[]{:S(2)}, u32[]{:S(2)}) %collective-permute-start.11) | collective-permute-done | bytes 786464 | tf_op jit(solution)/shard_map/ppermute | solution.py:76
  163.0 11.1 %collective-permute-done.12.refs_3_ = bf16[4,32,3072]{2,1,0:T(8,128)(2,1)S(1)} collective-permute-done((bf16[4,32,3072]{2,1,0:T(8,128)(2,1)S(1)}, bf16[4,32,3072]{2,1,0:T(8,128)(2,1)S(1)}, u32[]{:S(2)}, u32[]{:S(2)}) %collective-permute-start.12) | collective-permute-done | bytes 786464 | tf_op jit(solution)/shard_map/ppermute | solution.py:76
  176.9 8.8 %collective-permute-done.47.refs_1_ = bf16[4,128,1024]{2,1,0:T(8,128)(2,1)S(1)} collective-permute-done((bf16[4,128,1024]{2,1,0:T(8,128)(2,1)S(1)}, bf16[4,128,1024]{2,1,0:T(8,128)(2,1)S(1)}, u32[]{:S(2)}, u32[]{:S(2)}) %collective-permute-start.47) | collective-permute-done | bytes 1048608 | tf_op jit(solution)/shard_map/ppermute | solution.py:76
  194.1 20.0 %attention.1 = (bf16[32,32,1024]{2,1,0:T(8,128)(2,1)}, bf16[1024,3072]{1,0:T(8,128)(2,1)}, bf16[1024,1024]{1,0:T(8,128)(2,1)}, bf16[32,32,1024]{2,1,0:T(8,128)(2,1)}) custom-call(s32[32]{0:T(128)} %add_add_fusion.places, s32[32]{0:T(128)} %fusion.79.slots, bf16[1024,1024]{1,0:T(8,128)(2,1)} %tokens.5, f32[1,1024]{1,0:T(1,128)} %get-tuple-element.106.gain, ...), custom_call_target="tpu_custom_call" | custom-call | flops 12884901888 | bytes 20971520 | tf_op jit(solution)/shard_map/attention/pallas_call | solution.py:145
  214.2 9.3 %middle.1 = (f32[1024,1024]{1,0:T(8,128)}, bf16[1024,1024]{1,0:T(8,128)(2,1)}, bf16[32,32,1024]{2,1,0:T(8,128)(2,1)}) custom-call(s32[32]{0:T(128)} %add_add_fusion.places, s32[32]{0:T(128)} %fusion.79.slots, bf16[1024,1024]{1,0:T(8,128)(2,1)} %tokens.5, bf16[1024,1024]{1,0:T(8,128)(2,1)} %get-tuple-element.40.attended, f32[8,1024]{1,0:T(8,128)} %fusion.49.scales, ...), custom_call_target="tpu_custom_call" | custom-call | flops 4294967296 | bytes 14680064 | tf_op jit(solution)/shard_map/middle/pallas_call | solution.py:145
  224.6 28.8 %up.1 = (bf16[1024,4096]{1,0:T(8,128)(2,1)}, bf16[1024,4096]{1,0:T(8,128)(2,1)}) custom-call(s32[32]{0:T(128)} %add_add_fusion.places, bf16[1024,1024]{1,0:T(8,128)(2,1)} %get-tuple-element.41.act, f32[1,4096]{1,0:T(1,128)} %bitcast.246, bf16[4,32,4096]{2,1,0:T(8,128)(2,1)} %copy-done.10, bf16[4,32,4096]{2,1,0:T(8,128)(2,1)} %copy-done.27, ...), custom_call_target="tpu_custom_call" | custom-call | flops 17179869184 | bytes 27262976 | tf_op jit(solution)/shard_map/up/pallas_call | solution.py:145
  254.8 18.5 %pre_grad.1 = (bf16[1024,4096]{1,0:T(8,128)(2,1)}, f32[1,4096]{1,0:T(1,128)}) custom-call(s32[32]{0:T(128)} %add_add_fusion.places, bf16[1024,1024]{1,0:T(8,128)(2,1)} %refs_4_.3, bf16[1024,4096]{1,0:T(8,128)(2,1)} %get-tuple-element.44.slope, bf16[4,128,1024]{2,1,0:T(8,128)(2,1)} %copy-done.9, bf16[4,128,1024]{2,1,0:T(8,128)(2,1)} %copy-done.26, ...), custom_call_target="tpu_custom_call" | custom-call | flops 8589934592 | bytes 27262976 | tf_op jit(solution)/shard_map/pre_grad/pallas_call | solution.py:145
  273.3 19.5 %middle_grad.1 = (f32[1024,1024]{1,0:T(8,128)}, bf16[1024,1024]{1,0:T(8,128)(2,1)}, f32[8,1024]{1,0:T(8,128)}, f32[1,1024]{1,0:T(1,128)}, f32[1,1024]{1,0:T(1,128)}) custom-call(s32[32]{0:T(128)} %add_add_fusion.places, bf16[1024,4096]{1,0:T(8,128)(2,1)} %get-tuple-element.45.grad_pre.grad, f32[1024,1024]{1,0:T(8,128)} %get-tuple-element.43.middle, ...), custom_call_target="tpu_custom_call" | custom-call | flops 8589934592 | bytes 29360128 | tf_op jit(solution)/shard_map/middle_grad/pallas_call | solution.py:145
  293.5 29.2 %attention_grad.1.grad_projected.grad = bf16[1024,3072]{1,0:T(8,128)(2,1)} custom-call(s32[32]{0:T(128)} %add_add_fusion.places, bf16[1024,1024]{1,0:T(8,128)(2,1)} %get-tuple-element.46.grad_branch.grad, bf16[1024,3072]{1,0:T(8,128)(2,1)} %get-tuple-element.47.qkv, f32[256,128]{1,0:T(8,128)} %bitcast.238, f32[256,128]{1,0:T(8,128)} %bitcast.240, ...), custom_call_target="tpu_custom_call" | custom-call | flops 12884901888 | bytes 16777216 | tf_op jit(solution)/shard_map/attention_grad/pallas_call | solution.py:145
  322.8 15.4 %token_grad.1 = (f32[1024,1024]{1,0:T(8,128)}, f32[1,1024]{1,0:T(1,128)}, f32[1,1024]{1,0:T(1,128)}) custom-call(s32[32]{0:T(128)} %add_add_fusion.places, bf16[1024,3072]{1,0:T(8,128)(2,1)} %attention_grad.1.grad_projected.grad, bf16[1024,1024]{1,0:T(8,128)(2,1)} %tokens.5, f32[1024,1024]{1,0:T(8,128)} %get-tuple-element.48.grad_middle, ...), custom_call_target="tpu_custom_call" | custom-call | flops 6442450944 | bytes 23068672 | tf_op jit(solution)/shard_map/token_grad/pallas_call | solution.py:145
  343.9 8.2 %weight_grad.6 = bf16[4,4,32,3072]{3,2,1,0:T(8,128)(2,1)} custom-call(bf16[32,32,1024]{2,1,0:T(8,128)(2,1)} %get-tuple-element.55.turned_act, bf16[1024,3072]{1,0:T(8,128)(2,1)} %attention_grad.1.grad_projected.grad), custom_call_target="tpu_custom_call" | custom-call | flops 3221225472 | bytes 9437184 | tf_op jit(solution)/shard_map/weight_grad/pallas_call | solution.py:145
  352.6 10.5 %weight_grad.10 = bf16[4,4,32,4096]{3,2,1,0:T(8,128)(2,1)} custom-call(bf16[32,32,1024]{2,1,0:T(8,128)(2,1)} %get-tuple-element.62.turned_act, bf16[1024,4096]{1,0:T(8,128)(2,1)} %get-tuple-element.45.grad_pre.grad), custom_call_target="tpu_custom_call" | custom-call | flops 4294967296 | bytes 12582912 | tf_op jit(solution)/shard_map/weight_grad/pallas_call | solution.py:145
  363.2 15.8 %output.1 = bf16[1024,1024]{1,0:T(8,128)(2,1)} custom-call(s32[32]{0:T(128)} %add_add_fusion.places, bf16[1024,4096]{1,0:T(8,128)(2,1)} %get-tuple-element.42.hidden.refs_0_.refs_1_.refs_2_.refs_3_, f32[1024,1024]{1,0:T(8,128)} %get-tuple-element.43.middle, f32[1,1024]{1,0:T(1,128)} %get-tuple-element.102.bias, bf16[4,128,1024]{2,1,0:T(8,128)(2,1)} %copy-done.9, ...), custom_call_target="tpu_custom_call" | custom-call | flops 8589934592 | bytes 23068672 | tf_op jit(solution)/shard_map/output/pallas_call | solution.py:145
  379.0 9.3 %down_grad.2 = bf16[4,4,128,1024]{3,2,1,0:T(8,128)(2,1)} custom-call(s32[16]{0:T(128)} %reshape.402.t, s32[4]{0:T(128)} %constant.208.clone.o, bf16[1024,4096]{1,0:T(8,128)(2,1)} %get-tuple-element.42.hidden.refs_0_.refs_1_.refs_2_.refs_3_, bf16[1024,4096]{1,0:T(8,128)(2,1)} %get-tuple-element.42.hidden.refs_0_.refs_1_.refs_2_.refs_3_, ...), custom_call_target="tpu_custom_call" | custom-call | flops 4294967296 | bytes 8388608 | tf_op jit(solution)/shard_map/down_grad/pallas_call | solution.py:145
  414.5 4.2 weight_grad.9
  419.0 8.7 %weight_grad.7 = (bf16[2,4,32,3072]{3,2,1,0:T(8,128)(2,1)}, bf16[2,4,32,3072]{3,2,1,0:T(8,128)(2,1)}) custom-call(bf16[32,32,1024]{2,1,0:T(8,128)(2,1)} %get-tuple-element.55.turned_act, bf16[1024,3072]{1,0:T(8,128)(2,1)} %attention_grad.1.grad_projected.grad, bf16[4,4,32,3072]{3,2,1,0:T(8,128)(2,1)} %collective-permute-done.60.refs_0_), custom_call_target="tpu_custom_call" | custom-call | flops 3221225472 | bytes 9437184 | tf_op jit(solution)/shard_map/weight_grad/pallas_call | solution.py:145
  434.2 6.4 %collective-permute-done.71 = bf16[4,32,1024]{2,1,0:T(8,128)(2,1)S(1)} collective-permute-done((bf16[4,32,1024]{2,1,0:T(8,128)(2,1)S(1)}, bf16[4,32,1024]{2,1,0:T(8,128)(2,1)S(1)}, u32[]{:S(2)}, u32[]{:S(2)}) %collective-permute-start.71) | collective-permute-done | bytes 262176 | tf_op jit(solution)/shard_map/ppermute | solution.py:76
  452.0 11.0 %weight_grad.11 = (bf16[2,4,32,4096]{3,2,1,0:T(8,128)(2,1)}, bf16[2,4,32,4096]{3,2,1,0:T(8,128)(2,1)}) custom-call(bf16[32,32,1024]{2,1,0:T(8,128)(2,1)} %get-tuple-element.62.turned_act, bf16[1024,4096]{1,0:T(8,128)(2,1)} %get-tuple-element.45.grad_pre.grad, bf16[4,4,32,4096]{3,2,1,0:T(8,128)(2,1)} %collective-permute-done.84.refs_0_), custom_call_target="tpu_custom_call" | custom-call | flops 4294967296 | bytes 12582912 | tf_op jit(solution)/shard_map/weight_grad/pallas_call | solution.py:145
  466.7 11.0 %collective-permute-start.75 = (bf16[32,1024]{1,0:T(8,128)(2,1)S(1)}, bf16[32,1024]{1,0:T(8,128)(2,1)S(1)}, u32[]{:S(2)}, u32[]{:S(2)}) collective-permute-start(bf16[32,1024]{1,0:T(8,128)(2,1)S(1)} %fusion.34), channel_id=1, source_target_pairs={{0,8},{1,9},{2,10},{3,11},{4,12},{5,13},{6,14},{7,15},{8,0},{9,1},... | collective-permute-start | bytes 196616 | tf_op jit(solution)/shard_map/ppermute | solution.py:76
  477.8 10.7 %down_grad.3 = (bf16[2,4,128,1024]{3,2,1,0:T(8,128)(2,1)}, bf16[2,4,128,1024]{3,2,1,0:T(8,128)(2,1)}) custom-call(s32[16]{0:T(128)} %reshape.401.t, s32[4]{0:T(128)} %constant.209.clone.o, bf16[1024,4096]{1,0:T(8,128)(2,1)} %get-tuple-element.42.hidden.refs_0_.refs_1_.refs_2_.refs_3_, ...), custom_call_target="tpu_custom_call" | custom-call | flops 4294967296 | bytes 8388608 | tf_op jit(solution)/shard_map/down_grad/pallas_call | solution.py:145
  496.7 4.6 collective-permute-done.65
  501.4 7.0 %collective-permute-done.64 = bf16[32,3072]{1,0:T(8,128)(2,1)S(1)} collective-permute-done((bf16[32,3072]{1,0:T(8,128)(2,1)S(1)}, bf16[32,3072]{1,0:T(8,128)(2,1)S(1)}, u32[]{:S(2)}, u32[]{:S(2)}) %collective-permute-start.64) | collective-permute-done | bytes 196640 | tf_op jit(solution)/shard_map/ppermute | solution.py:76
  513.3 14.2 %collective-permute-done.67 = bf16[32,3072]{1,0:T(8,128)(2,1)S(1)} collective-permute-done((bf16[32,3072]{1,0:T(8,128)(2,1)S(1)}, bf16[32,3072]{1,0:T(8,128)(2,1)S(1)}, u32[]{:S(2)}, u32[]{:S(2)}) %collective-permute-start.67) | collective-permute-done | bytes 196640 | tf_op jit(solution)/shard_map/ppermute | solution.py:76
  529.1 4.7 collective-permute-done.86
  536.7 8.4 %collective-permute-done.95 = bf16[4,128,1024]{2,1,0:T(8,128)(2,1)S(1)} collective-permute-done((bf16[4,128,1024]{2,1,0:T(8,128)(2,1)S(1)}, bf16[4,128,1024]{2,1,0:T(8,128)(2,1)S(1)}, u32[]{:S(2)}, u32[]{:S(2)}) %collective-permute-start.95) | collective-permute-done | bytes 1048608 | tf_op jit(solution)/shard_map/ppermute | solution.py:76
  548.1 7.9 %collective-permute-done.88 = bf16[32,4096]{1,0:T(8,128)(2,1)S(1)} collective-permute-done((bf16[32,4096]{1,0:T(8,128)(2,1)S(1)}, bf16[32,4096]{1,0:T(8,128)(2,1)S(1)}, u32[]{:S(2)}, u32[]{:S(2)}) %collective-permute-start.88) | collective-permute-done | bytes 262176 | tf_op jit(solution)/shard_map/ppermute | solution.py:76
  557.0 4.2 collective-permute-start.90
  561.2 11.6 %collective-permute-done.96 = bf16[128,1024]{1,0:T(8,128)(2,1)S(1)} collective-permute-done((bf16[128,1024]{1,0:T(8,128)(2,1)S(1)}, bf16[128,1024]{1,0:T(8,128)(2,1)S(1)}, u32[]{:S(2)}, u32[]{:S(2)}) %collective-permute-start.96) | collective-permute-done | bytes 262176 | tf_op jit(solution)/shard_map/ppermute | solution.py:76
  (369 shorter events, 201.7 us)
Async XLA Ops:
  3.5 31.5 %collective-permute-start.6 = (bf16[10,128]{1,0:T(8,128)(2,1)S(1)}, bf16[10,128]{1,0:T(8,128)(2,1)S(1)}, u32[]{:S(2)}, u32[]{:S(2)}) collective-permute-start(bf16[10,128]{1,0:T(8,128)(2,1)S(1)} %concatenate.46), channel_id=1, source_target_pairs={{0,1},{1,2},{2,3},{3,4},{4,5},{5,6},{6,7},{7,0},{8,9},{9,10},{10,1... | collective-permute-start | bytes 7688 | tf_op jit(solution)/shard_map/ppermute | solution.py:76
  4.7 29.7 %collective-permute-start.5 = (bf16[10,128]{1,0:T(8,128)(2,1)S(1)}, bf16[10,128]{1,0:T(8,128)(2,1)S(1)}, u32[]{:S(2)}, u32[]{:S(2)}) collective-permute-start(bf16[10,128]{1,0:T(8,128)(2,1)S(1)} %concatenate.46), channel_id=1, source_target_pairs={{0,2},{1,3},{2,4},{3,5},{4,6},{5,7},{6,0},{7,1},{8,10},{9,11},{10,... | collective-permute-start | bytes 7688 | tf_op jit(solution)/shard_map/ppermute | solution.py:76
  71.0 30.4 %collective-permute-start.44 = (bf16[128,1024]{1,0:T(8,128)(2,1)}, bf16[128,1024]{1,0:T(8,128)(2,1)}, u32[]{:S(2)}, u32[]{:S(2)}) collective-permute-start(bf16[128,1024]{1,0:T(8,128)(2,1)} %constant_dynamic-slice_fusion), channel_id=1, source_target_pairs={{0,6},{1,7},{2,0},{3,1},{4,2},{5,3},{6,4},{7,5},{8,14},{9,15},{10,... | collective-permute-start | bytes 786440 | tf_op jit(solution)/shard_map/ppermute | solution.py:76
  71.1 33.4 %collective-permute-start.46 = (bf16[128,1024]{1,0:T(8,128)(2,1)}, bf16[128,1024]{1,0:T(8,128)(2,1)}, u32[]{:S(2)}, u32[]{:S(2)}) collective-permute-start(bf16[128,1024]{1,0:T(8,128)(2,1)} %constant_dynamic-slice_fusion), channel_id=1, source_target_pairs={{0,2},{1,3},{2,4},{3,5},{4,6},{5,7},{6,0},{7,1},{8,10},{9,11},{10,... | collective-permute-start | bytes 786440 | tf_op jit(solution)/shard_map/ppermute | solution.py:76
  72.5 37.6 %collective-permute-start.35 = (bf16[32,4096]{1,0:T(8,128)(2,1)}, bf16[32,4096]{1,0:T(8,128)(2,1)}, u32[]{:S(2)}, u32[]{:S(2)}) collective-permute-start(bf16[32,4096]{1,0:T(8,128)(2,1)} %constant_dynamic-slice_fusion.1), channel_id=1, source_target_pairs={{0,4},{1,5},{2,6},{3,7},{4,0},{5,1},{6,2},{7,3},{8,12},{9,13},{10,... | collective-permute-start | bytes 786440 | tf_op jit(solution)/shard_map/ppermute | solution.py:76
  74.4 35.8 %collective-permute-start.27 = (bf16[4,32,1024]{2,1,0:T(8,128)(2,1)}, bf16[4,32,1024]{2,1,0:T(8,128)(2,1)}, u32[]{:S(2)}, u32[]{:S(2)}) collective-permute-start(bf16[4,32,1024]{2,1,0:T(8,128)(2,1)} %pad_maximum_fusion.3.refs_0_), channel_id=1, source_target_pairs={{0,1},{1,0},{2,3},{3,2},{4,5},{5,4},{6,7},{7,6},{8,24},{9,25},{10,... | collective-permute-start | bytes 786440 | tf_op jit(solution)/shard_map/ppermute | solution.py:76
  121.2 40.3 %collective-permute-start.37 = (bf16[4,32,4096]{2,1,0:T(8,128)(2,1)S(1)}, bf16[4,32,4096]{2,1,0:T(8,128)(2,1)S(1)}, u32[]{:S(2)}, u32[]{:S(2)}) collective-permute-start(bf16[4,32,4096]{2,1,0:T(8,128)(2,1)S(1)} %pad_maximum_fusion.refs_0_), channel_id=1, source_target_pairs={{0,1},{1,0},{2,3},{3,2},{4,5},{5,4},{6,7},{7,6},{8,24},{9,25},{10,... | collective-permute-start | bytes 3145736 | tf_op jit(solution)/shard_map/ppermute | solution.py:76
  122.6 39.0 %collective-permute-start.40 = (bf16[4,32,4096]{2,1,0:T(8,128)(2,1)S(1)}, bf16[4,32,4096]{2,1,0:T(8,128)(2,1)S(1)}, u32[]{:S(2)}, u32[]{:S(2)}) collective-permute-start(bf16[4,32,4096]{2,1,0:T(8,128)(2,1)S(1)} %pad_maximum_fusion.refs_0_), channel_id=1, source_target_pairs={{0,8},{1,9},{2,10},{3,11},{4,12},{5,13},{6,14},{7,15},{8,0},{9,1},... | collective-permute-start | bytes 3145736 | tf_op jit(solution)/shard_map/ppermute | solution.py:76
  124.4 38.6 %collective-permute-start.38 = (bf16[4,32,4096]{2,1,0:T(8,128)(2,1)S(1)}, bf16[4,32,4096]{2,1,0:T(8,128)(2,1)}, u32[]{:S(2)}, u32[]{:S(2)}) collective-permute-start(bf16[4,32,4096]{2,1,0:T(8,128)(2,1)S(1)} %pad_maximum_fusion.refs_0_), channel_id=1, source_target_pairs={{0,16},{1,17},{2,18},{3,19},{4,20},{5,21},{6,22},{7,23},{8,9},{9,8... | collective-permute-start | bytes 3145736 | tf_op jit(solution)/shard_map/ppermute | solution.py:76
  126.0 34.3 %collective-permute-start.11 = (bf16[4,32,3072]{2,1,0:T(8,128)(2,1)S(1)}, bf16[4,32,3072]{2,1,0:T(8,128)(2,1)S(1)}, u32[]{:S(2)}, u32[]{:S(2)}) collective-permute-start(bf16[4,32,3072]{2,1,0:T(8,128)(2,1)S(1)} %pad_maximum_fusion.2.refs_0_), channel_id=1, source_target_pairs={{0,16},{1,17},{2,18},{3,19},{4,20},{5,21},{6,22},{7,23},{8,9},{9,8... | collective-permute-start | bytes 2359304 | tf_op jit(solution)/shard_map/ppermute | solution.py:76
  130.3 43.8 %collective-permute-start.12 = (bf16[4,32,3072]{2,1,0:T(8,128)(2,1)S(1)}, bf16[4,32,3072]{2,1,0:T(8,128)(2,1)S(1)}, u32[]{:S(2)}, u32[]{:S(2)}) collective-permute-start(bf16[4,32,3072]{2,1,0:T(8,128)(2,1)S(1)} %collective-permute-done.10.refs_1_), channel_id=1, source_target_pairs={{0,16},{1,17},{2,18},{3,19},{4,20},{5,21},{6,22},{7,23},{8,9},{9,8... | collective-permute-start | bytes 2359304 | tf_op jit(solution)/shard_map/ppermute | solution.py:76
  161.6 29.8 %collective-permute-start.39 = (bf16[4,32,4096]{2,1,0:T(8,128)(2,1)S(1)}, bf16[4,32,4096]{2,1,0:T(8,128)(2,1)}, u32[]{:S(2)}, u32[]{:S(2)}) collective-permute-start(bf16[4,32,4096]{2,1,0:T(8,128)(2,1)S(1)} %collective-permute-done.37.refs_1_), channel_id=1, source_target_pairs={{0,16},{1,17},{2,18},{3,19},{4,20},{5,21},{6,22},{7,23},{8,9},{9,8... | collective-permute-start | bytes 3145736 | tf_op jit(solution)/shard_map/ppermute | solution.py:76
  185.7 37.8 %collective-permute-start.48 = (bf16[4,128,1024]{2,1,0:T(8,128)(2,1)S(1)}, bf16[4,128,1024]{2,1,0:T(8,128)(2,1)}, u32[]{:S(2)}, u32[]{:S(2)}) collective-permute-start(bf16[4,128,1024]{2,1,0:T(8,128)(2,1)S(1)} %pad_maximum_fusion.1.refs_0_), channel_id=1, source_target_pairs={{0,16},{1,17},{2,18},{3,19},{4,20},{5,21},{6,22},{7,23},{8,9},{9,8... | collective-permute-start | bytes 3145736 | tf_op jit(solution)/shard_map/ppermute | solution.py:76
  185.7 38.4 %collective-permute-start.41 = (bf16[4,32,4096]{2,1,0:T(8,128)(2,1)S(1)}, bf16[4,32,4096]{2,1,0:T(8,128)(2,1)}, u32[]{:S(2)}, u32[]{:S(2)}) collective-permute-start(bf16[4,32,4096]{2,1,0:T(8,128)(2,1)S(1)} %collective-permute-done.37.refs_1_), channel_id=1, source_target_pairs={{0,8},{1,9},{2,10},{3,11},{4,12},{5,13},{6,14},{7,15},{8,0},{9,1},... | collective-permute-start | bytes 3145736 | tf_op jit(solution)/shard_map/ppermute | solution.py:76
  187.9 35.7 %collective-permute-start.42 = (bf16[4,32,4096]{2,1,0:T(8,128)(2,1)}, bf16[4,32,4096]{2,1,0:T(8,128)(2,1)}, u32[]{:S(2)}, u32[]{:S(2)}) collective-permute-start(bf16[4,32,4096]{2,1,0:T(8,128)(2,1)} %collective-permute-done.38.refs_2_), channel_id=1, source_target_pairs={{0,8},{1,9},{2,10},{3,11},{4,12},{5,13},{6,14},{7,15},{8,0},{9,1},... | collective-permute-start | bytes 3145736 | tf_op jit(solution)/shard_map/ppermute | solution.py:76
  191.3 32.9 %collective-permute-start.49 = (bf16[4,128,1024]{2,1,0:T(8,128)(2,1)S(1)}, bf16[4,128,1024]{2,1,0:T(8,128)(2,1)}, u32[]{:S(2)}, u32[]{:S(2)}) collective-permute-start(bf16[4,128,1024]{2,1,0:T(8,128)(2,1)S(1)} %collective-permute-done.47.refs_1_), channel_id=1, source_target_pairs={{0,16},{1,17},{2,18},{3,19},{4,20},{5,21},{6,22},{7,23},{8,9},{9,8... | collective-permute-start | bytes 3145736 | tf_op jit(solution)/shard_map/ppermute | solution.py:76
  191.3 33.3 %collective-permute-start.43 = (bf16[4,32,4096]{2,1,0:T(8,128)(2,1)}, bf16[4,32,4096]{2,1,0:T(8,128)(2,1)}, u32[]{:S(2)}, u32[]{:S(2)}) collective-permute-start(bf16[4,32,4096]{2,1,0:T(8,128)(2,1)} %collective-permute-done.39.refs_3_), channel_id=1, source_target_pairs={{0,8},{1,9},{2,10},{3,11},{4,12},{5,13},{6,14},{7,15},{8,0},{9,1},... | collective-permute-start | bytes 3145736 | tf_op jit(solution)/shard_map/ppermute | solution.py:76
  223.5 29.9 %collective-permute-start.50 = (bf16[4,128,1024]{2,1,0:T(8,128)(2,1)S(1)}, bf16[4,128,1024]{2,1,0:T(8,128)(2,1)S(1)}, u32[]{:S(2)}, u32[]{:S(2)}) collective-permute-start(bf16[4,128,1024]{2,1,0:T(8,128)(2,1)S(1)} %pad_maximum_fusion.1.refs_0_), channel_id=1, source_target_pairs={{0,8},{1,9},{2,10},{3,11},{4,12},{5,13},{6,14},{7,15},{8,0},{9,1},... | collective-permute-start | bytes 3145736 | tf_op jit(solution)/shard_map/ppermute | solution.py:76
  223.6 29.8 %collective-permute-start.51 = (bf16[4,128,1024]{2,1,0:T(8,128)(2,1)S(1)}, bf16[4,128,1024]{2,1,0:T(8,128)(2,1)}, u32[]{:S(2)}, u32[]{:S(2)}) collective-permute-start(bf16[4,128,1024]{2,1,0:T(8,128)(2,1)S(1)} %collective-permute-done.47.refs_1_), channel_id=1, source_target_pairs={{0,8},{1,9},{2,10},{3,11},{4,12},{5,13},{6,14},{7,15},{8,0},{9,1},... | collective-permute-start | bytes 3145736 | tf_op jit(solution)/shard_map/ppermute | solution.py:76
  224.1 29.3 %collective-permute-start.52 = (bf16[4,128,1024]{2,1,0:T(8,128)(2,1)}, bf16[4,128,1024]{2,1,0:T(8,128)(2,1)S(1)}, u32[]{:S(2)}, u32[]{:S(2)}) collective-permute-start(bf16[4,128,1024]{2,1,0:T(8,128)(2,1)} %collective-permute-done.48.refs_2_), channel_id=1, source_target_pairs={{0,8},{1,9},{2,10},{3,11},{4,12},{5,13},{6,14},{7,15},{8,0},{9,1},... | collective-permute-start | bytes 3145736 | tf_op jit(solution)/shard_map/ppermute | solution.py:76
  339.0 50.1 %collective-permute-start.54 = (f32[8,9,128]{2,1,0:T(8,128)S(1)}, f32[8,9,128]{2,1,0:T(8,128)S(1)}, u32[]{:S(2)}, u32[]{:S(2)}) collective-permute-start(f32[8,9,128]{2,1,0:T(8,128)S(1)} %concatenate.50), channel_id=1, source_target_pairs={{0,8},{1,9},{2,10},{3,11},{4,12},{5,13},{6,14},{7,15},{8,0},{9,1},... | collective-permute-start | bytes 110600 | tf_op jit(solution)/shard_map/ppermute | solution.py:76
  339.3 49.0 %collective-permute-start.78 = (bf16[8,1152]{1,0:T(8,128)(2,1)S(1)}, bf16[8,1152]{1,0:T(8,128)(2,1)S(1)}, u32[]{:S(2)}, u32[]{:S(2)}) collective-permute-start(bf16[8,1152]{1,0:T(8,128)(2,1)S(1)} %get-tuple-element.107), channel_id=1, source_target_pairs={{0,8},{1,9},{2,10},{3,11},{4,12},{5,13},{6,14},{7,15},{8,0},{9,1},... | collective-permute-start | bytes 55304 | tf_op jit(solution)/shard_map/ppermute | solution.py:76
  343.8 69.7 %collective-permute-start.69 = (bf16[4,4,32,1024]{3,2,1,0:T(8,128)(2,1)}, bf16[4,4,32,1024]{3,2,1,0:T(8,128)(2,1)S(1)}, u32[]{:S(2)}, u32[]{:S(2)}) collective-permute-start(bf16[4,4,32,1024]{3,2,1,0:T(8,128)(2,1)} %weight_grad.8), channel_id=1, source_target_pairs={{0,8},{1,9},{2,10},{3,11},{4,12},{5,13},{6,14},{7,15},{8,0},{9,1},... | collective-permute-start | bytes 3145736 | tf_op jit(solution)/shard_map/ppermute | solution.py:76
  352.2 66.8 %collective-permute-start.60 = (bf16[4,4,32,3072]{3,2,1,0:T(8,128)(2,1)}, bf16[4,4,32,3072]{3,2,1,0:T(8,128)(2,1)}, u32[]{:S(2)}, u32[]{:S(2)}) collective-permute-start(bf16[4,4,32,3072]{3,2,1,0:T(8,128)(2,1)} %weight_grad.6), channel_id=1, source_target_pairs={{0,8},{1,9},{2,10},{3,11},{4,12},{5,13},{6,14},{7,15},{8,0},{9,1},... | collective-permute-start | bytes 9437192 | tf_op jit(solution)/shard_map/ppermute | solution.py:76
  363.1 88.9 %collective-permute-start.84 = (bf16[4,4,32,4096]{3,2,1,0:T(8,128)(2,1)}, bf16[4,4,32,4096]{3,2,1,0:T(8,128)(2,1)}, u32[]{:S(2)}, u32[]{:S(2)}) collective-permute-start(bf16[4,4,32,4096]{3,2,1,0:T(8,128)(2,1)} %weight_grad.10), channel_id=1, source_target_pairs={{0,8},{1,9},{2,10},{3,11},{4,12},{5,13},{6,14},{7,15},{8,0},{9,1},... | collective-permute-start | bytes 12582920 | tf_op jit(solution)/shard_map/ppermute | solution.py:76
  396.8 81.1 %collective-permute-start.93 = (bf16[4,4,128,1024]{3,2,1,0:T(8,128)(2,1)}, bf16[4,4,128,1024]{3,2,1,0:T(8,128)(2,1)}, u32[]{:S(2)}, u32[]{:S(2)}) collective-permute-start(bf16[4,4,128,1024]{3,2,1,0:T(8,128)(2,1)} %down_grad.2), channel_id=1, source_target_pairs={{0,8},{1,9},{2,10},{3,11},{4,12},{5,13},{6,14},{7,15},{8,0},{9,1},... | collective-permute-start | bytes 12582920 | tf_op jit(solution)/shard_map/ppermute | solution.py:76
  451.4 37.5 %collective-permute-start.62 = (bf16[4,32,3072]{2,1,0:T(8,128)(2,1)S(1)}, bf16[4,32,3072]{2,1,0:T(8,128)(2,1)}, u32[]{:S(2)}, u32[]{:S(2)}) collective-permute-start(bf16[4,32,3072]{2,1,0:T(8,128)(2,1)S(1)} %fusion.4), channel_id=1, source_target_pairs={{0,16},{1,17},{2,18},{3,19},{4,20},{5,21},{6,22},{7,23},{8,9},{9,8... | collective-permute-start | bytes 2359304 | tf_op jit(solution)/shard_map/ppermute | solution.py:76
  463.0 46.6 %collective-permute-start.85 = (bf16[2,4,32,4096]{3,2,1,0:T(8,128)(2,1)}, bf16[2,4,32,4096]{3,2,1,0:T(8,128)(2,1)S(1)}, u32[]{:S(2)}, u32[]{:S(2)}) collective-permute-start(bf16[2,4,32,4096]{3,2,1,0:T(8,128)(2,1)} %get-tuple-element.64), channel_id=1, source_target_pairs={{0,1},{1,0},{2,3},{3,2},{4,5},{5,4},{6,7},{7,6},{8,24},{9,25},{10,... | collective-permute-start | bytes 6291464 | tf_op jit(solution)/shard_map/ppermute | solution.py:76
  488.6 38.9 %collective-permute-start.94 = (bf16[2,4,128,1024]{3,2,1,0:T(8,128)(2,1)}, bf16[2,4,128,1024]{3,2,1,0:T(8,128)(2,1)S(1)}, u32[]{:S(2)}, u32[]{:S(2)}) collective-permute-start(bf16[2,4,128,1024]{3,2,1,0:T(8,128)(2,1)} %get-tuple-element.66), channel_id=1, source_target_pairs={{0,1},{1,0},{2,3},{3,2},{4,5},{5,4},{6,7},{7,6},{8,24},{9,25},{10,... | collective-permute-start | bytes 6291464 | tf_op jit(solution)/shard_map/ppermute | solution.py:76
  545.6 29.5 %collective-permute-start.98 = (bf16[128,1024]{1,0:T(8,128)(2,1)S(1)}, bf16[128,1024]{1,0:T(8,128)(2,1)S(1)}, u32[]{:S(2)}, u32[]{:S(2)}) collective-permute-start(bf16[128,1024]{1,0:T(8,128)(2,1)S(1)} %get-tuple-element.68), channel_id=1, source_target_pairs={{0,6},{1,7},{2,0},{3,1},{4,2},{5,3},{6,4},{7,5},{8,14},{9,15},{10,... | collective-permute-start | bytes 786440 | tf_op jit(solution)/shard_map/ppermute | solution.py:76
  547.0 31.4 %collective-permute-start.97 = (bf16[128,1024]{1,0:T(8,128)(2,1)S(1)}, bf16[128,1024]{1,0:T(8,128)(2,1)S(1)}, u32[]{:S(2)}, u32[]{:S(2)}) collective-permute-start(bf16[128,1024]{1,0:T(8,128)(2,1)S(1)} %get-tuple-element.69), channel_id=1, source_target_pairs={{0,4},{1,5},{2,6},{3,7},{4,0},{5,1},{6,2},{7,3},{8,12},{9,13},{10,... | collective-permute-start | bytes 786440 | tf_op jit(solution)/shard_map/ppermute | solution.py:76
  557.0 30.5 %collective-permute-start.90 = (bf16[32,4096]{1,0:T(8,128)(2,1)S(1)}, bf16[32,4096]{1,0:T(8,128)(2,1)S(1)}, u32[]{:S(2)}, u32[]{:S(2)}) collective-permute-start(bf16[32,4096]{1,0:T(8,128)(2,1)S(1)} %fusion.19), channel_id=1, source_target_pairs={{0,8},{1,9},{2,10},{3,11},{4,12},{5,13},{6,14},{7,15},{8,0},{9,1},... | collective-permute-start | bytes 786440 | tf_op jit(solution)/shard_map/ppermute | solution.py:76
  (114 other events, 1990.7 us)

commit v2 on v1

v2 whole, which is shorter than its diff:
```python
import functools
import math

import jax
import jax.numpy as jnp
from jax import lax
from jax.experimental import pallas as pl
from jax.experimental.pallas import tpu as pltpu
from jax.sharding import PartitionSpec as P

HEAD_DIM = 64
EPSILON = 1e-05
BOTH = ("group", "wide")
F32 = jnp.float32
BF16 = jnp.bfloat16
BLOCKS = 32
VMEM_BYTES = 58 * 2**20


def sum_of(*terms):
    total = terms[0].astype(F32)
    for term in terms[1:]:
        total = total + term.astype(F32)
    return total.astype(BF16)


def tie(*values):
    return lax.optimization_barrier(values)


def dot(a, b):
    return jnp.dot(a, b, preferred_element_type=F32)


def dot_nt(a, b):
    return lax.dot_general(a, b, (((1,), (1,)), ((), ())), preferred_element_type=F32)


def dot_tn(a, b):
    return lax.dot_general(a, b, (((0,), (0,)), ((), ())), preferred_element_type=F32)


class Plan:
    def __init__(self):
        def pairs(target):
            found = []
            for index in range(32):
                group, wide = divmod(index, 8)
                y, core, z, x = target(group // 2, group % 2, wide // 2, wide % 2)
                found.append((index, (y * 2 + core) * 8 + z * 2 + x))
            return found

        self.core_pairs = pairs(lambda y, c, z, x: (y, 1 - c, z, x))
        self.y_pairs = pairs(lambda y, c, z, x: (1 - y, c, z, x))
        self.x_pairs = pairs(lambda y, c, z, x: (y, c, z, 1 - x))
        self.first_pairs = pairs(lambda y, c, z, x: (y, c, z, 1 - x) if c == 0 else (1 - y, c, z, x))
        self.second_pairs = pairs(lambda y, c, z, x: (1 - y, c, z, x) if c == 0 else (y, c, z, 1 - x))
        self.z_groups = [[(y * 2 + c) * 8 + z * 2 + x for z in range(4)] for y in (0, 1) for c in (0, 1) for x in (0, 1)]
        self.z_pairs = [pairs(lambda y, c, z, x, step=step: (y, c, (z - step) % 4, x)) for step in range(4)]

    def enter(self):
        self.group = lax.axis_index("group")
        self.wide = lax.axis_index("wide")
        y, core = self.group // 2, self.group % 2
        z, x = self.wide // 2, self.wide % 2
        self.z, self.x, self.y, self.core = z, x, y, core
        slot = jnp.arange(BLOCKS, dtype=jnp.int32)
        holder = core ^ (slot // 16)
        second, first, step = (slot // 8) % 2, (slot // 4) % 2, slot % 4
        across = jnp.where(holder == 0, first, second)
        along = jnp.where(holder == 0, second, first)
        spot = (x ^ across) * 4 + (y ^ along) * 2 + holder
        places, near_places = step * 8 + spot, ((z + step) % 4) * 8 + spot
        block_z, block_x, block_y, block_core = slot // 8, (slot // 4) % 2, (slot // 2) % 2, slot % 2
        off_x, off_y = block_x ^ x, block_y ^ y
        first = jnp.where(block_core == 0, off_x, off_y)
        second = jnp.where(block_core == 0, off_y, off_x)
        spot = (((block_core ^ core) * 2 + second) * 2 + first) * 4
        tables = places, near_places, spot + block_z, spot + (block_z - z) % 4
        return [table.astype(jnp.int32) for table in tables]

    def move(self, value, pairs):
        return lax.ppermute(value, BOTH, pairs)

    def own_block(self, shard):
        rows = shard.shape[0] // 4
        return lax.dynamic_slice_in_dim(shard, self.group * rows, rows, 0)

    def along_z(self, own):
        return lax.all_gather(own, BOTH, axis_index_groups=self.z_groups, axis=0)

    def near_z(self, own):
        return [own] + [self.move(own, self.z_pairs[step]) for step in (1, 2, 3)]

    def first(self, value):
        return self.move(value, self.first_pairs)

    def second(self, value):
        return self.move(value, self.second_pairs)

    def across(self, value):
        return self.move(value, self.core_pairs)

    def over_z(self, part):
        return lax.psum_scatter(part, BOTH, axis_index_groups=self.z_groups, scatter_dimension=0)

    def over_group(self, own):
        return lax.all_gather(own, "group", axis=0, tiled=True)

    def to_z(self, *weights):
        def part(step):
            return jnp.concatenate([sum_of(*[term[step] for term in terms]) for terms in weights], axis=1)

        return [part(0)] + [self.move(part(step), self.z_pairs[4 - step]) for step in (1, 2, 3)]

    def in_group(self, own):
        along = self.move(own, self.y_pairs)
        parts = [own, self.across(own), along, self.across(along)]
        parts = [jnp.where(self.core == 0, parts[i], parts[i ^ 1]) for i in range(4)]
        return jnp.concatenate([jnp.where(self.y == 0, parts[i], parts[i ^ 2]) for i in range(4)])

    def in_wide_order(self, near):
        near = jnp.where(self.x == 0, near, near[:, ::-1])
        near = lax.dynamic_slice_in_dim(jnp.concatenate([near, near]), (4 - self.z) % 4, 4, 0)
        return near.reshape((8,) + near.shape[2:])

    def sum_x(self, pair):
        return pair[0] + self.move(pair[1], self.x_pairs)

    def sum_z(self, near):
        total = near[0]
        for step in (1, 2, 3):
            total = total + self.move(near[step], self.z_pairs[4 - step])
        return total


def rotary_tables(length):
    half = HEAD_DIM // 2
    frequency = jnp.exp(jnp.arange(half, dtype=F32) * (-2.0 * math.log(10000.0) / HEAD_DIM))
    angles = jnp.arange(length, dtype=F32)[:, None] * frequency[None, :]
    sine = jnp.sin(angles)
    cosine = jnp.concatenate([jnp.cos(angles)] * 4, axis=1)
    return cosine, jnp.concatenate([-sine, sine, -sine, sine], axis=1)


def call(kernel, name, tables, grid, ins, outs, scratch=(), flops=0, moved=0):
    def spec(block, index, buffers=None):
        if buffers:
            return pl.BlockSpec(block, index, pipeline_mode=pl.Buffered(buffers))
        return pl.BlockSpec(block, index)

    return pl.pallas_call(
        kernel,
        out_shape=[jax.ShapeDtypeStruct(shape, dtype) for shape, dtype, *_ in outs],
        grid_spec=pltpu.PrefetchScalarGridSpec(
            num_scalar_prefetch=len(tables),
            grid=grid,
            in_specs=[spec(*rest) for _, *rest in ins],
            out_specs=[spec(*rest) for _, _, *rest in outs],
            scratch_shapes=list(scratch),
        ),
        compiler_params=pltpu.CompilerParams(vmem_limit_bytes=VMEM_BYTES),
        cost_estimate=pl.CostEstimate(flops=0, bytes_accessed=0, transcendentals=0),
        name=name,
    )(*tables, *[array for array, *_ in ins])


def whole(array, buffers=1):
    rank = array.ndim
    return (array, array.shape, lambda i, *_: (0,) * rank, buffers)


def columns_at(array, first, count):
    return (array, array.shape[:-1] + (count,), lambda i, *_: (0,) * (array.ndim - 1) + (first // count,), 1)


def rows_of(array, tile):
    return (array, (tile, array.shape[1]), lambda i, *_: (i, 0))


def out_rows(shape, dtype, tile):
    return (shape, dtype, (tile, shape[1]), lambda i, *_: (i, 0))


def out_whole(shape, dtype):
    return (shape, dtype, shape, lambda i, *_: (0,) * len(shape), 1)


def put_in_order(places, pieces, held):
    for i in range(BLOCKS):
        held[places[i]] = pieces[i // 4][i % 4]


def matrix(held):
    blocks, rows, columns = held.shape
    return held[...].reshape(blocks * rows, columns)


def normalise(values):
    average = jnp.mean(values, axis=-1, keepdims=True)
    centered = values - average
    scale = lax.rsqrt(jnp.mean(centered * centered, axis=-1, keepdims=True) + EPSILON)
    return centered * scale, scale


def norm_back(grad, hat, scale, gain):
    e = grad * gain
    inner = jnp.mean(e * hat, axis=-1, keepdims=True)
    return scale * (e - jnp.mean(e, axis=-1, keepdims=True) - hat * inner)


def turned(values):
    lane = lax.broadcasted_iota(jnp.int32, values.shape, 1)
    return jnp.where(lane % 64 < 32, pltpu.roll(values, 96, 1), pltpu.roll(values, 32, 1))


def heads(values):
    lane = lax.broadcasted_iota(jnp.int32, values.shape, 1)
    zero = jnp.zeros_like(values)
    return jnp.concatenate([jnp.where(lane < 64, values, zero), jnp.where(lane < 64, zero, values)], axis=0)


def put_turned(out, slots, values):
    rows = out.shape[1]
    flipped = values.T
    for j in range(BLOCKS):
        out[slots[j]] = flipped[j * rows : (j + 1) * rows]


def attention_kernel(length, places, slots, tokens, gain, shift, cosine, sine, *refs):
    pieces, (act_turned, qkv, attended, attended_turned), held = refs[:8], refs[8:12], refs[12]
    rows, width = tokens.shape

    @pl.when(pl.program_id(0) == 0)
    def _():
        put_in_order(places, pieces, held)

    hat, _ = normalise(tokens[...].astype(F32))
    act = (hat * gain[...] + shift[...]).astype(BF16)
    put_turned(act_turned, slots, act)
    cos, sin = cosine[...], sine[...]
    for start in range(0, 3 * width, 512):
        part = dot(act, held[:, :, start : start + 512].reshape(width, 512))
        if start < 2 * width:
            for lanes in range(0, 512, 128):
                piece = part[:, lanes : lanes + 128]
                qkv[:, start + lanes : start + lanes + 128] = (piece * cos + turned(piece) * sin).astype(BF16)
        else:
            qkv[:, start : start + 512] = part.astype(BF16)
    for top in range(0, rows, length):
        for lanes in range(0, width, 128):
            q = qkv[top : top + length, lanes : lanes + 128]
            k = heads(qkv[top : top + length, width + lanes : width + lanes + 128])
            v = heads(qkv[top : top + length, 2 * width + lanes : 2 * width + lanes + 128])
            scores = dot_nt(q, k) * HEAD_DIM ** (-0.5)
            probs = []
            for head in range(2):
                own = scores[:, head * length : (head + 1) * length]
                e = jnp.exp(own - jnp.max(own, axis=-1, keepdims=True))
                probs.append((e / jnp.sum(e, axis=-1, keepdims=True)).astype(BF16))
            out = dot(jnp.concatenate(probs, axis=1), v)
            attended[top : top + length, lanes : lanes + 128] = out.astype(BF16)
    put_turned(attended_turned, slots, attended[...])


def middle_kernel(length, places, near_slots, slots, tokens, attended, scales, gain, shift, *refs):
    pieces, (middle, act, act_turned), held = refs[:8], refs[8:11], refs[11]
    rows = tokens.shape[0]

    @pl.when(pl.program_id(0) == 0)
    def _():
        put_in_order(places, pieces, held)

    values = tokens[...].astype(F32) + dot(attended[...], matrix(held))
    middle[...] = values
    hat, _ = normalise(values)
    normed = hat * gain[...] + shift[...]
    first = pl.program_id(0) * (rows // length)
    for s in range(rows // length):
        act[s * length : (s + 1) * length, :] = (
            normed[s * length : (s + 1) * length, :] * scales[pl.ds(first + s, 1), :]
        ).astype(BF16)
    put_turned(act_turned, slots, act[...])


def split_out(slot, block, theirs, send, keep):
    piece, at = slot // 4, slot % 4

    @pl.when(slot >= BLOCKS // 2)
    def _():
        theirs[piece - 4, at] = block

    @pl.when((slot < BLOCKS // 2) & (piece % 2 == 1))
    def _():
        send[piece // 2, at] = block

    @pl.when((slot < BLOCKS // 2) & (piece % 2 == 0))
    def _():
        keep[piece // 2, at] = block


def up_kernel(places, slots, act, bias, cotangent, *refs):
    pieces, (hidden, slope, theirs, send, keep), held = refs[:8], refs[8:13], refs[13]
    put_in_order(places, pieces, held)
    v = dot(act[...], matrix(held)) + bias[...]
    area = 0.5 + 0.5 * lax.erf(v * math.sqrt(0.5))
    low = (v * area).astype(BF16)
    hidden[...] = low
    slope[...] = (area + v * jnp.exp(-0.5 * v * v) * (1.0 / math.sqrt(2.0 * math.pi))).astype(BF16)
    grad = dot_tn(low, cotangent[...]).astype(BF16)
    rows = theirs.shape[2]
    count = hidden.shape[1] // rows
    for k in range(count):
        split_out(slots[pl.program_id(0) * count + k], grad[k * rows : (k + 1) * rows], theirs, send, keep)


def near_grad_kernel(strips, act_one, grad_projected, attended, grad_branch, theirs, send, keep):
    blocks, rows = act_one.shape[:2]

    @pl.when(pl.program_id(0) < strips)
    def _():
        put_apart(dot(act_one[...].reshape(blocks * rows, -1), grad_projected[...]), rows, theirs, send, keep)

    @pl.when(pl.program_id(0) >= strips)
    def _():
        put_apart(dot(attended[...].reshape(blocks * rows, -1), grad_branch[...]), rows, theirs, send, keep)


def put_apart(total, rows, theirs, send, keep):
    total = total.astype(BF16).reshape(8, 4, rows, -1)
    theirs[...] = total[4:]
    for second in range(2):
        keep[second] = total[2 * second]
        send[second] = total[2 * second + 1]


def feed_back_kernel(length, places, cotangent, slope, turned_act, middle, scales, gain, shift, *refs):
    down, up = refs[:8], refs[8:16]
    theirs, send, keep, bias, grad_middle, grad_branch, grad_scale, gain_sum, shift_sum = refs[16:25]
    held_down, held_up, total = refs[25:]
    step = pl.program_id(0)

    @pl.when(step == 0)
    def _():
        put_in_order(places, down, held_down)
        total[...] = jnp.zeros_like(total)

    put_in_order(places, up, held_up)
    strip = slope.shape[1]
    count = strip // held_down.shape[1]
    rows = held_down[pl.ds(step * count, count)].reshape(strip, -1)
    grad = (dot_nt(cotangent[...], rows) * slope[...].astype(F32)).astype(BF16)
    bias[...] = jnp.sum(grad.astype(F32), axis=0, keepdims=True)
    blocks, deep = turned_act.shape[:2]
    put_apart(dot(turned_act[...].reshape(blocks * deep, -1), grad), deep, theirs, send, keep)
    total[...] += dot_nt(grad, matrix(held_up))

    @pl.when(step == pl.num_programs(0) - 1)
    def _():
        gains, shifts = jnp.zeros_like(gain_sum), jnp.zeros_like(shift_sum)
        for s in range(middle.shape[0] // length):
            at = slice(s * length, (s + 1) * length)
            own = total[at, :]
            hat, scale = normalise(middle[at, :])
            normed = hat * gain[...] + shift[...]
            grad_scale[s : s + 1, :] = jnp.sum(own * normed, axis=0, keepdims=True)
            grad = own * scales[s : s + 1, :]
            gains += jnp.sum(grad * hat, axis=0, keepdims=True)
            shifts += jnp.sum(grad, axis=0, keepdims=True)
            out = cotangent[at, :].astype(F32) + norm_back(grad, hat, scale, gain[...])
            grad_middle[at, :] = out
            grad_branch[at, :] = out.astype(BF16)
        gain_sum[...] = gains
        shift_sum[...] = shifts


def sum_kernel(*refs):
    total = refs[0][...].astype(F32)
    for ref in refs[1:-1]:
        total = total + ref[...].astype(F32)
    refs[-1][...] = total.astype(BF16)


def sum_pieces(count, *terms):
    _, _, rows, columns = terms[0][0].shape
    block = (1, 2, rows, columns)
    ins = [
        (array, block, lambda i, first=first, stride=stride: (first + stride * (i // 2), i % 2, 0, 0))
        for array, first, stride in terms
    ]
    out = ((count, 4, rows, columns), BF16, block, lambda i: (i // 2, i % 2, 0, 0))
    size = count * 4 * rows * columns
    return call(sum_kernel, "sum_pieces", (), (2 * count,), ins, [out], flops=size, moved=2 * size * (len(terms) + 1))[0]


def output_kernel(places, hidden, middle, bias, *refs):
    pieces, output, held = refs[:8], refs[8], refs[9]

    @pl.when(pl.program_id(0) == 0)
    def _():
        put_in_order(places, pieces, held)

    output[...] = (middle[...] + dot(hidden[...], matrix(held)) + bias[...]).astype(BF16)


def attention_grad_kernel(length, places, grad_branch, qkv, cosine, sine, *refs):
    pieces, grad_projected, held, grad_attended = refs[:8], refs[8], refs[9], refs[10]
    rows, width = grad_branch.shape
    factor = HEAD_DIM ** (-0.5)

    @pl.when(pl.program_id(0) == 0)
    def _():
        put_in_order(places, pieces, held)

    grad_attended[...] = dot_nt(grad_branch[...], matrix(held)).astype(BF16)
    cos, sin = cosine[...], sine[...]
    for top in range(0, rows, length):
        at = slice(top, top + length)
        for lanes in range(0, width, 128):
            q = heads(qkv[at, lanes : lanes + 128])
            k = qkv[at, width + lanes : width + lanes + 128]
            v = qkv[at, 2 * width + lanes : 2 * width + lanes + 128]
            g = heads(grad_attended[at, lanes : lanes + 128])
            scores = dot_nt(k, q) * factor
            e = jnp.exp(scores - jnp.max(scores, axis=0, keepdims=True))
            probs = e / jnp.sum(e, axis=0, keepdims=True)
            grad_values = dot(probs.astype(BF16), g)
            grad_probs = dot_nt(v, g)
            inner = jnp.sum(grad_probs * probs, axis=0, keepdims=True)
            grad_scores = (probs * (grad_probs - inner)).astype(BF16)
            grad_keys = dot(grad_scores, q) * factor
            flipped = jnp.concatenate([grad_scores[:, :length].T, grad_scores[:, length:].T], axis=1)
            grad_queries = dot(flipped, heads(k)) * factor
            for start, grad in ((lanes, grad_queries), (width + lanes, grad_keys)):
                grad_projected[at, start : start + 128] = (grad * cos[at] - turned(grad) * sin[at]).astype(BF16)
            grad_projected[at, 2 * width + lanes : 2 * width + lanes + 128] = grad_values.astype(BF16)


def token_grad_kernel(places, grad_projected, tokens, grad_middle, gain, *refs):
    pieces, (grad_tokens, gain_sum, shift_sum), held = refs[:8], refs[8:11], refs[11]

    @pl.when(pl.program_id(0) == 0)
    def _():
        put_in_order(places, pieces, held)
        gain_sum[...] = jnp.zeros_like(gain_sum)
        shift_sum[...] = jnp.zeros_like(shift_sum)

    grad = dot_nt(grad_projected[...], matrix(held))
    hat, scale = normalise(tokens[...].astype(F32))
    gain_sum[...] += jnp.sum(grad * hat, axis=0, keepdims=True)
    shift_sum[...] += jnp.sum(grad, axis=0, keepdims=True)
    grad_tokens[...] = grad_middle[...] + norm_back(grad, hat, scale, gain[...])


class Fallback:
    def vector(self, shard):
        return lax.all_gather(shard, "wide", axis=0, tiled=True).astype(F32)[None]

    def pieces(self, shard):
        full = lax.all_gather(shard, "wide", axis=0, tiled=True)
        return list(full.reshape(8, 4, full.shape[0] // BLOCKS, full.shape[1]))

    def sum(self, grad):
        grad = lax.psum_scatter(grad, "wide", scatter_dimension=0, tiled=True)
        return lax.psum(grad, "group").astype(F32)


class Layer:
    def __init__(self, tokens, cotangent, seqs, ff, places, near_places, slots, near_slots):
        self.tokens, self.cotangent = tokens, cotangent
        self.places, self.near_places, self.slots, self.near_slots = places, near_places, slots, near_slots
        self.rows, self.width = tokens.shape
        self.seqs, self.ff = seqs, ff
        self.length = self.rows // seqs
        self.tile = 2 * self.length
        self.steps = self.rows // self.tile
        self.strip = 512
        self.deep = self.width // BLOCKS
        cosine, sine = rotary_tables(self.length)
        self.tables = [jnp.tile(t, (self.tile // self.length, 1)) for t in (cosine, sine)]

    def held(self, pieces):
        return pltpu.VMEM((BLOCKS,) + pieces[0].shape[1:], BF16)

    def qkv_part(self, pieces):
        return [columns_at(p, 0, 3 * self.width) for p in pieces]

    def out_part(self, pieces):
        return [columns_at(p, 3 * self.width, self.width) for p in pieces]

    def held_part(self, columns):
        return pltpu.VMEM((BLOCKS, self.deep, columns), BF16)

    def turned_out(self):
        return ((BLOCKS, self.deep, self.rows), BF16, (BLOCKS, self.deep, self.tile), lambda i, *_: (0, 0, i))

    def by_rows(self, array):
        return rows_of(array, self.tile)

    def rows_out(self, columns, dtype):
        return out_rows((self.rows, columns), dtype, self.tile)

    def by_columns(self, array):
        return (array, array.shape[:-1] + (self.strip,), lambda i, *_: (0,) * (array.ndim - 1) + (i,))

    def columns_out(self, shape, dtype):
        return (shape, dtype, shape[:-1] + (self.strip,), lambda i, *_: (0,) * (len(shape) - 1) + (i,))

    def attention(self, gain, shift, pieces):
        rows, width = self.rows, self.width
        return call(
            functools.partial(attention_kernel, self.length), "attention", (self.near_places, self.near_slots), (self.steps,),
            [self.by_rows(self.tokens), whole(gain), whole(shift)] + [whole(t) for t in self.tables]
            + self.qkv_part(pieces),
            [self.turned_out(), self.rows_out(3 * width, BF16), self.rows_out(width, BF16), self.turned_out()],
            [self.held_part(3 * width)], flops=12 * rows * width * width, moved=20 * rows * width,
        )

    def middle(self, attended, scales, gain, shift, pieces):
        rows, width = self.rows, self.width
        return call(
            functools.partial(middle_kernel, self.length), "middle", (self.near_places, self.near_slots, self.slots), (self.steps,),
            [self.by_rows(self.tokens), self.by_rows(attended), whole(scales), whole(gain), whole(shift)]
            + self.out_part(pieces),
            [self.rows_out(width, F32), self.rows_out(width, BF16), self.turned_out()],
            [self.held_part(width)], flops=4 * rows * width * width, moved=14 * rows * width,
        )

    def up(self, act, bias, pieces):
        rows, width, ff = self.rows, self.width, self.ff
        fr = ff // BLOCKS
        return call(
            up_kernel, "up", (self.places, self.slots), (ff // self.strip,),
            [whole(act), self.by_columns(bias), whole(self.cotangent)] + [self.by_columns(p) for p in pieces],
            [self.columns_out((rows, ff), BF16)] * 2 + [out_whole((n, 4, fr, width), BF16) for n in (4, 2, 2)],
            [pltpu.VMEM((BLOCKS, self.deep, self.strip), BF16)],
            flops=4 * rows * width * ff, moved=8 * rows * ff,
        )

    def near_grad(self, act_one, grad_projected, attended, grad_branch, half):
        columns, strip = 2 * self.width, self.strip
        strips = 3 * self.width // strip
        at = half * columns // strip
        ins = [
            whole(act_one),
            (grad_projected, (self.rows, strip), lambda i: (0, jnp.minimum(i + at, strips - 1))),
            whole(attended),
            (grad_branch, (self.rows, strip), lambda i: (0, jnp.maximum(i + at - strips, 0))),
        ]
        return call(
            functools.partial(near_grad_kernel, strips - at), "near_grad", (), (columns // strip,), ins,
            [self.columns_out((n, 4, self.deep, columns), BF16) for n in (4, 2, 2)],
            flops=2 * self.rows * self.width * columns, moved=4 * self.rows * columns,
        )

    def feed_back(self, slope, act, middle, scales, gain, shift, down, up):
        rows, width, ff = self.rows, self.width, self.ff
        return call(
            functools.partial(feed_back_kernel, self.length), "feed_back", (self.places,), (ff // self.strip,),
            [whole(self.cotangent), self.by_columns(slope)] + [whole(v) for v in (act, middle, scales, gain, shift)]
            + [whole(p) for p in down] + [self.by_columns(p) for p in up],
            [self.columns_out((n, 4, self.deep, ff), BF16) for n in (4, 2, 2)]
            + [self.columns_out((1, ff), F32), out_whole((rows, width), F32), out_whole((rows, width), BF16)]
            + [out_whole((self.seqs, width), F32)] + [out_whole((1, width), F32)] * 2,
            [self.held(down), pltpu.VMEM((BLOCKS, self.deep, self.strip), BF16), pltpu.VMEM((rows, width), F32)],
            flops=6 * rows * width * ff, moved=10 * rows * ff,
        )

    def output(self, hidden, middle, bias, pieces):
        rows, width = self.rows, self.width
        return call(
            output_kernel, "output", (self.places,), (self.steps,),
            [self.by_rows(hidden), self.by_rows(middle), whole(bias)] + [whole(p) for p in pieces],
            [self.rows_out(width, BF16)],
            [self.held(pieces)], flops=2 * rows * width * self.ff, moved=22 * rows * width,
        )[0]

    def attention_grad(self, grad_branch, qkv, pieces):
        rows, width = self.rows, self.width
        return call(
            functools.partial(attention_grad_kernel, self.length), "attention_grad", (self.near_places,), (self.steps,),
            [self.by_rows(grad_branch), self.by_rows(qkv)] + [whole(t) for t in self.tables] + self.out_part(pieces),
            [self.rows_out(3 * width, BF16)],
            [self.held_part(width), pltpu.VMEM((self.tile, width), BF16)],
            flops=12 * rows * width * width, moved=16 * rows * width,
        )[0]

    def token_grad(self, grad_projected, grad_middle, gain, pieces):
        rows, width = self.rows, self.width
        return call(
            token_grad_kernel, "token_grad", (self.near_places,), (self.steps,),
            [self.by_rows(grad_projected), self.by_rows(self.tokens), self.by_rows(grad_middle), whole(gain)]
            + self.qkv_part(pieces),
            [self.rows_out(width, F32)] + [out_whole((1, width), F32)] * 2,
            [self.held_part(3 * width)], flops=6 * rows * width * width, moved=22 * rows * width,
        )


def chosen(index, table):
    levels = jnp.arange(table.shape[0], dtype=jnp.int32)
    return dot((index[:, None] == levels[None, :]).astype(BF16), table).astype(BF16)


def outer(a, b):
    return lax.dot_general(a, b, (((0,), (0,)), ((), ())), preferred_element_type=F32)


def fallback_shards(tokens, cotangent, noise_index, time_embed, ln1_gain, ln1_shift, w_qkv, w_out, ln2_gain, ln2_shift,
                    w_time, w_up, up_bias, w_down, down_bias):
    net = Fallback()
    order = jnp.arange(BLOCKS, dtype=jnp.int32)
    layer = Layer(tokens, cotangent, noise_index.shape[0], w_up.shape[1], order, order, order, order)
    gain_one, shift_one, gain_two, shift_two, bias_down, bias_up = [
        net.vector(v) for v in (ln1_gain, ln1_shift, ln2_gain, ln2_shift, down_bias, up_bias)
    ]
    embedded = chosen(noise_index, time_embed)
    scales = 1.0 + dot(embedded, lax.all_gather(w_time, "wide", axis=0, tiled=True))
    near_pieces, up_pieces, down_pieces = [
        net.pieces(w) for w in (jnp.concatenate([w_qkv, w_out], axis=1), w_up, w_down)
    ]
    act_one, qkv, attended, attended_turned = layer.attention(gain_one, shift_one, near_pieces)
    middle, act_two, act_two_turned = layer.middle(attended, scales, gain_two, shift_two, near_pieces)
    hidden, slope, *down_terms = layer.up(act_two, bias_up, up_pieces)
    output = layer.output(hidden, middle, bias_down, down_pieces)
    *up_terms, grad_up_bias, grad_middle, grad_branch, grad_scale, grad_gain_two, grad_shift_two = layer.feed_back(
        slope, act_two_turned, middle, scales, gain_two, shift_two, down_pieces, up_pieces
    )
    grad_projected = layer.attention_grad(grad_branch, qkv, near_pieces)
    grad_tokens, grad_gain_one, grad_shift_one = layer.token_grad(grad_projected, grad_middle, gain_one, near_pieces)

    def summed(theirs, send, keep):
        mine = jnp.stack([keep[0], send[0], keep[1], send[1]])
        return net.sum(jnp.concatenate([mine, theirs]).reshape(-1, theirs.shape[-1]))

    grads = (act_one, grad_projected, attended_turned, grad_branch)
    near = jnp.concatenate([summed(*layer.near_grad(*grads, half)) for half in range(2)], axis=1)
    width = tokens.shape[1]
    return (
        output,
        grad_tokens,
        net.sum(grad_gain_one[0]),
        net.sum(grad_shift_one[0]),
        near[:, : 3 * width],
        near[:, 3 * width :],
        net.sum(grad_gain_two[0]),
        net.sum(grad_shift_two[0]),
        net.sum(outer(embedded, grad_scale.astype(BF16))),
        summed(*up_terms),
        net.sum(grad_up_bias[0]),
        summed(*down_terms),
        net.sum(jnp.sum(cotangent.astype(F32), axis=0)),
    )


def plan_shards(plan, tokens, cotangent, noise_index, time_embed, ln1_gain, ln1_shift, w_qkv, w_out, ln2_gain,
                ln2_shift, w_time, w_up, up_bias, w_down, down_bias):
    seqs, per, width = noise_index.shape[0], ln1_gain.shape[0], tokens.shape[1]
    layer = Layer(tokens, cotangent, seqs, w_up.shape[1], *plan.enter())
    first, second, across = plan.first, plan.second, plan.across

    lines = [v.reshape(-1, per) for v in (ln1_gain, ln1_shift, ln2_gain, ln2_shift, down_bias, up_bias)]
    index_line = jnp.pad(noise_index.astype(BF16), (0, per - seqs))[None]
    lines = jnp.concatenate(lines + [index_line])
    lines = jnp.concatenate([lines, plan.move(lines, plan.x_pairs)])
    line_count = lines.shape[0]
    lines = jnp.pad(lines, ((0, w_qkv.shape[0] // 4 - line_count), (0, 0)))
    parts = plan.near_z(jnp.concatenate([plan.own_block(w_qkv), plan.own_block(w_out), lines], axis=1))
    own_up, own_down = plan.own_block(w_up), plan.own_block(w_down)

    *parts, own_up = tie(*parts, own_up)
    near_z = jnp.stack(parts)
    near_1, near_2 = first(near_z), second(near_z)
    up_z = plan.along_z(own_up)
    lines = jnp.stack([part[:line_count, -per:] for part in parts]).reshape(4, 2, -1, per)
    own_levels = lax.dynamic_slice_in_dim(time_embed, plan.wide * per, per, 1)
    index = lines[:, :, -1, :seqs].reshape(-1).astype(jnp.int32)
    partial = plan.sum_z(dot(chosen(index, own_levels), w_time).reshape(4, 2, seqs, width))
    vectors = plan.in_wide_order(lines)
    gain_one, shift_one, gain_two, shift_two, bias_down = [vectors[:, i].reshape(1, -1).astype(F32) for i in range(5)]
    bias_up = vectors[:, 5:-1].reshape(1, -1).astype(F32)

    near_1, near_2, own_down, partial, gain_one, shift_one = tie(near_1, near_2, own_down, partial, gain_one, shift_one)
    near_12, near_1c, near_2c, near_c = second(near_1), across(near_1), across(near_2), across(near_z)
    scales = 1.0 + plan.sum_x(partial)
    down_z = plan.along_z(own_down)

    near_12, near_1c, near_2c, near_c, up_z, scales = tie(near_12, near_1c, near_2c, near_c, up_z, scales)
    near_12c, up_1, up_2 = across(near_12), first(up_z), second(up_z)
    near_pieces = [near_z, near_1, near_2, near_12, near_c, near_1c, near_2c, near_12c]
    act_one, qkv, attended, attended_turned = layer.attention(gain_one, shift_one, near_pieces)

    attended, up_1, up_2 = tie(attended, up_1, up_2)
    up_12, up_c, up_1c, up_2c = second(up_1), across(up_z), across(up_1), across(up_2)
    middle, act_two, act_two_turned = layer.middle(attended, scales, gain_two, shift_two, near_pieces)

    act_two, up_12, up_2c, up_c, up_1c, down_z = tie(act_two, up_12, up_2c, up_c, up_1c, down_z)
    up_12c = across(up_12)
    down_1, down_2, down_c = first(down_z), second(down_z), across(down_z)
    up_pieces = [up_z, up_1, up_2, up_12, up_c, up_1c, up_2c, up_12c]
    hidden, slope, down_theirs, down_send, down_keep = layer.up(act_two, bias_up, up_pieces)

    hidden, slope, down_theirs, down_1, down_2, down_c = tie(hidden, slope, down_theirs, down_1, down_2, down_c)
    down_12, down_sent, down_1c, down_2c = second(down_1), across(down_theirs), across(down_1), across(down_2)

    down_sent, down_1c, down_2c = tie(down_sent, down_1c, down_2c)
    down_sum = sum_pieces(2, (down_send, 0, 1), (down_sent, 1, 2))

    down_sum, down_12, slope = tie(down_sum, down_12, slope)
    down_got, down_12c = first(down_sum), across(down_12)
    down_pieces = [down_z, down_1, down_2, down_12, down_c, down_1c, down_2c, down_12c]
    up_theirs, up_send, up_keep, grad_up_bias, grad_middle, grad_branch, grad_scale, grad_gain_two, grad_shift_two = (
        layer.feed_back(slope, act_two_turned, middle, scales, gain_two, shift_two, down_pieces, up_pieces)
    )

    up_theirs, grad_branch, down_got, grad_scale, cotangent = tie(
        up_theirs, grad_branch, down_got, grad_scale, cotangent
    )
    up_sent = across(up_theirs)
    down_fold = sum_pieces(1, (down_keep, 1, 1), (down_sent, 2, 1), (down_got, 1, 1))[0]
    sums = (grad_gain_two, grad_shift_two, jnp.sum(cotangent.astype(F32), axis=0), grad_up_bias)
    rows = [grad_scale, jnp.broadcast_to(noise_index[:, None], (seqs, 128)).astype(F32)]
    everyone = jnp.concatenate(rows + [v.reshape(seqs, -1) for v in sums], axis=1).astype(BF16)[None]

    up_sent, down_fold, everyone, grad_branch = tie(up_sent, down_fold, everyone, grad_branch)
    down_more = second(down_fold)
    up_fold = sum_pieces(2, (up_send, 0, 1), (up_sent, 1, 2))
    everyone = plan.near_z(everyone)

    up_fold, grad_branch = tie(up_fold, grad_branch)
    up_got = first(up_fold)
    grad_projected = layer.attention_grad(grad_branch, qkv, near_pieces)

    grad_projected, down_more, up_got, *everyone = tie(grad_projected, down_more, up_got, *everyone)
    everyone = jnp.concatenate(everyone)
    more = plan.move(everyone, plan.x_pairs)
    up_fold = sum_pieces(1, (up_keep, 1, 1), (up_sent, 2, 1), (up_got, 1, 1))[0]

    up_fold, grad_projected = tie(up_fold, grad_projected)
    up_more = second(up_fold)
    down_join = sum_pieces(1, (down_keep, 0, 1), (down_sent, 0, 1), (down_got, 0, 1), (down_more[None], 0, 1))[0]

    down_join, grad_projected = tie(down_join, grad_projected)
    grad_w_down = plan.over_z(down_join)
    grads = (act_one, grad_projected, attended_turned, grad_branch)
    low_theirs, low_send, low_keep = layer.near_grad(*grads, 0)

    low_theirs, grad_projected, grad_branch, more = tie(low_theirs, grad_projected, grad_branch, more)
    low_sent = across(low_theirs)
    everyone = jnp.concatenate([everyone, more])
    more = plan.move(everyone, plan.y_pairs)
    high_theirs, high_send, high_keep = layer.near_grad(act_one, grad_projected, attended_turned, grad_branch, 1)

    high_theirs, grad_projected, low_sent = tie(high_theirs, grad_projected, low_sent)
    high_sent = across(high_theirs)
    low_fold = sum_pieces(2, (low_send, 0, 1), (low_sent, 1, 2))

    low_fold, high_sent = tie(low_fold, high_sent)
    low_got = first(low_fold)
    high_fold = sum_pieces(2, (high_send, 0, 1), (high_sent, 1, 2))

    high_fold, up_more, grad_projected = tie(high_fold, up_more, grad_projected)
    high_got = first(high_fold)
    up_join = sum_pieces(1, (up_keep, 0, 1), (up_sent, 0, 1), (up_got, 0, 1), (up_more[None], 0, 1))[0]

    up_join, grad_projected = tie(up_join, grad_projected)
    grad_w_up = plan.over_z(up_join)
    grad_tokens, grad_gain_one, grad_shift_one = layer.token_grad(grad_projected, grad_middle, gain_one, near_pieces)

    grad_tokens, grad_gain_one, grad_shift_one, more, low_got, high_got, grad_w_down, hidden = tie(
        grad_tokens, grad_gain_one, grad_shift_one, more, low_got, high_got, grad_w_down, hidden
    )
    low_fold = sum_pieces(1, (low_keep, 1, 1), (low_sent, 2, 1), (low_got, 1, 1))[0]
    high_fold = sum_pieces(1, (high_keep, 1, 1), (high_sent, 2, 1), (high_got, 1, 1))[0]

    low_fold, high_fold, hidden = tie(low_fold, high_fold, hidden)
    low_more, high_more = second(low_fold), second(high_fold)
    grad_w_down = plan.over_group(grad_w_down)
    everyone = jnp.concatenate([everyone, more])
    more = across(everyone)
    ones = jnp.stack([grad_gain_one.reshape(8, per), grad_shift_one.reshape(8, per)], axis=1)
    ones_z = plan.near_z(ones)
    output = layer.output(hidden, middle, bias_down, down_pieces)

    output, low_more, high_more, grad_w_up, more, *ones_z = tie(output, low_more, high_more, grad_w_up, more, *ones_z)
    parts = plan.to_z(
        [low_keep[0], low_sent[0], low_got[0], low_more], [high_keep[0], high_sent[0], high_got[0], high_more]
    )
    grad_w_up = plan.over_group(grad_w_up)
    ones = sum(ones_z)
    ones = ones + across(ones)
    ones = ones + plan.move(ones, plan.x_pairs)
    ones = ones + plan.move(ones, plan.y_pairs)
    ones = lax.dynamic_index_in_dim(ones, plan.wide, 0, keepdims=False)
    everyone = jnp.concatenate([everyone, more])
    rest = everyone[..., width:].astype(F32)
    picked = chosen(rest[..., 0].reshape(-1).astype(jnp.int32), own_levels)
    grad_w_time = outer(picked, everyone[..., :width].reshape(-1, width))
    rest = jnp.sum(lax.dynamic_index_in_dim(rest, plan.wide, 1, keepdims=False)[:, 128:], axis=0)
    gain_sum, shift_sum, down_sum, up_sum = jnp.split(rest, (per, 2 * per, 3 * per))
    grad_w_down = grad_w_down.astype(F32)

    ones, grad_w_time, grad_w_down, grad_w_up, *parts = tie(ones, grad_w_time, grad_w_down, grad_w_up, *parts)
    near = plan.in_group(sum_of(*parts))
    grad_w_up = grad_w_up.astype(F32)

    near, grad_w_up = tie(near, grad_w_up)
    near = near.astype(F32)
    return (output, grad_tokens, ones[0], ones[1], near[:, : 3 * width], near[:, 3 * width :], gain_sum, shift_sum,
            grad_w_time, grad_w_up, up_sum, grad_w_down, down_sum)


def solution(mesh):
    fits = (mesh.shape["group"], mesh.shape["wide"]) == (4, 8)
    shards = functools.partial(plan_shards, Plan()) if fits else fallback_shards
    split, rows, line = P(BOTH, None), P("wide", None), P("wide")
    in_specs = (split, split, P(BOTH), P(), line, line, rows, rows, line, line, rows, rows, line, rows, line)
    out_specs = (split, split, line, line, rows, rows, line, line, rows, rows, line, rows, line)
    return jax.shard_map(shards, mesh=mesh, in_specs=in_specs, out_specs=out_specs, check_vma=False)
```

time: 603 us -> 447 us (0.74); the launches traced: 591 us -> 443 us
  waiting for transfers between devices: 193 us -> 113 us
  starting transfers between devices: 118 us -> 43.2 us
  between operations: 1.59 us -> 15.2 us
    ppermute x102 -> x59, waiting for transfers between devices: 193 us -> 113 us  [move(): return lax.ppermute(value, BOTH, pairs)]
    ppermute x102 -> x59, starting transfers between devices: 118 us -> 42.4 us  [move(): return lax.ppermute(value, BOTH, pairs)]
    pallas_call x16 -> x19, Pallas kernels: 223 us -> 220 us  [call(): pl.pallas_call(kernel, out_shape=[jax.ShapeDtypeStruct(shape, dtype) for...]
    convert_element_type x21 -> x10, other arithmetic: 14 us -> 11.1 us  [the longest x3 5.44 us: sum_of(): return total.astype(BF16)]
    unnamed x107 -> x100, local copies, waits for them, and re-layouts: 10.9 us -> 13 us
  transfers between devices with their start and end apart: 102 -> 65, of which waited for: 35 -> 23; matrix products, arithmetic and copies ran while one was open for 8% -> 8% of each run, Pallas kernels for 24% -> 49%
where the time goes in v2:
time: 447 us; the launch traced here: 443 us
  Pallas kernels  220 us (49%)
  waiting for transfers between devices  113 us (25%)
  starting transfers between devices  43.2 us (10%)
  local copies, waits for them, and re-layouts  27.5 us (6%)
  other arithmetic  19.9 us (4%)
  between operations  15.2 us (3%)
    pallas_call x19, Pallas kernels, call(): pl.pallas_call(kernel, out_shape=[jax.ShapeDtypeStruct(shape, dtype) for...  220 us
    ppermute x59, waiting for transfers between devices, move(): return lax.ppermute(value, BOTH, pairs)  113 us
    ppermute x59, starting transfers between devices, move(): return lax.ppermute(value, BOTH, pairs)  42.4 us
    unnamed x100, local copies, waits for them, and re-layouts  13 us
  transfers between devices with their start and end apart: 65, of which 23 were waited for; matrix products, arithmetic and copies ran while one was open for 8% of the time, Pallas kernels for 49%

profile of v2, /device:TPU:9, one launch (start us, length us, event | category | flops | bytes accessed | tf_op | source)
XLA Modules:
  0.0 442.7 jit_solution(3248367335414011715)
XLA Ops:
  21.1 16.5 %collective-permute-done.2 = bf16[32,4224]{1,0:T(8,128)(2,1)S(1)} collective-permute-done((bf16[32,4224]{1,0:T(8,128)(2,1)S(1)}, bf16[32,4224]{1,0:T(8,128)(2,1)S(1)}, u32[]{:S(2)}, u32[]{:S(2)}) %collective-permute-start.2) | collective-permute-done | bytes 270368 | tf_op jit(solution)/shard_map/ppermute | solution.py:83
  37.5 3.5 collective-permute-done.1
  48.4 2.4 collective-permute-start.12
  50.8 13.9 %collective-permute-done.5.refs_2_ = bf16[4,32,4224]{2,1,0:T(8,128)(2,1)S(1)} collective-permute-done((bf16[4,32,4224]{2,1,0:T(8,128)(2,1)S(1)}, bf16[4,32,4224]{2,1,0:T(8,128)(2,1)S(1)}, u32[]{:S(2)}, u32[]{:S(2)}) %collective-permute-start.5) | collective-permute-done | bytes 1081376 | tf_op jit(solution)/shard_map/ppermute | solution.py:83
  64.7 2.9 collective-permute-done.4.refs_1_
  69.8 13.8 %collective-permute-done.13 = f32[8,1024]{1,0:T(8,128)S(1)} collective-permute-done((f32[8,1024]{1,0:T(8,128)S(1)}, f32[8,1024]{1,0:T(8,128)S(1)}, u32[]{:S(2)}, u32[]{:S(2)}) %collective-permute-start.13) | collective-permute-done | bytes 32800 | tf_op jit(solution)/shard_map/ppermute | solution.py:83
  90.4 20.0 %attention.1 = (bf16[32,32,1024]{2,1,0:T(8,128)(2,1)}, bf16[1024,3072]{1,0:T(8,128)(2,1)}, bf16[1024,1024]{1,0:T(8,128)(2,1)}, bf16[32,32,1024]{2,1,0:T(8,128)(2,1)}) custom-call(s32[32]{0:T(128)} %get-tuple-element.329.places, s32[32]{0:T(128)} %get-tuple-element.328.slots.near_slots, bf16[1024,1024]{1,0:T(8,128)(2,1)} %tokens.5, f32[1,1024]{1,0:T(1,128)} %bitcast.146, ...), custom_call_target="tpu_custom_call" | custom-call | tf_op jit(solution)/shard_map/attention/pallas_call | solution.py:152
  112.3 9.3 %middle.1 = (f32[1024,1024]{1,0:T(8,128)}, bf16[1024,1024]{1,0:T(8,128)(2,1)}, bf16[32,32,1024]{2,1,0:T(8,128)(2,1)}) custom-call(s32[32]{0:T(128)} %get-tuple-element.329.places, s32[32]{0:T(128)} %get-tuple-element.328.slots.near_slots, s32[32]{0:T(128)} %fusion.51.slots, bf16[1024,1024]{1,0:T(8,128)(2,1)} %tokens.5, ...), custom_call_target="tpu_custom_call" | custom-call | tf_op jit(solution)/shard_map/middle/pallas_call | solution.py:152
  121.7 3.7 collective-permute-done.17.refs_3_.refs_11_
  130.7 34.4 %up.1 = (bf16[1024,4096]{1,0:T(8,128)(2,1)}, bf16[1024,4096]{1,0:T(8,128)(2,1)}, bf16[4,4,128,1024]{3,2,1,0:T(8,128)(2,1)}, bf16[2,4,128,1024]{3,2,1,0:T(8,128)(2,1)}, bf16[2,4,128,1024]{3,2,1,0:T(8,128)(2,1)}) custom-call(s32[32]{0:T(128)} %multiply_add_fusion.places, s32[32]{0:T(128)} %fusion.51.slots, bf16[1024,1024]{1,0:T(8,128)(2,1)} %get-tuple-element.170.act, ...), custom_call_target="tpu_custom_call" | custom-call | tf_op jit(solution)/shard_map/up/pallas_call | solution.py:152
  168.1 7.3 %collective-permute-done.27.refs_6_ = bf16[4,128,1024]{2,1,0:T(8,128)(2,1)S(1)} collective-permute-done((bf16[4,128,1024]{2,1,0:T(8,128)(2,1)}, bf16[4,128,1024]{2,1,0:T(8,128)(2,1)S(1)}, u32[]{:S(2)}, u32[]{:S(2)}) %collective-permute-start.27) | collective-permute-done | bytes 1048608 | tf_op jit(solution)/shard_map/ppermute | solution.py:83
  179.9 4.3 sum_pieces.10
  185.6 2.8 collective-permute-done.29.refs_7_
  189.4 44.6 %feed_back.1 = (bf16[4,4,32,4096]{3,2,1,0:T(8,128)(2,1)}, bf16[2,4,32,4096]{3,2,1,0:T(8,128)(2,1)}, bf16[2,4,32,4096]{3,2,1,0:T(8,128)(2,1)}, f32[1,4096]{1,0:T(...) custom-call(s32[32]{0:T(128)} %multiply_add_fusion.places, ...), custom_call_target="tpu_custom_call" | custom-call | tf_op jit(solution)/shard_map/feed_back/pallas_call | solution.py:152
  236.8 2.9 sum_pieces.11
  241.6 4.4 sum_pieces.12
  249.2 29.4 %attention_grad.1.grad_projected = bf16[1024,3072]{1,0:T(8,128)(2,1)} custom-call(s32[32]{0:T(128)} %get-tuple-element.329.places, bf16[1024,1024]{1,0:T(8,128)(2,1)} %get-tuple-element.227.grad_branch, bf16[1024,3072]{1,0:T(8,128)(2,1)} %get-tuple-element.209.qkv, f32[256,128]{1,0:T(8,128)} %bitcast.128, f32[256,128]{1,0:T(8,128)} %bitcast.130, ...), custom_call_target="tpu_custom_call" | custom-call | tf_op jit(solution)/shard_map/attention_grad/pallas_call | solution.py:152
  278.7 3.9 collective-permute-done.33.refs_2_
  283.4 3.2 sum_pieces.13
  286.6 2.9 sum_pieces.14
  289.5 9.4 %near_grad.2 = (bf16[4,4,32,2048]{3,2,1,0:T(8,128)(2,1)}, bf16[2,4,32,2048]{3,2,1,0:T(8,128)(2,1)}, bf16[2,4,32,2048]{3,2,1,0:T(8,128)(2,1)}) custom-call(bf16[32,32,1024]{2,1,0:T(8,128)(2,1)} %get-tuple-element.161.act_one, bf16[1024,3072]{1,0:T(8,128)(2,1)} %attention_grad.1.grad_projected, bf16[32,32,1024]{2,1,0:T(8,128)(2,1)} %get-tuple-element.219.attended, ...), custom_call_target="tpu_custom_call" | custom-call | tf_op jit(solution)/shard_map/near_grad/pallas_call | solution.py:152
  300.3 9.3 %near_grad.3 = (bf16[4,4,32,2048]{3,2,1,0:T(8,128)(2,1)}, bf16[2,4,32,2048]{3,2,1,0:T(8,128)(2,1)}, bf16[2,4,32,2048]{3,2,1,0:T(8,128)(2,1)}) custom-call(bf16[32,32,1024]{2,1,0:T(8,128)(2,1)} %get-tuple-element.161.act_one, bf16[1024,3072]{1,0:T(8,128)(2,1)} %attention_grad.1.grad_projected, bf16[32,32,1024]{2,1,0:T(8,128)(2,1)} %get-tuple-element.219.attended, ...), custom_call_target="tpu_custom_call" | custom-call | tf_op jit(solution)/shard_map/near_grad/pallas_call | solution.py:152
  310.9 3.6 sum_pieces.15
  314.5 3.7 sum_pieces.16
  318.2 5.8 %collective-permute-done.40 = bf16[4,32,4096]{2,1,0:T(8,128)(2,1)S(1)} collective-permute-done((bf16[4,32,4096]{2,1,0:T(8,128)(2,1)S(1)}, bf16[4,32,4096]{2,1,0:T(8,128)(2,1)S(1)}, u32[]{:S(2)}, u32[]{:S(2)}) %collective-permute-start.40) | collective-permute-done | bytes 1048608 | tf_op jit(solution)/shard_map/ppermute | solution.py:83
  324.9 3.2 sum_pieces.17
  333.4 15.6 %token_grad.1 = (f32[1024,1024]{1,0:T(8,128)}, f32[1,1024]{1,0:T(1,128)}, f32[1,1024]{1,0:T(1,128)}) custom-call(s32[32]{0:T(128)} %get-tuple-element.329.places, bf16[1024,3072]{1,0:T(8,128)(2,1)} %attention_grad.1.grad_projected, bf16[1024,1024]{1,0:T(8,128)(2,1)} %tokens.5, f32[1024,1024]{1,0:T(8,128)} %get-tuple-element.240.grad_middle, ...), custom_call_target="tpu_custom_call" | custom-call | tf_op jit(solution)/shard_map/token_grad/pallas_call | solution.py:152
  349.0 11.0 %collective-permute-done.41 = bf16[8,8,2048]{2,1,0:T(8,128)(2,1)S(1)} collective-permute-done((bf16[8,8,2048]{2,1,0:T(8,128)(2,1)S(1)}, bf16[8,8,2048]{2,1,0:T(8,128)(2,1)S(1)}, u32[]{:S(2)}, u32[]{:S(2)}) %collective-permute-start.41) | collective-permute-done | bytes 262176 | tf_op jit(solution)/shard_map/ppermute | solution.py:83
  370.6 15.9 %output.1 = bf16[1024,1024]{1,0:T(8,128)(2,1)} custom-call(s32[32]{0:T(128)} %multiply_add_fusion.places, bf16[1024,4096]{1,0:T(8,128)(2,1)} %get-tuple-element.253.hidden, f32[1024,1024]{1,0:T(8,128)} %get-tuple-element.188.middle, f32[1,1024]{1,0:T(1,128)} %bitcast.153, bf16[4,128,1024]{2,1,0:T(8,128)(2,1)} %bitcast.119, bf16[4,128,1024]{2,1,0:T(8,128)(2,1)} %copy-done.10, ...), custom_call_target="tpu_custom_call" | custom-call | tf_op jit(solution)/shard_map/output/pallas_call | solution.py:152
  405.0 2.8 convert_element_type.315
  407.8 9.3 %collective-permute-done.54 = bf16[32,4096]{1,0:T(8,128)(2,1)S(1)} collective-permute-done((bf16[32,4096]{1,0:T(8,128)(2,1)}, bf16[32,4096]{1,0:T(8,128)(2,1)S(1)}, u32[]{:S(2)}, u32[]{:S(2)}) %collective-permute-start.54) | collective-permute-done | bytes 262176 | tf_op jit(solution)/shard_map/ppermute | solution.py:83
  422.8 6.0 %collective-permute-done.57 = bf16[32,4096]{1,0:T(8,128)(2,1)S(1)} collective-permute-done((bf16[32,4096]{1,0:T(8,128)(2,1)S(1)}, bf16[32,4096]{1,0:T(8,128)(2,1)S(1)}, u32[]{:S(2)}, u32[]{:S(2)}) %collective-permute-start.57) | collective-permute-done | bytes 262176 | tf_op jit(solution)/shard_map/ppermute | solution.py:83
  (299 shorter events, 105.8 us)
Async XLA Ops:
  7.2 77.0 %all-gather.11.cloned.1.call-start = ((), (), s32[]{:S(2)}) async-start(), calls=%async_computation.6 | async-start | bytes 1310720 | tf_op jit(solution)/shard_map/all_gather | solution.py:90
  15.7 21.9 %collective-permute-start.2 = (bf16[32,4224]{1,0:T(8,128)(2,1)S(1)}, bf16[32,4224]{1,0:T(8,128)(2,1)S(1)}, u32[]{:S(2)}, u32[]{:S(2)}) collective-permute-start(bf16[32,4224]{1,0:T(8,128)(2,1)S(1)} %fusion.3), channel_id=1, source_target_pairs={{0,4},{1,5},{2,6},{3,7},{4,0},{5,1},{6,2},{7,3},{8,12},{9,13},{10,... | collective-permute-start | bytes 811016 | tf_op jit(solution)/shard_map/ppermute | solution.py:83
  16.7 24.3 %collective-permute-start.1 = (bf16[32,4224]{1,0:T(8,128)(2,1)S(1)}, bf16[32,4224]{1,0:T(8,128)(2,1)S(1)}, u32[]{:S(2)}, u32[]{:S(2)}) collective-permute-start(bf16[32,4224]{1,0:T(8,128)(2,1)S(1)} %fusion.3), channel_id=1, source_target_pairs={{0,6},{1,7},{2,0},{3,1},{4,2},{5,3},{6,4},{7,5},{8,14},{9,15},{10,... | collective-permute-start | bytes 811016 | tf_op jit(solution)/shard_map/ppermute | solution.py:83
  41.2 23.5 %collective-permute-start.5 = (bf16[4,32,4224]{2,1,0:T(8,128)(2,1)S(1)}, bf16[4,32,4224]{2,1,0:T(8,128)(2,1)S(1)}, u32[]{:S(2)}, u32[]{:S(2)}) collective-permute-start(bf16[4,32,4224]{2,1,0:T(8,128)(2,1)S(1)} %pad_maximum_fusion.refs_0_), channel_id=1, source_target_pairs={{0,16},{1,17},{2,18},{3,19},{4,20},{5,21},{6,22},{7,23},{8,9},{9,8... | collective-permute-start | bytes 3244040 | tf_op jit(solution)/shard_map/ppermute | solution.py:83
  42.0 25.7 %collective-permute-start.4 = (bf16[4,32,4224]{2,1,0:T(8,128)(2,1)S(1)}, bf16[4,32,4224]{2,1,0:T(8,128)(2,1)}, u32[]{:S(2)}, u32[]{:S(2)}) collective-permute-start(bf16[4,32,4224]{2,1,0:T(8,128)(2,1)S(1)} %pad_maximum_fusion.refs_0_), channel_id=1, source_target_pairs={{0,1},{1,0},{2,3},{3,2},{4,5},{5,4},{6,7},{7,6},{8,24},{9,25},{10,... | collective-permute-start | bytes 3244040 | tf_op jit(solution)/shard_map/ppermute | solution.py:83
  43.2 78.4 %all-gather.13.cloned.1.call-start = ((), (), s32[]{:S(2)}) async-start(), calls=%async_computation.7 | async-start | bytes 1310720 | tf_op jit(solution)/shard_map/all_gather | solution.py:90
  48.4 35.8 %collective-permute-start.12 = (bf16[4,32,4224]{2,1,0:T(8,128)(2,1)S(1)}, bf16[4,32,4224]{2,1,0:T(8,128)(2,1)}, u32[]{:S(2)}, u32[]{:S(2)}) collective-permute-start(bf16[4,32,4224]{2,1,0:T(8,128)(2,1)S(1)} %pad_maximum_fusion.refs_0_), channel_id=1, source_target_pairs={{0,8},{1,9},{2,10},{3,11},{4,12},{5,13},{6,14},{7,15},{8,0},{9,1},... | collective-permute-start | bytes 3244040 | tf_op jit(solution)/shard_map/ppermute | solution.py:83
  84.3 26.1 %collective-permute-start.16 = (bf16[4,32,4096]{2,1,0:T(8,128)(2,1)}, bf16[4,32,4096]{2,1,0:T(8,128)(2,1)S(1)}, u32[]{:S(2)}, u32[]{:S(2)}) collective-permute-start(bf16[4,32,4096]{2,1,0:T(8,128)(2,1)} %bitcast.120), channel_id=1, source_target_pairs={{0,16},{1,17},{2,18},{3,19},{4,20},{5,21},{6,22},{7,23},{8,9},{9,8... | collective-permute-start | bytes 3145736 | tf_op jit(solution)/shard_map/ppermute | solution.py:83
  85.2 25.4 %collective-permute-start.15 = (bf16[4,32,4096]{2,1,0:T(8,128)(2,1)}, bf16[4,32,4096]{2,1,0:T(8,128)(2,1)}, u32[]{:S(2)}, u32[]{:S(2)}) collective-permute-start(bf16[4,32,4096]{2,1,0:T(8,128)(2,1)} %bitcast.121), channel_id=1, source_target_pairs={{0,1},{1,0},{2,3},{3,2},{4,5},{5,4},{6,7},{7,6},{8,24},{9,25},{10,... | collective-permute-start | bytes 3145736 | tf_op jit(solution)/shard_map/ppermute | solution.py:83
  86.5 273.5 %reduce-scatter.3.cloned.1.call-start = ((), (), s32[]{:S(2)}) async-start(), calls=%async_computation.2 | async-start | bytes 1310720 | tf_op jit(solution)/shard_map/reduce_scatter | solution.py:105
  88.0 33.6 %collective-permute-start.19 = (bf16[4,32,4096]{2,1,0:T(8,128)(2,1)}, bf16[4,32,4096]{2,1,0:T(8,128)(2,1)}, u32[]{:S(2)}, u32[]{:S(2)}) collective-permute-start(bf16[4,32,4096]{2,1,0:T(8,128)(2,1)} %bitcast.122), channel_id=1, source_target_pairs={{0,8},{1,9},{2,10},{3,11},{4,12},{5,13},{6,14},{7,15},{8,0},{9,1},... | collective-permute-start | bytes 3145736 | tf_op jit(solution)/shard_map/ppermute | solution.py:83
  126.6 38.5 %collective-permute-start.24 = (bf16[4,128,1024]{2,1,0:T(8,128)(2,1)}, bf16[4,128,1024]{2,1,0:T(8,128)(2,1)S(1)}, u32[]{:S(2)}, u32[]{:S(2)}) collective-permute-start(bf16[4,128,1024]{2,1,0:T(8,128)(2,1)} %bitcast.115), channel_id=1, source_target_pairs={{0,8},{1,9},{2,10},{3,11},{4,12},{5,13},{6,14},{7,15},{8,0},{9,1},... | collective-permute-start | bytes 3145736 | tf_op jit(solution)/shard_map/ppermute | solution.py:83
  126.6 38.5 %collective-permute-start.23 = (bf16[4,128,1024]{2,1,0:T(8,128)(2,1)}, bf16[4,128,1024]{2,1,0:T(8,128)(2,1)S(1)}, u32[]{:S(2)}, u32[]{:S(2)}) collective-permute-start(bf16[4,128,1024]{2,1,0:T(8,128)(2,1)} %bitcast.116), channel_id=1, source_target_pairs={{0,16},{1,17},{2,18},{3,19},{4,20},{5,21},{6,22},{7,23},{8,9},{9,8... | collective-permute-start | bytes 3145736 | tf_op jit(solution)/shard_map/ppermute | solution.py:83
  127.3 37.9 %collective-permute-start.22 = (bf16[4,128,1024]{2,1,0:T(8,128)(2,1)}, bf16[4,128,1024]{2,1,0:T(8,128)(2,1)S(1)}, u32[]{:S(2)}, u32[]{:S(2)}) collective-permute-start(bf16[4,128,1024]{2,1,0:T(8,128)(2,1)} %bitcast.117), channel_id=1, source_target_pairs={{0,1},{1,0},{2,3},{3,2},{4,5},{5,4},{6,7},{7,6},{8,24},{9,25},{10,... | collective-permute-start | bytes 3145736 | tf_op jit(solution)/shard_map/ppermute | solution.py:83
  184.2 49.8 %collective-permute-start.30 = (bf16[2,4,128,1024]{3,2,1,0:T(8,128)(2,1)}, bf16[2,4,128,1024]{3,2,1,0:T(8,128)(2,1)}, u32[]{:S(2)}, u32[]{:S(2)}) collective-permute-start(bf16[2,4,128,1024]{3,2,1,0:T(8,128)(2,1)} %sum_pieces.10), channel_id=1, source_target_pairs={{0,1},{1,0},{2,3},{3,2},{4,5},{5,4},{6,7},{7,6},{8,24},{9,25},{10,... | collective-permute-start | bytes 6291464 | tf_op jit(solution)/shard_map/ppermute | solution.py:83
  246.0 36.6 %collective-permute-start.33 = (bf16[2,4,32,4096]{3,2,1,0:T(8,128)(2,1)}, bf16[2,4,32,4096]{3,2,1,0:T(8,128)(2,1)S(1)}, u32[]{:S(2)}, u32[]{:S(2)}) collective-permute-start(bf16[2,4,32,4096]{3,2,1,0:T(8,128)(2,1)} %sum_pieces.12), channel_id=1, source_target_pairs={{0,1},{1,0},{2,3},{3,2},{4,5},{5,4},{6,7},{7,6},{8,24},{9,25},{10,... | collective-permute-start | bytes 6291464 | tf_op jit(solution)/shard_map/ppermute | solution.py:83
  247.0 31.7 %collective-permute-start.32 = (bf16[4,128,1024]{2,1,0:T(8,128)(2,1)S(1)}, bf16[4,128,1024]{2,1,0:T(8,128)(2,1)S(1)}, u32[]{:S(2)}, u32[]{:S(2)}) collective-permute-start(bf16[4,128,1024]{2,1,0:T(8,128)(2,1)S(1)} %bitcast.132), channel_id=1, source_target_pairs={{0,16},{1,17},{2,18},{3,19},{4,20},{5,21},{6,22},{7,23},{8,9},{9,8... | collective-permute-start | bytes 3145736 | tf_op jit(solution)/shard_map/ppermute | solution.py:83
  247.8 30.9 %collective-permute-start.36 = (bf16[1,8,2048]{2,1,0:T(8,128)(2,1)S(1)}, bf16[1,8,2048]{2,1,0:T(8,128)(2,1)S(1)}, u32[]{:S(2)}, u32[]{:S(2)}) collective-permute-start(bf16[1,8,2048]{2,1,0:T(8,128)(2,1)S(1)} %constant_dynamic-update-slice_fusion.4), channel_id=1, source_target_pairs={{0,2},{1,3},{2,4},{3,5},{4,6},{5,7},{6,0},{7,1},{8,10},{9,11},{10,... | collective-permute-start | bytes 98312 | tf_op jit(solution)/shard_map/ppermute | solution.py:83
  247.8 30.9 %collective-permute-start.35 = (bf16[1,8,2048]{2,1,0:T(8,128)(2,1)S(1)}, bf16[1,8,2048]{2,1,0:T(8,128)(2,1)S(1)}, u32[]{:S(2)}, u32[]{:S(2)}) collective-permute-start(bf16[1,8,2048]{2,1,0:T(8,128)(2,1)S(1)} %constant_dynamic-update-slice_fusion.4), channel_id=1, source_target_pairs={{0,4},{1,5},{2,6},{3,7},{4,0},{5,1},{6,2},{7,3},{8,12},{9,13},{10,... | collective-permute-start | bytes 98312 | tf_op jit(solution)/shard_map/ppermute | solution.py:83
  247.8 30.9 %collective-permute-start.34 = (bf16[1,8,2048]{2,1,0:T(8,128)(2,1)S(1)}, bf16[1,8,2048]{2,1,0:T(8,128)(2,1)S(1)}, u32[]{:S(2)}, u32[]{:S(2)}) collective-permute-start(bf16[1,8,2048]{2,1,0:T(8,128)(2,1)S(1)} %constant_dynamic-update-slice_fusion.4), channel_id=1, source_target_pairs={{0,6},{1,7},{2,0},{3,1},{4,2},{5,3},{6,4},{7,5},{8,14},{9,15},{10,... | collective-permute-start | bytes 98312 | tf_op jit(solution)/shard_map/ppermute | solution.py:83
  309.8 76.9 %reduce-scatter.5.cloned.1.call-start = ((), (), s32[]{:S(2)}) async-start(), calls=%async_computation.3 | async-start | bytes 1310720 | tf_op jit(solution)/shard_map/reduce_scatter | solution.py:105
  328.2 76.9 %all-gather.7.cloned.1.call-start = ((), (), s32[]{:S(2)}) async-start(), calls=%async_computation.4 | async-start | bytes 1310720 | tf_op jit(solution)/shard_map/all_gather | solution.py:108
  328.8 31.1 %collective-permute-start.43 = (bf16[2,4,32,2048]{3,2,1,0:T(8,128)(2,1)}, bf16[2,4,32,2048]{3,2,1,0:T(8,128)(2,1)S(1)}, u32[]{:S(2)}, u32[]{:S(2)}) collective-permute-start(bf16[2,4,32,2048]{3,2,1,0:T(8,128)(2,1)} %sum_pieces.16), channel_id=1, source_target_pairs={{0,1},{1,0},{2,3},{3,2},{4,5},{5,4},{6,7},{7,6},{8,24},{9,25},{10,... | collective-permute-start | bytes 3145736 | tf_op jit(solution)/shard_map/ppermute | solution.py:83
  329.4 30.6 %collective-permute-start.42 = (bf16[2,4,32,2048]{3,2,1,0:T(8,128)(2,1)}, bf16[2,4,32,2048]{3,2,1,0:T(8,128)(2,1)S(1)}, u32[]{:S(2)}, u32[]{:S(2)}) collective-permute-start(bf16[2,4,32,2048]{3,2,1,0:T(8,128)(2,1)} %sum_pieces.15), channel_id=1, source_target_pairs={{0,1},{1,0},{2,3},{3,2},{4,5},{5,4},{6,7},{7,6},{8,24},{9,25},{10,... | collective-permute-start | bytes 3145736 | tf_op jit(solution)/shard_map/ppermute | solution.py:83
  332.8 27.1 %collective-permute-start.41 = (bf16[8,8,2048]{2,1,0:T(8,128)(2,1)S(1)}, bf16[8,8,2048]{2,1,0:T(8,128)(2,1)S(1)}, u32[]{:S(2)}, u32[]{:S(2)}) collective-permute-start(bf16[8,8,2048]{2,1,0:T(8,128)(2,1)S(1)} %get-tuple-element.300), channel_id=1, source_target_pairs={{0,16},{1,17},{2,18},{3,19},{4,20},{5,21},{6,22},{7,23},{8,24},{9,... | collective-permute-start | bytes 786440 | tf_op jit(solution)/shard_map/ppermute | solution.py:83
  365.3 21.3 %collective-permute-start.44 = (bf16[4,32,2048]{2,1,0:T(8,128)(2,1)}, bf16[4,32,2048]{2,1,0:T(8,128)(2,1)}, u32[]{:S(2)}, u32[]{:S(2)}) collective-permute-start(bf16[4,32,2048]{2,1,0:T(8,128)(2,1)} %bitcast.36), channel_id=1, source_target_pairs={{0,16},{1,17},{2,18},{3,19},{4,20},{5,21},{6,22},{7,23},{8,9},{9,8... | collective-permute-start | bytes 1572872 | tf_op jit(solution)/shard_map/ppermute | solution.py:83
  366.0 20.6 %collective-permute-start.45 = (bf16[4,32,2048]{2,1,0:T(8,128)(2,1)}, bf16[4,32,2048]{2,1,0:T(8,128)(2,1)}, u32[]{:S(2)}, u32[]{:S(2)}) collective-permute-start(bf16[4,32,2048]{2,1,0:T(8,128)(2,1)} %bitcast.136), channel_id=1, source_target_pairs={{0,16},{1,17},{2,18},{3,19},{4,20},{5,21},{6,22},{7,23},{8,9},{9,8... | collective-permute-start | bytes 1572872 | tf_op jit(solution)/shard_map/ppermute | solution.py:83
  367.5 19.1 %collective-permute-start.46 = (bf16[16,8,2048]{2,1,0:T(8,128)(2,1)}, bf16[16,8,2048]{2,1,0:T(8,128)(2,1)}, u32[]{:S(2)}, u32[]{:S(2)}) collective-permute-start(bf16[16,8,2048]{2,1,0:T(8,128)(2,1)} %get-tuple-element.294), channel_id=1, source_target_pairs={{0,8},{1,9},{2,10},{3,11},{4,12},{5,13},{6,14},{7,15},{8,0},{9,1},... | collective-permute-start | bytes 1572872 | tf_op jit(solution)/shard_map/ppermute | solution.py:83
  367.6 19.0 %collective-permute-start.48 = (f32[8,2,128]{2,0,1:T(8,128)S(1)}, f32[8,2,128]{2,0,1:T(8,128)S(1)}, u32[]{:S(2)}, u32[]{:S(2)}) collective-permute-start(f32[8,2,128]{2,0,1:T(8,128)S(1)} %pad_maximum_fusion.9), channel_id=1, source_target_pairs={{0,4},{1,5},{2,6},{3,7},{4,0},{5,1},{6,2},{7,3},{8,12},{9,13},{10,... | collective-permute-start | bytes 24584 | tf_op jit(solution)/shard_map/ppermute | solution.py:83
  370.5 49.4 %all-gather.9.cloned.1.call-start = ((), (), s32[]{:S(2)}) async-start(), calls=%async_computation.5 | async-start | bytes 1310720 | tf_op jit(solution)/shard_map/all_gather | solution.py:108
  395.2 21.9 %collective-permute-start.54 = (bf16[32,4096]{1,0:T(8,128)(2,1)}, bf16[32,4096]{1,0:T(8,128)(2,1)S(1)}, u32[]{:S(2)}, u32[]{:S(2)}) collective-permute-start(bf16[32,4096]{1,0:T(8,128)(2,1)} %pad_maximum_fusion.4), channel_id=1, source_target_pairs={{0,4},{1,5},{2,6},{3,7},{4,0},{5,1},{6,2},{7,3},{8,12},{9,13},{10,... | collective-permute-start | bytes 786440 | tf_op jit(solution)/shard_map/ppermute | solution.py:83
  397.9 21.3 %collective-permute-start.55 = (bf16[32,4096]{1,0:T(8,128)(2,1)}, bf16[32,4096]{1,0:T(8,128)(2,1)S(1)}, u32[]{:S(2)}, u32[]{:S(2)}) collective-permute-start(bf16[32,4096]{1,0:T(8,128)(2,1)} %pad_maximum_fusion.5), channel_id=1, source_target_pairs={{0,6},{1,7},{2,0},{3,1},{4,2},{5,3},{6,4},{7,5},{8,14},{9,15},{10,... | collective-permute-start | bytes 786440 | tf_op jit(solution)/shard_map/ppermute | solution.py:83
  (76 other events, 667.1 us)
Sparse Core Ops, SparseCore 0:
  43.3 26.8 all-gather.10
  86.6 25.6 all-gather.12
  309.9 22.8 reduce-scatter.2
  335.1 25.7 reduce-scatter.4
  370.7 17.1 all-gather.6
  396.4 16.2 all-gather.8

commit v3 on v2

--- a/solution.py
+++ b/solution.py
@@ -247,19 +247,24 @@
                 qkv[:, start + lanes : start + lanes + 128] = (piece * cos + turned(piece) * sin).astype(BF16)
         else:
             qkv[:, start : start + 512] = part.astype(BF16)
+    group = 1024
+    factor = HEAD_DIM ** (-0.5)
     for top in range(0, rows, length):
-        for lanes in range(0, width, 128):
-            q = qkv[top : top + length, lanes : lanes + 128]
-            k = heads(qkv[top : top + length, width + lanes : width + lanes + 128])
-            v = heads(qkv[top : top + length, 2 * width + lanes : 2 * width + lanes + 128])
-            scores = dot_nt(q, k) * HEAD_DIM ** (-0.5)
+        at = slice(top, top + length)
+        for first in range(0, width, group):
+            starts = range(first, first + group, 128)
+            queries = [heads(qkv[at, lanes : lanes + 128]) for lanes in starts]
+            scores = [
+                dot_nt(qkv[at, width + lanes : width + lanes + 128], q) for lanes, q in zip(starts, queries, strict=True)
+            ]
             probs = []
-            for head in range(2):
-                own = scores[:, head * length : (head + 1) * length]
-                e = jnp.exp(own - jnp.max(own, axis=-1, keepdims=True))
-                probs.append((e / jnp.sum(e, axis=-1, keepdims=True)).astype(BF16))
-            out = dot(jnp.concatenate(probs, axis=1), v)
-            attended[top : top + length, lanes : lanes + 128] = out.astype(BF16)
+            for score in scores:
+                e = jnp.exp(factor * (score - jnp.max(score, axis=0, keepdims=True)))
+                probs.append((e * (1.0 / jnp.sum(e, axis=0, keepdims=True))).astype(BF16))
+            probs = [jnp.concatenate([p[:, :length].T, p[:, length:].T], axis=1) for p in probs]
+            for lanes, p in zip(starts, probs, strict=True):
+                v = heads(qkv[at, 2 * width + lanes : 2 * width + lanes + 128])
+                attended[at, lanes : lanes + 128] = dot(p, v).astype(BF16)
     put_turned(attended_turned, slots, attended[...])
 
 
@@ -414,26 +419,34 @@
 
     grad_attended[...] = dot_nt(grad_branch[...], matrix(held)).astype(BF16)
     cos, sin = cosine[...], sine[...]
+    group = 512
     for top in range(0, rows, length):
         at = slice(top, top + length)
-        for lanes in range(0, width, 128):
-            q = heads(qkv[at, lanes : lanes + 128])
-            k = qkv[at, width + lanes : width + lanes + 128]
-            v = qkv[at, 2 * width + lanes : 2 * width + lanes + 128]
-            g = heads(grad_attended[at, lanes : lanes + 128])
-            scores = dot_nt(k, q) * factor
-            e = jnp.exp(scores - jnp.max(scores, axis=0, keepdims=True))
-            probs = e / jnp.sum(e, axis=0, keepdims=True)
-            grad_values = dot(probs.astype(BF16), g)
-            grad_probs = dot_nt(v, g)
-            inner = jnp.sum(grad_probs * probs, axis=0, keepdims=True)
-            grad_scores = (probs * (grad_probs - inner)).astype(BF16)
-            grad_keys = dot(grad_scores, q) * factor
-            flipped = jnp.concatenate([grad_scores[:, :length].T, grad_scores[:, length:].T], axis=1)
-            grad_queries = dot(flipped, heads(k)) * factor
-            for start, grad in ((lanes, grad_queries), (width + lanes, grad_keys)):
-                grad_projected[at, start : start + 128] = (grad * cos[at] - turned(grad) * sin[at]).astype(BF16)
-            grad_projected[at, 2 * width + lanes : 2 * width + lanes + 128] = grad_values.astype(BF16)
+        for first in range(0, width, group):
+            starts = range(first, first + group, 128)
+            q = [heads(qkv[at, lanes : lanes + 128]) for lanes in starts]
+            k = [qkv[at, width + lanes : width + lanes + 128] for lanes in starts]
+            g = [heads(grad_attended[at, lanes : lanes + 128]) for lanes in starts]
+            scores = [dot_nt(a, b) for a, b in zip(k, q, strict=True)]
+            grad_probs = [
+                dot_nt(qkv[at, 2 * width + lanes : 2 * width + lanes + 128], b) for lanes, b in zip(starts, g, strict=True)
+            ]
+            probs = []
+            for score in scores:
+                e = jnp.exp(factor * (score - jnp.max(score, axis=0, keepdims=True)))
+                probs.append(e * (1.0 / jnp.sum(e, axis=0, keepdims=True)))
+            grad_values = [dot(p.astype(BF16), b) for p, b in zip(probs, g, strict=True)]
+            grad_scores = []
+            for p, gp in zip(probs, grad_probs, strict=True):
+                inner = jnp.sum(gp * p, axis=0, keepdims=True)
+                grad_scores.append((p * (gp - inner)).astype(BF16))
+            grad_keys = [dot(gs, b) * factor for gs, b in zip(grad_scores, q, strict=True)]
+            flipped = [jnp.concatenate([gs[:, :length].T, gs[:, length:].T], axis=1) for gs in grad_scores]
+            grad_queries = [dot(f, heads(b)) * factor for f, b in zip(flipped, k, strict=True)]
+            for n, lanes in enumerate(starts):
+                for start, grad in ((lanes, grad_queries[n]), (width + lanes, grad_keys[n])):
+                    grad_projected[at, start : start + 128] = (grad * cos[at] - turned(grad) * sin[at]).astype(BF16)
+                grad_projected[at, 2 * width + lanes : 2 * width + lanes + 128] = grad_values[n].astype(BF16)
 
 
 def token_grad_kernel(places, grad_projected, tokens, grad_middle, gain, *refs):
@@ -712,100 +725,109 @@
         layer.feed_back(slope, act_two_turned, middle, scales, gain_two, shift_two, down_pieces, up_pieces)
     )
 
-    up_theirs, grad_branch, down_got, grad_scale, cotangent = tie(
-        up_theirs, grad_branch, down_got, grad_scale, cotangent
-    )
+    up_theirs, grad_branch, down_got = tie(up_theirs, grad_branch, down_got)
     up_sent = across(up_theirs)
     down_fold = sum_pieces(1, (down_keep, 1, 1), (down_sent, 2, 1), (down_got, 1, 1))[0]
+
+    up_sent, down_fold, grad_branch = tie(up_sent, down_fold, grad_branch)
+    up_fold = sum_pieces(2, (up_send, 0, 1), (up_sent, 1, 2))
+
+    up_fold, grad_branch = tie(up_fold, grad_branch)
+    up_got = first(up_fold)
+    grad_projected = layer.attention_grad(grad_branch, qkv, near_pieces)
+
+    grad_projected, grad_scale, cotangent, down_fold = tie(grad_projected, grad_scale, cotangent, down_fold)
+    down_more = second(down_fold)
+    low_theirs, low_send, low_keep = layer.near_grad(act_one, grad_projected, attended_turned, grad_branch, 0)
+
+    low_theirs, grad_projected, grad_branch, up_got, grad_scale = tie(
+        low_theirs, grad_projected, grad_branch, up_got, grad_scale
+    )
+    low_sent = across(low_theirs)
     sums = (grad_gain_two, grad_shift_two, jnp.sum(cotangent.astype(F32), axis=0), grad_up_bias)
     rows = [grad_scale, jnp.broadcast_to(noise_index[:, None], (seqs, 128)).astype(F32)]
     everyone = jnp.concatenate(rows + [v.reshape(seqs, -1) for v in sums], axis=1).astype(BF16)[None]
-
-    up_sent, down_fold, everyone, grad_branch = tie(up_sent, down_fold, everyone, grad_branch)
-    down_more = second(down_fold)
-    up_fold = sum_pieces(2, (up_send, 0, 1), (up_sent, 1, 2))
+    up_fold = sum_pieces(1, (up_keep, 1, 1), (up_sent, 2, 1), (up_got, 1, 1))[0]
+
+    up_fold, everyone, grad_projected, grad_branch, down_more = tie(
+        up_fold, everyone, grad_projected, grad_branch, down_more
+    )
+    up_more = second(up_fold)
     everyone = plan.near_z(everyone)
-
-    up_fold, grad_branch = tie(up_fold, grad_branch)
-    up_got = first(up_fold)
-    grad_projected = layer.attention_grad(grad_branch, qkv, near_pieces)
-
-    grad_projected, down_more, up_got, *everyone = tie(grad_projected, down_more, up_got, *everyone)
+    down_join = sum_pieces(1, (down_keep, 0, 1), (down_sent, 0, 1), (down_got, 0, 1), (down_more[None], 0, 1))[0]
+
+    down_join, grad_projected, grad_branch = tie(down_join, grad_projected, grad_branch)
+    grad_w_down = plan.over_z(down_join)
+    high_theirs, high_send, high_keep = layer.near_grad(act_one, grad_projected, attended_turned, grad_branch, 1)
+
+    high_theirs, grad_projected, low_sent, up_more, *everyone = tie(
+        high_theirs, grad_projected, low_sent, up_more, *everyone
+    )
+    high_sent = across(high_theirs)
     everyone = jnp.concatenate(everyone)
     more = plan.move(everyone, plan.x_pairs)
-    up_fold = sum_pieces(1, (up_keep, 1, 1), (up_sent, 2, 1), (up_got, 1, 1))[0]
-
-    up_fold, grad_projected = tie(up_fold, grad_projected)
-    up_more = second(up_fold)
-    down_join = sum_pieces(1, (down_keep, 0, 1), (down_sent, 0, 1), (down_got, 0, 1), (down_more[None], 0, 1))[0]
-
-    down_join, grad_projected = tie(down_join, grad_projected)
-    grad_w_down = plan.over_z(down_join)
-    grads = (act_one, grad_projected, attended_turned, grad_branch)
-    low_theirs, low_send, low_keep = layer.near_grad(*grads, 0)
-
-    low_theirs, grad_projected, grad_branch, more = tie(low_theirs, grad_projected, grad_branch, more)
-    low_sent = across(low_theirs)
+    low_fold = sum_pieces(2, (low_send, 0, 1), (low_sent, 1, 2))
+
+    low_fold, high_sent, more = tie(low_fold, high_sent, more)
+    low_got = first(low_fold)
     everyone = jnp.concatenate([everyone, more])
+    high_fold = sum_pieces(2, (high_send, 0, 1), (high_sent, 1, 2))
+
+    high_fold, everyone, grad_projected = tie(high_fold, everyone, grad_projected)
     more = plan.move(everyone, plan.y_pairs)
-    high_theirs, high_send, high_keep = layer.near_grad(act_one, grad_projected, attended_turned, grad_branch, 1)
-
-    high_theirs, grad_projected, low_sent = tie(high_theirs, grad_projected, low_sent)
-    high_sent = across(high_theirs)
-    low_fold = sum_pieces(2, (low_send, 0, 1), (low_sent, 1, 2))
-
-    low_fold, high_sent = tie(low_fold, high_sent)
-    low_got = first(low_fold)
-    high_fold = sum_pieces(2, (high_send, 0, 1), (high_sent, 1, 2))
-
-    high_fold, up_more, grad_projected = tie(high_fold, up_more, grad_projected)
     high_got = first(high_fold)
+    grad_tokens, grad_gain_one, grad_shift_one = layer.token_grad(grad_projected, grad_middle, gain_one, near_pieces)
+
+    grad_tokens, grad_gain_one, grad_shift_one = tie(grad_tokens, grad_gain_one, grad_shift_one)
+    ones = jnp.stack([grad_gain_one.reshape(8, per), grad_shift_one.reshape(8, per)], axis=1)
+    ones_sent = across(ones)
+
+    ones_sent, grad_w_down, ones = tie(ones_sent, grad_w_down, ones)
+    ones = ones + ones_sent
+    ones_sent = plan.move(ones, plan.x_pairs)
+    grad_w_down = plan.over_group(grad_w_down)
     up_join = sum_pieces(1, (up_keep, 0, 1), (up_sent, 0, 1), (up_got, 0, 1), (up_more[None], 0, 1))[0]
 
-    up_join, grad_projected = tie(up_join, grad_projected)
-    grad_w_up = plan.over_z(up_join)
-    grad_tokens, grad_gain_one, grad_shift_one = layer.token_grad(grad_projected, grad_middle, gain_one, near_pieces)
-
-    grad_tokens, grad_gain_one, grad_shift_one, more, low_got, high_got, grad_w_down, hidden = tie(
-        grad_tokens, grad_gain_one, grad_shift_one, more, low_got, high_got, grad_w_down, hidden
-    )
+    ones_sent, low_got, high_got, up_join = tie(ones_sent, low_got, high_got, up_join)
+    ones = ones + ones_sent
+    ones_sent = plan.move(ones, plan.y_pairs)
     low_fold = sum_pieces(1, (low_keep, 1, 1), (low_sent, 2, 1), (low_got, 1, 1))[0]
     high_fold = sum_pieces(1, (high_keep, 1, 1), (high_sent, 2, 1), (high_got, 1, 1))[0]
 
-    low_fold, high_fold, hidden = tie(low_fold, high_fold, hidden)
+    low_fold, high_fold, middle, more, up_join = tie(low_fold, high_fold, middle, more, up_join)
     low_more, high_more = second(low_fold), second(high_fold)
-    grad_w_down = plan.over_group(grad_w_down)
+    grad_w_up = plan.over_z(up_join)
     everyone = jnp.concatenate([everyone, more])
     more = across(everyone)
-    ones = jnp.stack([grad_gain_one.reshape(8, per), grad_shift_one.reshape(8, per)], axis=1)
-    ones_z = plan.near_z(ones)
     output = layer.output(hidden, middle, bias_down, down_pieces)
 
-    output, low_more, high_more, grad_w_up, more, *ones_z = tie(output, low_more, high_more, grad_w_up, more, *ones_z)
+    output, low_more, high_more, more, ones_sent, grad_w_down = tie(
+        output, low_more, high_more, more, ones_sent, grad_w_down
+    )
+    ones = ones + ones_sent
+    ones = lax.dynamic_index_in_dim(ones.reshape(4, 2, 2, per), plan.x, 1, keepdims=False)
+    ones = lax.dynamic_slice_in_dim(jnp.concatenate([ones, ones]), plan.z, 4, 0)
+    ones = jnp.pad(ones, ((0, 0), (0, layer.deep - 2), (0, 0)))
     parts = plan.to_z(
-        [low_keep[0], low_sent[0], low_got[0], low_more], [high_keep[0], high_sent[0], high_got[0], high_more]
+        [low_keep[0], low_sent[0], low_got[0], low_more], [high_keep[0], high_sent[0], high_got[0], high_more], [ones]
     )
-    grad_w_up = plan.over_group(grad_w_up)
-    ones = sum(ones_z)
-    ones = ones + across(ones)
-    ones = ones + plan.move(ones, plan.x_pairs)
-    ones = ones + plan.move(ones, plan.y_pairs)
-    ones = lax.dynamic_index_in_dim(ones, plan.wide, 0, keepdims=False)
+
+    grad_w_up, grad_w_down = tie(grad_w_up, grad_w_down)
+    grad_w_up, grad_w_down = plan.over_group(grad_w_up), grad_w_down.astype(F32)
+
+    grad_w_up, everyone, more, grad_w_down, *parts = tie(grad_w_up, everyone, more, grad_w_down, *parts)
+    near = plan.in_group(sum_of(*parts))
+    grad_w_up = grad_w_up.astype(F32)
     everyone = jnp.concatenate([everyone, more])
     rest = everyone[..., width:].astype(F32)
     picked = chosen(rest[..., 0].reshape(-1).astype(jnp.int32), own_levels)
     grad_w_time = outer(picked, everyone[..., :width].reshape(-1, width))
     rest = jnp.sum(lax.dynamic_index_in_dim(rest, plan.wide, 1, keepdims=False)[:, 128:], axis=0)
     gain_sum, shift_sum, down_sum, up_sum = jnp.split(rest, (per, 2 * per, 3 * per))
-    grad_w_down = grad_w_down.astype(F32)
-
-    ones, grad_w_time, grad_w_down, grad_w_up, *parts = tie(ones, grad_w_time, grad_w_down, grad_w_up, *parts)
-    near = plan.in_group(sum_of(*parts))
-    grad_w_up = grad_w_up.astype(F32)
-
-    near, grad_w_up = tie(near, grad_w_up)
-    near = near.astype(F32)
-    return (output, grad_tokens, ones[0], ones[1], near[:, : 3 * width], near[:, 3 * width :], gain_sum, shift_sum,
+
+    near, grad_w_up, grad_w_time = tie(near, grad_w_up, grad_w_time)
+    grad_w_qkv, grad_w_out, ones = jnp.split(near.astype(F32), (3 * width, 4 * width), axis=1)
+    return (output, grad_tokens, ones[0], ones[1], grad_w_qkv, grad_w_out, gain_sum, shift_sum,
             grad_w_time, grad_w_up, up_sum, grad_w_down, down_sum)
 
 

time: 447 us -> 431 us (0.964)
  Pallas kernels: 220 us -> 208 us
  waiting for transfers between devices: 113 us -> 108 us
    pallas_call x19, Pallas kernels: 220 us -> 208 us  [call(): pl.pallas_call(kernel, out_shape=[jax.ShapeDtypeStruct(shape, dtype) for...]
    ppermute x59 -> x56, waiting for transfers between devices: 113 us -> 104 us  [move(): return lax.ppermute(value, BOTH, pairs)]
    ppermute x59 -> x56, starting transfers between devices: 42.4 us -> 45.1 us  [move(): return lax.ppermute(value, BOTH, pairs)]
    unnamed x100 -> x80, local copies, waits for them, and re-layouts: 13 us -> 11.5 us
  transfers between devices with their start and end apart: 65 -> 62, of which waited for: 23 -> 24; matrix products, arithmetic and copies ran while one was open for 8% -> 7% of each run, Pallas kernels for 49% -> 48%
where the time goes in v3:
time: 431 us; the launch traced here: 427 us
  Pallas kernels  208 us (48%)
  waiting for transfers between devices  108 us (25%)
  starting transfers between devices  45.8 us (11%)
  local copies, waits for them, and re-layouts  28.4 us (7%)
  other arithmetic  17.6 us (4%)
  between operations  15.2 us (4%)
    pallas_call x19, Pallas kernels, call(): pl.pallas_call(kernel, out_shape=[jax.ShapeDtypeStruct(shape, dtype) for...  208 us
    ppermute x56, waiting for transfers between devices, move(): return lax.ppermute(value, BOTH, pairs)  104 us
    ppermute x56, starting transfers between devices, move(): return lax.ppermute(value, BOTH, pairs)  45.1 us
    unnamed x80, local copies, waits for them, and re-layouts  11.5 us
  transfers between devices with their start and end apart: 62, of which 24 were waited for; matrix products, arithmetic and copies ran while one was open for 7% of the time, Pallas kernels for 48%

profile of v3, /device:TPU:9, one launch (start us, length us, event | category | flops | bytes accessed | tf_op | source)
XLA Modules:
  0.0 426.9 jit_solution(14388017092577526625)
XLA Ops:
  21.1 16.5 %collective-permute-done.2 = bf16[32,4224]{1,0:T(8,128)(2,1)S(1)} collective-permute-done((bf16[32,4224]{1,0:T(8,128)(2,1)S(1)}, bf16[32,4224]{1,0:T(8,128)(2,1)S(1)}, u32[]{:S(2)}, u32[]{:S(2)}) %collective-permute-start.2) | collective-permute-done | bytes 270368 | tf_op jit(solution)/shard_map/ppermute | solution.py:83
  37.5 3.5 collective-permute-done.1
  50.8 13.9 %collective-permute-done.5.refs_2_ = bf16[4,32,4224]{2,1,0:T(8,128)(2,1)S(1)} collective-permute-done((bf16[4,32,4224]{2,1,0:T(8,128)(2,1)S(1)}, bf16[4,32,4224]{2,1,0:T(8,128)(2,1)S(1)}, u32[]{:S(2)}, u32[]{:S(2)}) %collective-permute-start.5) | collective-permute-done | bytes 1081376 | tf_op jit(solution)/shard_map/ppermute | solution.py:83
  64.7 2.9 collective-permute-done.4.refs_1_
  69.8 13.8 %collective-permute-done.13 = f32[8,1024]{1,0:T(8,128)S(1)} collective-permute-done((f32[8,1024]{1,0:T(8,128)S(1)}, f32[8,1024]{1,0:T(8,128)S(1)}, u32[]{:S(2)}, u32[]{:S(2)}) %collective-permute-start.13) | collective-permute-done | bytes 32800 | tf_op jit(solution)/shard_map/ppermute | solution.py:83
  90.4 19.8 %attention.1 = (bf16[32,32,1024]{2,1,0:T(8,128)(2,1)}, bf16[1024,3072]{1,0:T(8,128)(2,1)}, bf16[1024,1024]{1,0:T(8,128)(2,1)}, bf16[32,32,1024]{2,1,0:T(8,128)(2,1)}) custom-call(s32[32]{0:T(128)} %get-tuple-element.324.places, s32[32]{0:T(128)} %get-tuple-element.323.slots.near_slots, bf16[1024,1024]{1,0:T(8,128)(2,1)} %tokens.5, f32[1,1024]{1,0:T(1,128)} %bitcast.156, ...), custom_call_target="tpu_custom_call" | custom-call | tf_op jit(solution)/shard_map/attention/pallas_call | solution.py:152
  112.3 9.3 %middle.1 = (f32[1024,1024]{1,0:T(8,128)}, bf16[1024,1024]{1,0:T(8,128)(2,1)}, bf16[32,32,1024]{2,1,0:T(8,128)(2,1)}) custom-call(s32[32]{0:T(128)} %get-tuple-element.324.places, s32[32]{0:T(128)} %get-tuple-element.323.slots.near_slots, s32[32]{0:T(128)} %fusion.51.slots, bf16[1024,1024]{1,0:T(8,128)(2,1)} %tokens.5, ...), custom_call_target="tpu_custom_call" | custom-call | tf_op jit(solution)/shard_map/middle/pallas_call | solution.py:152
  121.6 3.7 collective-permute-done.17.refs_3_.refs_11_
  130.7 34.3 %up.1 = (bf16[1024,4096]{1,0:T(8,128)(2,1)}, bf16[1024,4096]{1,0:T(8,128)(2,1)}, bf16[4,4,128,1024]{3,2,1,0:T(8,128)(2,1)}, bf16[2,4,128,1024]{3,2,1,0:T(8,128)(2,1)}, bf16[2,4,128,1024]{3,2,1,0:T(8,128)(2,1)}) custom-call(s32[32]{0:T(128)} %multiply_add_fusion.places, s32[32]{0:T(128)} %fusion.51.slots, bf16[1024,1024]{1,0:T(8,128)(2,1)} %get-tuple-element.173.act, ...), custom_call_target="tpu_custom_call" | custom-call | tf_op jit(solution)/shard_map/up/pallas_call | solution.py:152
  168.0 7.3 %collective-permute-done.27.refs_6_ = bf16[4,128,1024]{2,1,0:T(8,128)(2,1)S(1)} collective-permute-done((bf16[4,128,1024]{2,1,0:T(8,128)(2,1)}, bf16[4,128,1024]{2,1,0:T(8,128)(2,1)S(1)}, u32[]{:S(2)}, u32[]{:S(2)}) %collective-permute-start.27) | collective-permute-done | bytes 1048608 | tf_op jit(solution)/shard_map/ppermute | solution.py:83
  179.8 4.3 %sum_pieces.10 = bf16[2,4,128,1024]{3,2,1,0:T(8,128)(2,1)} custom-call(bf16[2,4,128,1024]{3,2,1,0:T(8,128)(2,1)} %get-tuple-element.184.refs_0_, bf16[4,4,128,1024]{3,2,1,0:T(8,128)(2,1)} %copy-done.3), custom_call_target="tpu_custom_call" | custom-call | tf_op jit(solution)/shard_map/sum_pieces/pallas_call | solution.py:152
  185.4 2.8 collective-permute-done.29.refs_7_
  189.2 44.5 %feed_back.1 = (bf16[4,4,32,4096]{3,2,1,0:T(8,128)(2,1)}, bf16[2,4,32,4096]{3,2,1,0:T(8,128)(2,1)}, bf16[2,4,32,4096]{3,2,1,0:T(8,128)(2,1)}, f32[1,4096]{1,0:T(...) custom-call(s32[32]{0:T(128)} %multiply_add_fusion.places, ...), custom_call_target="tpu_custom_call" | custom-call | tf_op jit(solution)/shard_map/feed_back/pallas_call | solution.py:152
  235.2 2.9 sum_pieces.11
  238.0 4.4 %collective-permute-done.31.refs_1_ = bf16[4,4,32,4096]{3,2,1,0:T(8,128)(2,1)S(1)} collective-permute-done((bf16[4,4,32,4096]{3,2,1,0:T(8,128)(2,1)}, bf16[4,4,32,4096]{3,2,1,0:T(8,128)(2,1)S(1)}, u32[]{:S(2)}, u32[]{:S(2)}) %collective-permute-start.31) | collective-permute-done | bytes 4194336 | tf_op jit(solution)/shard_map/ppermute | solution.py:83
  244.4 4.3 %sum_pieces.12 = bf16[2,4,32,4096]{3,2,1,0:T(8,128)(2,1)} custom-call(bf16[2,4,32,4096]{3,2,1,0:T(8,128)(2,1)} %get-tuple-element.197.refs_0_, bf16[4,4,32,4096]{3,2,1,0:T(8,128)(2,1)} %copy-done.2), custom_call_target="tpu_custom_call" | custom-call | tf_op jit(solution)/shard_map/sum_pieces/pallas_call | solution.py:152
  249.8 17.7 %attention_grad.1.grad_projected = bf16[1024,3072]{1,0:T(8,128)(2,1)} custom-call(s32[32]{0:T(128)} %get-tuple-element.324.places, bf16[1024,1024]{1,0:T(8,128)(2,1)} %get-tuple-element.231.grad_branch, bf16[1024,3072]{1,0:T(8,128)(2,1)} %get-tuple-element.208.qkv, f32[256,128]{1,0:T(8,128)} %bitcast.139, f32[256,128]{1,0:T(8,128)} %bitcast.141, ...), custom_call_target="tpu_custom_call" | custom-call | tf_op jit(solution)/shard_map/attention_grad/pallas_call | solution.py:152
  268.8 9.4 %near_grad.2 = (bf16[4,4,32,2048]{3,2,1,0:T(8,128)(2,1)}, bf16[2,4,32,2048]{3,2,1,0:T(8,128)(2,1)}, bf16[2,4,32,2048]{3,2,1,0:T(8,128)(2,1)}) custom-call(bf16[32,32,1024]{2,1,0:T(8,128)(2,1)} %get-tuple-element.183.act_one, bf16[1024,3072]{1,0:T(8,128)(2,1)} %attention_grad.1.grad_projected, bf16[32,32,1024]{2,1,0:T(8,128)(2,1)} %get-tuple-element.212.attended, ...), custom_call_target="tpu_custom_call" | custom-call | tf_op jit(solution)/shard_map/near_grad/pallas_call | solution.py:152
  279.5 2.9 sum_pieces.13
  282.5 3.3 collective-permute-done.33
  287.9 3.2 sum_pieces.14
  291.1 9.3 %near_grad.3 = (bf16[4,4,32,2048]{3,2,1,0:T(8,128)(2,1)}, bf16[2,4,32,2048]{3,2,1,0:T(8,128)(2,1)}, bf16[2,4,32,2048]{3,2,1,0:T(8,128)(2,1)}) custom-call(bf16[32,32,1024]{2,1,0:T(8,128)(2,1)} %get-tuple-element.183.act_one, bf16[1024,3072]{1,0:T(8,128)(2,1)} %attention_grad.1.grad_projected, bf16[32,32,1024]{2,1,0:T(8,128)(2,1)} %get-tuple-element.212.attended, ...), custom_call_target="tpu_custom_call" | custom-call | tf_op jit(solution)/shard_map/near_grad/pallas_call | solution.py:152
  302.7 3.6 sum_pieces.15
  307.1 3.7 sum_pieces.16
  312.4 15.4 %token_grad.1 = (f32[1024,1024]{1,0:T(8,128)}, f32[1,1024]{1,0:T(1,128)}, f32[1,1024]{1,0:T(1,128)}) custom-call(s32[32]{0:T(128)} %get-tuple-element.324.places, bf16[1024,3072]{1,0:T(8,128)(2,1)} %attention_grad.1.grad_projected, bf16[1024,1024]{1,0:T(8,128)(2,1)} %tokens.5, f32[1024,1024]{1,0:T(8,128)} %get-tuple-element.248.grad_middle, ...), custom_call_target="tpu_custom_call" | custom-call | tf_op jit(solution)/shard_map/token_grad/pallas_call | solution.py:152
  331.3 3.2 sum_pieces.17
  349.0 16.2 %output.1 = bf16[1024,1024]{1,0:T(8,128)(2,1)} custom-call(s32[32]{0:T(128)} %multiply_add_fusion.places, bf16[1024,4096]{1,0:T(8,128)(2,1)} %get-tuple-element.182.hidden, f32[1024,1024]{1,0:T(8,128)} %get-tuple-element.262.middle, f32[1,1024]{1,0:T(1,128)} %bitcast.164, bf16[4,128,1024]{2,1,0:T(8,128)(2,1)} %bitcast.130, bf16[4,128,1024]{2,1,0:T(8,128)(2,1)} %copy-done.11, ...), custom_call_target="tpu_custom_call" | custom-call | tf_op jit(solution)/shard_map/output/pallas_call | solution.py:152
  366.0 2.4 fusion.4
  372.1 4.2 reduce-scatter.5.cloned.1.call-done
  383.1 13.6 %collective-permute-done.51 = bf16[32,4224]{1,0:T(8,128)(2,1)S(1)} collective-permute-done((bf16[32,4224]{1,0:T(8,128)(2,1)S(1)}, bf16[32,4224]{1,0:T(8,128)(2,1)S(1)}, u32[]{:S(2)}, u32[]{:S(2)}) %collective-permute-start.51) | collective-permute-done | bytes 270368 | tf_op jit(solution)/shard_map/ppermute | solution.py:83
  396.7 5.0 %collective-permute-done.52 = bf16[32,4224]{1,0:T(8,128)(2,1)} collective-permute-done((bf16[32,4224]{1,0:T(8,128)(2,1)S(1)}, bf16[32,4224]{1,0:T(8,128)(2,1)}, u32[]{:S(2)}, u32[]{:S(2)}) %collective-permute-start.52) | collective-permute-done | bytes 270368 | tf_op jit(solution)/shard_map/ppermute | solution.py:83
  407.1 3.3 collective-permute-done.54
  (280 shorter events, 106.9 us)
Async XLA Ops:
  7.2 77.0 %all-gather.11.cloned.1.call-start = ((), (), s32[]{:S(2)}) async-start(), calls=%async_computation.6 | async-start | bytes 1310720 | tf_op jit(solution)/shard_map/all_gather | solution.py:90
  15.7 21.9 %collective-permute-start.2 = (bf16[32,4224]{1,0:T(8,128)(2,1)S(1)}, bf16[32,4224]{1,0:T(8,128)(2,1)S(1)}, u32[]{:S(2)}, u32[]{:S(2)}) collective-permute-start(bf16[32,4224]{1,0:T(8,128)(2,1)S(1)} %fusion.3), channel_id=1, source_target_pairs={{0,4},{1,5},{2,6},{3,7},{4,0},{5,1},{6,2},{7,3},{8,12},{9,13},{10,... | collective-permute-start | bytes 811016 | tf_op jit(solution)/shard_map/ppermute | solution.py:83
  16.7 24.3 %collective-permute-start.1 = (bf16[32,4224]{1,0:T(8,128)(2,1)S(1)}, bf16[32,4224]{1,0:T(8,128)(2,1)S(1)}, u32[]{:S(2)}, u32[]{:S(2)}) collective-permute-start(bf16[32,4224]{1,0:T(8,128)(2,1)S(1)} %fusion.3), channel_id=1, source_target_pairs={{0,6},{1,7},{2,0},{3,1},{4,2},{5,3},{6,4},{7,5},{8,14},{9,15},{10,... | collective-permute-start | bytes 811016 | tf_op jit(solution)/shard_map/ppermute | solution.py:83
  41.2 23.5 %collective-permute-start.5 = (bf16[4,32,4224]{2,1,0:T(8,128)(2,1)S(1)}, bf16[4,32,4224]{2,1,0:T(8,128)(2,1)S(1)}, u32[]{:S(2)}, u32[]{:S(2)}) collective-permute-start(bf16[4,32,4224]{2,1,0:T(8,128)(2,1)S(1)} %pad_maximum_fusion.refs_0_), channel_id=1, source_target_pairs={{0,16},{1,17},{2,18},{3,19},{4,20},{5,21},{6,22},{7,23},{8,9},{9,8... | collective-permute-start | bytes 3244040 | tf_op jit(solution)/shard_map/ppermute | solution.py:83
  42.0 25.7 %collective-permute-start.4 = (bf16[4,32,4224]{2,1,0:T(8,128)(2,1)S(1)}, bf16[4,32,4224]{2,1,0:T(8,128)(2,1)}, u32[]{:S(2)}, u32[]{:S(2)}) collective-permute-start(bf16[4,32,4224]{2,1,0:T(8,128)(2,1)S(1)} %pad_maximum_fusion.refs_0_), channel_id=1, source_target_pairs={{0,1},{1,0},{2,3},{3,2},{4,5},{5,4},{6,7},{7,6},{8,24},{9,25},{10,... | collective-permute-start | bytes 3244040 | tf_op jit(solution)/shard_map/ppermute | solution.py:83
  43.2 78.4 %all-gather.13.cloned.1.call-start = ((), (), s32[]{:S(2)}) async-start(), calls=%async_computation.7 | async-start | bytes 1310720 | tf_op jit(solution)/shard_map/all_gather | solution.py:90
  48.4 35.8 %collective-permute-start.12 = (bf16[4,32,4224]{2,1,0:T(8,128)(2,1)S(1)}, bf16[4,32,4224]{2,1,0:T(8,128)(2,1)}, u32[]{:S(2)}, u32[]{:S(2)}) collective-permute-start(bf16[4,32,4224]{2,1,0:T(8,128)(2,1)S(1)} %pad_maximum_fusion.refs_0_), channel_id=1, source_target_pairs={{0,8},{1,9},{2,10},{3,11},{4,12},{5,13},{6,14},{7,15},{8,0},{9,1},... | collective-permute-start | bytes 3244040 | tf_op jit(solution)/shard_map/ppermute | solution.py:83
  67.6 16.6 %collective-permute-start.11 = (bf16[4,32,4224]{2,1,0:T(8,128)(2,1)S(1)}, bf16[4,32,4224]{2,1,0:T(8,128)(2,1)}, u32[]{:S(2)}, u32[]{:S(2)}) collective-permute-start(bf16[4,32,4224]{2,1,0:T(8,128)(2,1)S(1)} %collective-permute-done.5.refs_2_), channel_id=1, source_target_pairs={{0,8},{1,9},{2,10},{3,11},{4,12},{5,13},{6,14},{7,15},{8,0},{9,1},... | collective-permute-start | bytes 3244040 | tf_op jit(solution)/shard_map/ppermute | solution.py:83
  68.2 16.0 %collective-permute-start.10 = (bf16[4,32,4224]{2,1,0:T(8,128)(2,1)}, bf16[4,32,4224]{2,1,0:T(8,128)(2,1)}, u32[]{:S(2)}, u32[]{:S(2)}) collective-permute-start(bf16[4,32,4224]{2,1,0:T(8,128)(2,1)} %collective-permute-done.4.refs_1_), channel_id=1, source_target_pairs={{0,8},{1,9},{2,10},{3,11},{4,12},{5,13},{6,14},{7,15},{8,0},{9,1},... | collective-permute-start | bytes 3244040 | tf_op jit(solution)/shard_map/ppermute | solution.py:83
  84.3 25.9 %collective-permute-start.16 = (bf16[4,32,4096]{2,1,0:T(8,128)(2,1)}, bf16[4,32,4096]{2,1,0:T(8,128)(2,1)S(1)}, u32[]{:S(2)}, u32[]{:S(2)}) collective-permute-start(bf16[4,32,4096]{2,1,0:T(8,128)(2,1)} %bitcast.131), channel_id=1, source_target_pairs={{0,16},{1,17},{2,18},{3,19},{4,20},{5,21},{6,22},{7,23},{8,9},{9,8... | collective-permute-start | bytes 3145736 | tf_op jit(solution)/shard_map/ppermute | solution.py:83
  85.2 25.4 %collective-permute-start.15 = (bf16[4,32,4096]{2,1,0:T(8,128)(2,1)}, bf16[4,32,4096]{2,1,0:T(8,128)(2,1)}, u32[]{:S(2)}, u32[]{:S(2)}) collective-permute-start(bf16[4,32,4096]{2,1,0:T(8,128)(2,1)} %bitcast.132), channel_id=1, source_target_pairs={{0,1},{1,0},{2,3},{3,2},{4,5},{5,4},{6,7},{7,6},{8,24},{9,25},{10,... | collective-permute-start | bytes 3145736 | tf_op jit(solution)/shard_map/ppermute | solution.py:83
  86.5 243.4 %reduce-scatter.3.cloned.1.call-start = ((), (), s32[]{:S(2)}) async-start(), calls=%async_computation.2 | async-start | bytes 1310720 | tf_op jit(solution)/shard_map/reduce_scatter | solution.py:105
  88.0 33.6 %collective-permute-start.19 = (bf16[4,32,4096]{2,1,0:T(8,128)(2,1)}, bf16[4,32,4096]{2,1,0:T(8,128)(2,1)}, u32[]{:S(2)}, u32[]{:S(2)}) collective-permute-start(bf16[4,32,4096]{2,1,0:T(8,128)(2,1)} %bitcast.133), channel_id=1, source_target_pairs={{0,8},{1,9},{2,10},{3,11},{4,12},{5,13},{6,14},{7,15},{8,0},{9,1},... | collective-permute-start | bytes 3145736 | tf_op jit(solution)/shard_map/ppermute | solution.py:83
  126.6 38.4 %collective-permute-start.24 = (bf16[4,128,1024]{2,1,0:T(8,128)(2,1)}, bf16[4,128,1024]{2,1,0:T(8,128)(2,1)S(1)}, u32[]{:S(2)}, u32[]{:S(2)}) collective-permute-start(bf16[4,128,1024]{2,1,0:T(8,128)(2,1)} %bitcast.126), channel_id=1, source_target_pairs={{0,8},{1,9},{2,10},{3,11},{4,12},{5,13},{6,14},{7,15},{8,0},{9,1},... | collective-permute-start | bytes 3145736 | tf_op jit(solution)/shard_map/ppermute | solution.py:83
  126.6 38.4 %collective-permute-start.23 = (bf16[4,128,1024]{2,1,0:T(8,128)(2,1)}, bf16[4,128,1024]{2,1,0:T(8,128)(2,1)S(1)}, u32[]{:S(2)}, u32[]{:S(2)}) collective-permute-start(bf16[4,128,1024]{2,1,0:T(8,128)(2,1)} %bitcast.127), channel_id=1, source_target_pairs={{0,16},{1,17},{2,18},{3,19},{4,20},{5,21},{6,22},{7,23},{8,9},{9,8... | collective-permute-start | bytes 3145736 | tf_op jit(solution)/shard_map/ppermute | solution.py:83
  127.3 37.8 %collective-permute-start.22 = (bf16[4,128,1024]{2,1,0:T(8,128)(2,1)}, bf16[4,128,1024]{2,1,0:T(8,128)(2,1)S(1)}, u32[]{:S(2)}, u32[]{:S(2)}) collective-permute-start(bf16[4,128,1024]{2,1,0:T(8,128)(2,1)} %bitcast.128), channel_id=1, source_target_pairs={{0,1},{1,0},{2,3},{3,2},{4,5},{5,4},{6,7},{7,6},{8,24},{9,25},{10,... | collective-permute-start | bytes 3145736 | tf_op jit(solution)/shard_map/ppermute | solution.py:83
  167.4 16.7 %collective-permute-start.28 = (bf16[4,128,1024]{2,1,0:T(8,128)(2,1)}, bf16[4,128,1024]{2,1,0:T(8,128)(2,1)}, u32[]{:S(2)}, u32[]{:S(2)}) collective-permute-start(bf16[4,128,1024]{2,1,0:T(8,128)(2,1)} %copy-done.11), channel_id=1, source_target_pairs={{0,16},{1,17},{2,18},{3,19},{4,20},{5,21},{6,22},{7,23},{8,9},{9,8... | collective-permute-start | bytes 3145736 | tf_op jit(solution)/shard_map/ppermute | solution.py:83
  184.1 49.6 %collective-permute-start.30 = (bf16[2,4,128,1024]{3,2,1,0:T(8,128)(2,1)}, bf16[2,4,128,1024]{3,2,1,0:T(8,128)(2,1)S(1)}, u32[]{:S(2)}, u32[]{:S(2)}) collective-permute-start(bf16[2,4,128,1024]{3,2,1,0:T(8,128)(2,1)} %sum_pieces.10), channel_id=1, source_target_pairs={{0,1},{1,0},{2,3},{3,2},{4,5},{5,4},{6,7},{7,6},{8,24},{9,25},{10,... | collective-permute-start | bytes 6291464 | tf_op jit(solution)/shard_map/ppermute | solution.py:83
  248.7 29.5 %collective-permute-start.32 = (bf16[2,4,32,4096]{3,2,1,0:T(8,128)(2,1)}, bf16[2,4,32,4096]{3,2,1,0:T(8,128)(2,1)}, u32[]{:S(2)}, u32[]{:S(2)}) collective-permute-start(bf16[2,4,32,4096]{3,2,1,0:T(8,128)(2,1)} %sum_pieces.12), channel_id=1, source_target_pairs={{0,1},{1,0},{2,3},{3,2},{4,5},{5,4},{6,7},{7,6},{8,24},{9,25},{10,... | collective-permute-start | bytes 6291464 | tf_op jit(solution)/shard_map/ppermute | solution.py:83
  267.5 18.2 %collective-permute-start.33 = (bf16[4,128,1024]{2,1,0:T(8,128)(2,1)S(1)}, bf16[4,128,1024]{2,1,0:T(8,128)(2,1)}, u32[]{:S(2)}, u32[]{:S(2)}) collective-permute-start(bf16[4,128,1024]{2,1,0:T(8,128)(2,1)S(1)} %bitcast.144), channel_id=1, source_target_pairs={{0,16},{1,17},{2,18},{3,19},{4,20},{5,21},{6,22},{7,23},{8,9},{9,8... | collective-permute-start | bytes 3145736 | tf_op jit(solution)/shard_map/ppermute | solution.py:83
  278.2 22.4 %collective-permute-start.34 = (bf16[4,4,32,2048]{3,2,1,0:T(8,128)(2,1)}, bf16[4,4,32,2048]{3,2,1,0:T(8,128)(2,1)S(1)}, u32[]{:S(2)}, u32[]{:S(2)}) collective-permute-start(bf16[4,4,32,2048]{3,2,1,0:T(8,128)(2,1)} %get-tuple-element.233), channel_id=1, source_target_pairs={{0,8},{1,9},{2,10},{3,11},{4,12},{5,13},{6,14},{7,15},{8,0},{9,1},... | collective-permute-start | bytes 6291464 | tf_op jit(solution)/shard_map/ppermute | solution.py:83
  301.8 63.5 %all-gather.7.cloned.1.call-start = ((), (), s32[]{:S(2)}) async-start(), calls=%async_computation.3 | async-start | bytes 1310720 | tf_op jit(solution)/shard_map/all_gather | solution.py:108
  310.8 26.8 %collective-permute-start.44 = (bf16[2,4,32,2048]{3,2,1,0:T(8,128)(2,1)}, bf16[2,4,32,2048]{3,2,1,0:T(8,128)(2,1)S(1)}, u32[]{:S(2)}, u32[]{:S(2)}) collective-permute-start(bf16[2,4,32,2048]{3,2,1,0:T(8,128)(2,1)} %sum_pieces.16), channel_id=1, source_target_pairs={{0,1},{1,0},{2,3},{3,2},{4,5},{5,4},{6,7},{7,6},{8,24},{9,25},{10,... | collective-permute-start | bytes 3145736 | tf_op jit(solution)/shard_map/ppermute | solution.py:83
  311.4 26.9 %collective-permute-start.43 = (bf16[2,4,32,2048]{3,2,1,0:T(8,128)(2,1)S(1)}, bf16[2,4,32,2048]{3,2,1,0:T(8,128)(2,1)S(1)}, u32[]{:S(2)}, u32[]{:S(2)}) collective-permute-start(bf16[2,4,32,2048]{3,2,1,0:T(8,128)(2,1)S(1)} %copy-done.27), channel_id=1, source_target_pairs={{0,1},{1,0},{2,3},{3,2},{4,5},{5,4},{6,7},{7,6},{8,24},{9,25},{10,... | collective-permute-start | bytes 3145736 | tf_op jit(solution)/shard_map/ppermute | solution.py:83
  330.7 45.6 %reduce-scatter.5.cloned.1.call-start = ((), (), s32[]{:S(2)}) async-start(), calls=%async_computation.4 | async-start | bytes 1310720 | tf_op jit(solution)/shard_map/reduce_scatter | solution.py:105
  344.4 20.8 %collective-permute-start.46 = (bf16[4,32,2048]{2,1,0:T(8,128)(2,1)}, bf16[4,32,2048]{2,1,0:T(8,128)(2,1)}, u32[]{:S(2)}, u32[]{:S(2)}) collective-permute-start(bf16[4,32,2048]{2,1,0:T(8,128)(2,1)} %bitcast.38), channel_id=1, source_target_pairs={{0,16},{1,17},{2,18},{3,19},{4,20},{5,21},{6,22},{7,23},{8,9},{9,8... | collective-permute-start | bytes 1572872 | tf_op jit(solution)/shard_map/ppermute | solution.py:83
  344.4 20.8 %collective-permute-start.47 = (bf16[4,32,2048]{2,1,0:T(8,128)(2,1)}, bf16[4,32,2048]{2,1,0:T(8,128)(2,1)}, u32[]{:S(2)}, u32[]{:S(2)}) collective-permute-start(bf16[4,32,2048]{2,1,0:T(8,128)(2,1)} %bitcast.146), channel_id=1, source_target_pairs={{0,16},{1,17},{2,18},{3,19},{4,20},{5,21},{6,22},{7,23},{8,9},{9,8... | collective-permute-start | bytes 1572872 | tf_op jit(solution)/shard_map/ppermute | solution.py:83
  347.6 17.7 %collective-permute-start.48 = (bf16[16,8,2048]{2,1,0:T(8,128)(2,1)}, bf16[16,8,2048]{2,1,0:T(8,128)(2,1)}, u32[]{:S(2)}, u32[]{:S(2)}) collective-permute-start(bf16[16,8,2048]{2,1,0:T(8,128)(2,1)} %constant_dynamic-update-slice_fusion.15), channel_id=1, source_target_pairs={{0,8},{1,9},{2,10},{3,11},{4,12},{5,13},{6,14},{7,15},{8,0},{9,1},... | collective-permute-start | bytes 1572872 | tf_op jit(solution)/shard_map/ppermute | solution.py:83
  347.9 53.8 %all-gather.9.cloned.1.call-start = ((), (), s32[]{:S(2)}) async-start(), calls=%async_computation.5 | async-start | bytes 1310720 | tf_op jit(solution)/shard_map/all_gather | solution.py:108
  348.0 17.2 %collective-permute-start.49 = (f32[8,2,128]{2,0,1:T(8,128)S(1)}, f32[8,2,128]{2,0,1:T(8,128)S(1)}, u32[]{:S(2)}, u32[]{:S(2)}) collective-permute-start(f32[8,2,128]{2,0,1:T(8,128)S(1)} %add.296), channel_id=1, source_target_pairs={{0,16},{1,17},{2,18},{3,19},{4,20},{5,21},{6,22},{7,23},{8,24},{9,... | collective-permute-start | bytes 24584 | tf_op jit(solution)/shard_map/ppermute | solution.py:83
  377.4 19.3 %collective-permute-start.51 = (bf16[32,4224]{1,0:T(8,128)(2,1)S(1)}, bf16[32,4224]{1,0:T(8,128)(2,1)S(1)}, u32[]{:S(2)}, u32[]{:S(2)}) collective-permute-start(bf16[32,4224]{1,0:T(8,128)(2,1)S(1)} %pad_maximum_fusion.4), channel_id=1, source_target_pairs={{0,4},{1,5},{2,6},{3,7},{4,0},{5,1},{6,2},{7,3},{8,12},{9,13},{10,... | collective-permute-start | bytes 811016 | tf_op jit(solution)/shard_map/ppermute | solution.py:83
  380.3 21.4 %collective-permute-start.52 = (bf16[32,4224]{1,0:T(8,128)(2,1)S(1)}, bf16[32,4224]{1,0:T(8,128)(2,1)}, u32[]{:S(2)}, u32[]{:S(2)}) collective-permute-start(bf16[32,4224]{1,0:T(8,128)(2,1)S(1)} %pad_maximum_fusion.5), channel_id=1, source_target_pairs={{0,6},{1,7},{2,0},{3,1},{4,2},{5,3},{6,4},{7,5},{8,14},{9,15},{10,... | collective-permute-start | bytes 811016 | tf_op jit(solution)/shard_map/ppermute | solution.py:83
  (63 other events, 574.0 us)
Sparse Core Ops, SparseCore 0:
  43.3 26.8 all-gather.10
  86.6 25.6 all-gather.12
  301.9 24.8 reduce-scatter.2
  330.9 18.7 all-gather.6
  351.9 24.3 reduce-scatter.4
  377.7 18.5 all-gather.8

commit v4 on v3

--- a/solution.py
+++ b/solution.py
@@ -388,14 +388,15 @@
 
 def sum_pieces(count, *terms):
     _, _, rows, columns = terms[0][0].shape
-    block = (1, 2, rows, columns)
+    halves = 1 if count > 1 else 2
+    block = (1, 4 // halves, rows, columns)
     ins = [
-        (array, block, lambda i, first=first, stride=stride: (first + stride * (i // 2), i % 2, 0, 0))
+        (array, block, lambda i, first=first, stride=stride: (first + stride * (i // halves), i % halves, 0, 0))
         for array, first, stride in terms
     ]
-    out = ((count, 4, rows, columns), BF16, block, lambda i: (i // 2, i % 2, 0, 0))
+    out = ((count, 4, rows, columns), BF16, block, lambda i: (i // halves, i % halves, 0, 0))
     size = count * 4 * rows * columns
-    return call(sum_kernel, "sum_pieces", (), (2 * count,), ins, [out], flops=size, moved=2 * size * (len(terms) + 1))[0]
+    return call(sum_kernel, "sum_pieces", (), (halves * count,), ins, [out], flops=size, moved=2 * size * (len(terms) + 1))[0]
 
 
 def output_kernel(places, hidden, middle, bias, *refs):
@@ -513,11 +514,11 @@
     def rows_out(self, columns, dtype):
         return out_rows((self.rows, columns), dtype, self.tile)
 
-    def by_columns(self, array):
-        return (array, array.shape[:-1] + (self.strip,), lambda i, *_: (0,) * (array.ndim - 1) + (i,))
-
-    def columns_out(self, shape, dtype):
-        return (shape, dtype, shape[:-1] + (self.strip,), lambda i, *_: (0,) * (len(shape) - 1) + (i,))
+    def by_columns(self, array, strip):
+        return (array, array.shape[:-1] + (strip,), lambda i, *_: (0,) * (array.ndim - 1) + (i,))
+
+    def columns_out(self, shape, dtype, strip):
+        return (shape, dtype, shape[:-1] + (strip,), lambda i, *_: (0,) * (len(shape) - 1) + (i,))
 
     def attention(self, gain, shift, pieces):
         rows, width = self.rows, self.width
@@ -541,17 +542,17 @@
 
     def up(self, act, bias, pieces):
         rows, width, ff = self.rows, self.width, self.ff
-        fr = ff // BLOCKS
+        fr, strip = ff // BLOCKS, 2 * self.strip
         return call(
-            up_kernel, "up", (self.places, self.slots), (ff // self.strip,),
-            [whole(act), self.by_columns(bias), whole(self.cotangent)] + [self.by_columns(p) for p in pieces],
-            [self.columns_out((rows, ff), BF16)] * 2 + [out_whole((n, 4, fr, width), BF16) for n in (4, 2, 2)],
-            [pltpu.VMEM((BLOCKS, self.deep, self.strip), BF16)],
+            up_kernel, "up", (self.places, self.slots), (ff // strip,),
+            [whole(act), self.by_columns(bias, strip), whole(self.cotangent)] + [self.by_columns(p, strip) for p in pieces],
+            [self.columns_out((rows, ff), BF16, strip)] * 2 + [out_whole((n, 4, fr, width), BF16) for n in (4, 2, 2)],
+            [pltpu.VMEM((BLOCKS, self.deep, strip), BF16)],
             flops=4 * rows * width * ff, moved=8 * rows * ff,
         )
 
     def near_grad(self, act_one, grad_projected, attended, grad_branch, half):
-        columns, strip = 2 * self.width, self.strip
+        columns, strip = 2 * self.width, 2 * self.strip
         strips = 3 * self.width // strip
         at = half * columns // strip
         ins = [
@@ -562,7 +563,7 @@
         ]
         return call(
             functools.partial(near_grad_kernel, strips - at), "near_grad", (), (columns // strip,), ins,
-            [self.columns_out((n, 4, self.deep, columns), BF16) for n in (4, 2, 2)],
+            [self.columns_out((n, 4, self.deep, columns), BF16, strip) for n in (4, 2, 2)],
             flops=2 * self.rows * self.width * columns, moved=4 * self.rows * columns,
         )
 
@@ -570,10 +571,10 @@
         rows, width, ff = self.rows, self.width, self.ff
         return call(
             functools.partial(feed_back_kernel, self.length), "feed_back", (self.places,), (ff // self.strip,),
-            [whole(self.cotangent), self.by_columns(slope)] + [whole(v) for v in (act, middle, scales, gain, shift)]
-            + [whole(p) for p in down] + [self.by_columns(p) for p in up],
-            [self.columns_out((n, 4, self.deep, ff), BF16) for n in (4, 2, 2)]
-            + [self.columns_out((1, ff), F32), out_whole((rows, width), F32), out_whole((rows, width), BF16)]
+            [whole(self.cotangent), self.by_columns(slope, self.strip)] + [whole(v) for v in (act, middle, scales, gain, shift)]
+            + [whole(p) for p in down] + [self.by_columns(p, self.strip) for p in up],
+            [self.columns_out((n, 4, self.deep, ff), BF16, self.strip) for n in (4, 2, 2)]
+            + [self.columns_out((1, ff), F32, self.strip), out_whole((rows, width), F32), out_whole((rows, width), BF16)]
             + [out_whole((self.seqs, width), F32)] + [out_whole((1, width), F32)] * 2,
             [self.held(down), pltpu.VMEM((BLOCKS, self.deep, self.strip), BF16), pltpu.VMEM((rows, width), F32)],
             flops=6 * rows * width * ff, moved=10 * rows * ff,

time: 431 us -> 425 us (0.986)
  Pallas kernels: 208 us -> 203 us
    pallas_call x19, Pallas kernels: 208 us -> 203 us  [call(): pl.pallas_call(kernel, out_shape=[jax.ShapeDtypeStruct(shape, dtype) for...]
  transfers between devices with their start and end apart: 62 -> 62, of which waited for: 24 -> 24; matrix products, arithmetic and copies ran while one was open for 7% -> 7% of each run, Pallas kernels for 48% -> 47%
where the time goes in v4:
time: 425 us; the launch traced here: 421 us
  Pallas kernels  203 us (48%)
  waiting for transfers between devices  110 us (26%)
  starting transfers between devices  44.7 us (11%)
  local copies, waits for them, and re-layouts  28.4 us (7%)
  other arithmetic  17.6 us (4%)
  between operations  15.1 us (4%)
    pallas_call x19, Pallas kernels, call(): pl.pallas_call(kernel, out_shape=[jax.ShapeDtypeStruct(shape, dtype) for...  203 us
    ppermute x56, waiting for transfers between devices, move(): return lax.ppermute(value, BOTH, pairs)  105 us
    ppermute x56, starting transfers between devices, move(): return lax.ppermute(value, BOTH, pairs)  44.3 us
    unnamed x80, local copies, waits for them, and re-layouts  11.5 us
  transfers between devices with their start and end apart: 62, of which 24 were waited for; matrix products, arithmetic and copies ran while one was open for 7% of the time, Pallas kernels for 47%

profile of v4, /device:TPU:9, one launch (start us, length us, event | category | flops | bytes accessed | tf_op | source)
XLA Modules:
  0.0 421.4 jit_solution(12940897028705877587)
XLA Ops:
  21.1 16.5 %collective-permute-done.2 = bf16[32,4224]{1,0:T(8,128)(2,1)S(1)} collective-permute-done((bf16[32,4224]{1,0:T(8,128)(2,1)S(1)}, bf16[32,4224]{1,0:T(8,128)(2,1)S(1)}, u32[]{:S(2)}, u32[]{:S(2)}) %collective-permute-start.2) | collective-permute-done | bytes 270368 | tf_op jit(solution)/shard_map/ppermute | solution.py:83
  37.5 3.5 collective-permute-done.1
  50.8 13.9 %collective-permute-done.5.refs_2_ = bf16[4,32,4224]{2,1,0:T(8,128)(2,1)S(1)} collective-permute-done((bf16[4,32,4224]{2,1,0:T(8,128)(2,1)S(1)}, bf16[4,32,4224]{2,1,0:T(8,128)(2,1)S(1)}, u32[]{:S(2)}, u32[]{:S(2)}) %collective-permute-start.5) | collective-permute-done | bytes 1081376 | tf_op jit(solution)/shard_map/ppermute | solution.py:83
  64.7 2.9 collective-permute-done.4.refs_1_
  69.8 13.8 %collective-permute-done.13 = f32[8,1024]{1,0:T(8,128)S(1)} collective-permute-done((f32[8,1024]{1,0:T(8,128)S(1)}, f32[8,1024]{1,0:T(8,128)S(1)}, u32[]{:S(2)}, u32[]{:S(2)}) %collective-permute-start.13) | collective-permute-done | bytes 32800 | tf_op jit(solution)/shard_map/ppermute | solution.py:83
  89.9 20.0 %attention.1 = (bf16[32,32,1024]{2,1,0:T(8,128)(2,1)}, bf16[1024,3072]{1,0:T(8,128)(2,1)}, bf16[1024,1024]{1,0:T(8,128)(2,1)}, bf16[32,32,1024]{2,1,0:T(8,128)(2,1)}) custom-call(s32[32]{0:T(128)} %get-tuple-element.324.places, s32[32]{0:T(128)} %get-tuple-element.323.slots.near_slots, bf16[1024,1024]{1,0:T(8,128)(2,1)} %tokens.5, f32[1,1024]{1,0:T(1,128)} %bitcast.156, ...), custom_call_target="tpu_custom_call" | custom-call | tf_op jit(solution)/shard_map/attention/pallas_call | solution.py:152
  112.3 9.3 %middle.1 = (f32[1024,1024]{1,0:T(8,128)}, bf16[1024,1024]{1,0:T(8,128)(2,1)}, bf16[32,32,1024]{2,1,0:T(8,128)(2,1)}) custom-call(s32[32]{0:T(128)} %get-tuple-element.324.places, s32[32]{0:T(128)} %get-tuple-element.323.slots.near_slots, s32[32]{0:T(128)} %fusion.51.slots, bf16[1024,1024]{1,0:T(8,128)(2,1)} %tokens.5, ...), custom_call_target="tpu_custom_call" | custom-call | tf_op jit(solution)/shard_map/middle/pallas_call | solution.py:152
  121.6 3.8 collective-permute-done.17.refs_3_.refs_11_
  130.7 32.0 %up.1 = (bf16[1024,4096]{1,0:T(8,128)(2,1)}, bf16[1024,4096]{1,0:T(8,128)(2,1)}, bf16[4,4,128,1024]{3,2,1,0:T(8,128)(2,1)}, bf16[2,4,128,1024]{3,2,1,0:T(8,128)(2,1)}, bf16[2,4,128,1024]{3,2,1,0:T(8,128)(2,1)}) custom-call(s32[32]{0:T(128)} %multiply_add_fusion.places, s32[32]{0:T(128)} %fusion.51.slots, bf16[1024,1024]{1,0:T(8,128)(2,1)} %get-tuple-element.173.act, ...), custom_call_target="tpu_custom_call" | custom-call | tf_op jit(solution)/shard_map/up/pallas_call | solution.py:152
  165.6 7.3 %collective-permute-done.27.refs_6_ = bf16[4,128,1024]{2,1,0:T(8,128)(2,1)S(1)} collective-permute-done((bf16[4,128,1024]{2,1,0:T(8,128)(2,1)}, bf16[4,128,1024]{2,1,0:T(8,128)(2,1)S(1)}, u32[]{:S(2)}, u32[]{:S(2)}) %collective-permute-start.27) | collective-permute-done | bytes 1048608 | tf_op jit(solution)/shard_map/ppermute | solution.py:83
  177.4 3.4 sum_pieces.10
  182.0 2.8 collective-permute-done.29.refs_7_
  185.8 44.6 %feed_back.1 = (bf16[4,4,32,4096]{3,2,1,0:T(8,128)(2,1)}, bf16[2,4,32,4096]{3,2,1,0:T(8,128)(2,1)}, bf16[2,4,32,4096]{3,2,1,0:T(8,128)(2,1)}, f32[1,4096]{1,0:T(...) custom-call(s32[32]{0:T(128)} %multiply_add_fusion.places, ...), custom_call_target="tpu_custom_call" | custom-call | tf_op jit(solution)/shard_map/feed_back/pallas_call | solution.py:152
  231.8 2.9 sum_pieces.11
  234.7 4.4 %collective-permute-done.31.refs_1_ = bf16[4,4,32,4096]{3,2,1,0:T(8,128)(2,1)S(1)} collective-permute-done((bf16[4,4,32,4096]{3,2,1,0:T(8,128)(2,1)}, bf16[4,4,32,4096]{3,2,1,0:T(8,128)(2,1)S(1)}, u32[]{:S(2)}, u32[]{:S(2)}) %collective-permute-start.31) | collective-permute-done | bytes 4194336 | tf_op jit(solution)/shard_map/ppermute | solution.py:83
  241.1 3.4 sum_pieces.12
  245.6 17.9 %attention_grad.1.grad_projected = bf16[1024,3072]{1,0:T(8,128)(2,1)} custom-call(s32[32]{0:T(128)} %get-tuple-element.324.places, bf16[1024,1024]{1,0:T(8,128)(2,1)} %get-tuple-element.231.grad_branch, bf16[1024,3072]{1,0:T(8,128)(2,1)} %get-tuple-element.208.qkv, f32[256,128]{1,0:T(8,128)} %bitcast.139, f32[256,128]{1,0:T(8,128)} %bitcast.141, ...), custom_call_target="tpu_custom_call" | custom-call | tf_op jit(solution)/shard_map/attention_grad/pallas_call | solution.py:152
  264.7 9.6 %near_grad.2 = (bf16[4,4,32,2048]{3,2,1,0:T(8,128)(2,1)}, bf16[2,4,32,2048]{3,2,1,0:T(8,128)(2,1)}, bf16[2,4,32,2048]{3,2,1,0:T(8,128)(2,1)}) custom-call(bf16[32,32,1024]{2,1,0:T(8,128)(2,1)} %get-tuple-element.183.act_one, bf16[1024,3072]{1,0:T(8,128)(2,1)} %attention_grad.1.grad_projected, bf16[32,32,1024]{2,1,0:T(8,128)(2,1)} %get-tuple-element.212.attended, ...), custom_call_target="tpu_custom_call" | custom-call | tf_op jit(solution)/shard_map/near_grad/pallas_call | solution.py:152
  275.3 2.9 sum_pieces.13
  278.3 3.2 collective-permute-done.33
  283.7 3.2 sum_pieces.14
  286.9 9.6 %near_grad.3 = (bf16[4,4,32,2048]{3,2,1,0:T(8,128)(2,1)}, bf16[2,4,32,2048]{3,2,1,0:T(8,128)(2,1)}, bf16[2,4,32,2048]{3,2,1,0:T(8,128)(2,1)}) custom-call(bf16[32,32,1024]{2,1,0:T(8,128)(2,1)} %get-tuple-element.183.act_one, bf16[1024,3072]{1,0:T(8,128)(2,1)} %attention_grad.1.grad_projected, bf16[32,32,1024]{2,1,0:T(8,128)(2,1)} %get-tuple-element.212.attended, ...), custom_call_target="tpu_custom_call" | custom-call | tf_op jit(solution)/shard_map/near_grad/pallas_call | solution.py:152
  298.7 2.4 sum_pieces.15
  303.0 2.7 sum_pieces.16
  307.3 15.4 %token_grad.1 = (f32[1024,1024]{1,0:T(8,128)}, f32[1,1024]{1,0:T(1,128)}, f32[1,1024]{1,0:T(1,128)}) custom-call(s32[32]{0:T(128)} %get-tuple-element.324.places, bf16[1024,3072]{1,0:T(8,128)(2,1)} %attention_grad.1.grad_projected, bf16[1024,1024]{1,0:T(8,128)(2,1)} %tokens.5, f32[1024,1024]{1,0:T(8,128)} %get-tuple-element.248.grad_middle, ...), custom_call_target="tpu_custom_call" | custom-call | tf_op jit(solution)/shard_map/token_grad/pallas_call | solution.py:152
  326.2 3.2 sum_pieces.17
  344.0 15.9 %output.1 = bf16[1024,1024]{1,0:T(8,128)(2,1)} custom-call(s32[32]{0:T(128)} %multiply_add_fusion.places, bf16[1024,4096]{1,0:T(8,128)(2,1)} %get-tuple-element.182.hidden, f32[1024,1024]{1,0:T(8,128)} %get-tuple-element.262.middle, f32[1,1024]{1,0:T(1,128)} %bitcast.164, bf16[4,128,1024]{2,1,0:T(8,128)(2,1)} %bitcast.130, bf16[4,128,1024]{2,1,0:T(8,128)(2,1)} %copy-done.11, ...), custom_call_target="tpu_custom_call" | custom-call | tf_op jit(solution)/shard_map/output/pallas_call | solution.py:152
  360.7 2.4 fusion.4
  366.8 4.4 %reduce-scatter.5.cloned.1.call-done = bf16[1,32,4096]{2,1,0:T(8,128)(2,1)} async-done(((bf16[4,32,4096]{2,1,0:T(8,128)(2,1)}), bf16[1,32,4096]{2,1,0:T(8,128)(2,1)}) %reduce-scatter.5.cloned.1.call-update) | async-done | bytes 262160 | tf_op jit(solution)/shard_map/reduce_scatter | solution.py:105
  378.1 13.6 %collective-permute-done.51 = bf16[32,4224]{1,0:T(8,128)(2,1)S(1)} collective-permute-done((bf16[32,4224]{1,0:T(8,128)(2,1)S(1)}, bf16[32,4224]{1,0:T(8,128)(2,1)S(1)}, u32[]{:S(2)}, u32[]{:S(2)}) %collective-permute-start.51) | collective-permute-done | bytes 270368 | tf_op jit(solution)/shard_map/ppermute | solution.py:83
  391.7 4.6 %collective-permute-done.52 = bf16[32,4224]{1,0:T(8,128)(2,1)} collective-permute-done((bf16[32,4224]{1,0:T(8,128)(2,1)S(1)}, bf16[32,4224]{1,0:T(8,128)(2,1)}, u32[]{:S(2)}, u32[]{:S(2)}) %collective-permute-start.52) | collective-permute-done | bytes 270368 | tf_op jit(solution)/shard_map/ppermute | solution.py:83
  401.6 3.4 collective-permute-done.54
  (280 shorter events, 107.4 us)
Async XLA Ops:
  7.2 77.0 %all-gather.11.cloned.1.call-start = ((), (), s32[]{:S(2)}) async-start(), calls=%async_computation.6 | async-start | bytes 1310720 | tf_op jit(solution)/shard_map/all_gather | solution.py:90
  15.7 21.9 %collective-permute-start.2 = (bf16[32,4224]{1,0:T(8,128)(2,1)S(1)}, bf16[32,4224]{1,0:T(8,128)(2,1)S(1)}, u32[]{:S(2)}, u32[]{:S(2)}) collective-permute-start(bf16[32,4224]{1,0:T(8,128)(2,1)S(1)} %fusion.3), channel_id=1, source_target_pairs={{0,4},{1,5},{2,6},{3,7},{4,0},{5,1},{6,2},{7,3},{8,12},{9,13},{10,... | collective-permute-start | bytes 811016 | tf_op jit(solution)/shard_map/ppermute | solution.py:83
  16.7 24.3 %collective-permute-start.1 = (bf16[32,4224]{1,0:T(8,128)(2,1)S(1)}, bf16[32,4224]{1,0:T(8,128)(2,1)S(1)}, u32[]{:S(2)}, u32[]{:S(2)}) collective-permute-start(bf16[32,4224]{1,0:T(8,128)(2,1)S(1)} %fusion.3), channel_id=1, source_target_pairs={{0,6},{1,7},{2,0},{3,1},{4,2},{5,3},{6,4},{7,5},{8,14},{9,15},{10,... | collective-permute-start | bytes 811016 | tf_op jit(solution)/shard_map/ppermute | solution.py:83
  41.2 23.5 %collective-permute-start.5 = (bf16[4,32,4224]{2,1,0:T(8,128)(2,1)S(1)}, bf16[4,32,4224]{2,1,0:T(8,128)(2,1)S(1)}, u32[]{:S(2)}, u32[]{:S(2)}) collective-permute-start(bf16[4,32,4224]{2,1,0:T(8,128)(2,1)S(1)} %pad_maximum_fusion.refs_0_), channel_id=1, source_target_pairs={{0,16},{1,17},{2,18},{3,19},{4,20},{5,21},{6,22},{7,23},{8,9},{9,8... | collective-permute-start | bytes 3244040 | tf_op jit(solution)/shard_map/ppermute | solution.py:83
  42.0 25.7 %collective-permute-start.4 = (bf16[4,32,4224]{2,1,0:T(8,128)(2,1)S(1)}, bf16[4,32,4224]{2,1,0:T(8,128)(2,1)}, u32[]{:S(2)}, u32[]{:S(2)}) collective-permute-start(bf16[4,32,4224]{2,1,0:T(8,128)(2,1)S(1)} %pad_maximum_fusion.refs_0_), channel_id=1, source_target_pairs={{0,1},{1,0},{2,3},{3,2},{4,5},{5,4},{6,7},{7,6},{8,24},{9,25},{10,... | collective-permute-start | bytes 3244040 | tf_op jit(solution)/shard_map/ppermute | solution.py:83
  43.2 78.4 %all-gather.13.cloned.1.call-start = ((), (), s32[]{:S(2)}) async-start(), calls=%async_computation.7 | async-start | bytes 1310720 | tf_op jit(solution)/shard_map/all_gather | solution.py:90
  48.4 35.8 %collective-permute-start.12 = (bf16[4,32,4224]{2,1,0:T(8,128)(2,1)S(1)}, bf16[4,32,4224]{2,1,0:T(8,128)(2,1)}, u32[]{:S(2)}, u32[]{:S(2)}) collective-permute-start(bf16[4,32,4224]{2,1,0:T(8,128)(2,1)S(1)} %pad_maximum_fusion.refs_0_), channel_id=1, source_target_pairs={{0,8},{1,9},{2,10},{3,11},{4,12},{5,13},{6,14},{7,15},{8,0},{9,1},... | collective-permute-start | bytes 3244040 | tf_op jit(solution)/shard_map/ppermute | solution.py:83
  67.6 16.6 %collective-permute-start.11 = (bf16[4,32,4224]{2,1,0:T(8,128)(2,1)S(1)}, bf16[4,32,4224]{2,1,0:T(8,128)(2,1)}, u32[]{:S(2)}, u32[]{:S(2)}) collective-permute-start(bf16[4,32,4224]{2,1,0:T(8,128)(2,1)S(1)} %collective-permute-done.5.refs_2_), channel_id=1, source_target_pairs={{0,8},{1,9},{2,10},{3,11},{4,12},{5,13},{6,14},{7,15},{8,0},{9,1},... | collective-permute-start | bytes 3244040 | tf_op jit(solution)/shard_map/ppermute | solution.py:83
  68.2 16.0 %collective-permute-start.10 = (bf16[4,32,4224]{2,1,0:T(8,128)(2,1)}, bf16[4,32,4224]{2,1,0:T(8,128)(2,1)}, u32[]{:S(2)}, u32[]{:S(2)}) collective-permute-start(bf16[4,32,4224]{2,1,0:T(8,128)(2,1)} %collective-permute-done.4.refs_1_), channel_id=1, source_target_pairs={{0,8},{1,9},{2,10},{3,11},{4,12},{5,13},{6,14},{7,15},{8,0},{9,1},... | collective-permute-start | bytes 3244040 | tf_op jit(solution)/shard_map/ppermute | solution.py:83
  68.3 15.9 %collective-permute-start.9 = (bf16[4,32,4224]{2,1,0:T(8,128)(2,1)}, bf16[4,32,4224]{2,1,0:T(8,128)(2,1)}, u32[]{:S(2)}, u32[]{:S(2)}) collective-permute-start(bf16[4,32,4224]{2,1,0:T(8,128)(2,1)} %collective-permute-done.4.refs_1_), channel_id=1, source_target_pairs={{0,16},{1,17},{2,18},{3,19},{4,20},{5,21},{6,22},{7,23},{8,9},{9,8... | collective-permute-start | bytes 3244040 | tf_op jit(solution)/shard_map/ppermute | solution.py:83
  84.3 25.6 %collective-permute-start.16 = (bf16[4,32,4096]{2,1,0:T(8,128)(2,1)}, bf16[4,32,4096]{2,1,0:T(8,128)(2,1)S(1)}, u32[]{:S(2)}, u32[]{:S(2)}) collective-permute-start(bf16[4,32,4096]{2,1,0:T(8,128)(2,1)} %bitcast.131), channel_id=1, source_target_pairs={{0,16},{1,17},{2,18},{3,19},{4,20},{5,21},{6,22},{7,23},{8,9},{9,8... | collective-permute-start | bytes 3145736 | tf_op jit(solution)/shard_map/ppermute | solution.py:83
  85.2 25.4 %collective-permute-start.15 = (bf16[4,32,4096]{2,1,0:T(8,128)(2,1)}, bf16[4,32,4096]{2,1,0:T(8,128)(2,1)}, u32[]{:S(2)}, u32[]{:S(2)}) collective-permute-start(bf16[4,32,4096]{2,1,0:T(8,128)(2,1)} %bitcast.132), channel_id=1, source_target_pairs={{0,1},{1,0},{2,3},{3,2},{4,5},{5,4},{6,7},{7,6},{8,24},{9,25},{10,... | collective-permute-start | bytes 3145736 | tf_op jit(solution)/shard_map/ppermute | solution.py:83
  86.5 238.2 %reduce-scatter.3.cloned.1.call-start = ((), (), s32[]{:S(2)}) async-start(), calls=%async_computation.2 | async-start | bytes 1310720 | tf_op jit(solution)/shard_map/reduce_scatter | solution.py:105
  87.5 34.1 %collective-permute-start.19 = (bf16[4,32,4096]{2,1,0:T(8,128)(2,1)}, bf16[4,32,4096]{2,1,0:T(8,128)(2,1)}, u32[]{:S(2)}, u32[]{:S(2)}) collective-permute-start(bf16[4,32,4096]{2,1,0:T(8,128)(2,1)} %bitcast.133), channel_id=1, source_target_pairs={{0,8},{1,9},{2,10},{3,11},{4,12},{5,13},{6,14},{7,15},{8,0},{9,1},... | collective-permute-start | bytes 3145736 | tf_op jit(solution)/shard_map/ppermute | solution.py:83
  126.6 36.1 %collective-permute-start.24 = (bf16[4,128,1024]{2,1,0:T(8,128)(2,1)}, bf16[4,128,1024]{2,1,0:T(8,128)(2,1)S(1)}, u32[]{:S(2)}, u32[]{:S(2)}) collective-permute-start(bf16[4,128,1024]{2,1,0:T(8,128)(2,1)} %bitcast.126), channel_id=1, source_target_pairs={{0,8},{1,9},{2,10},{3,11},{4,12},{5,13},{6,14},{7,15},{8,0},{9,1},... | collective-permute-start | bytes 3145736 | tf_op jit(solution)/shard_map/ppermute | solution.py:83
  126.6 36.1 %collective-permute-start.23 = (bf16[4,128,1024]{2,1,0:T(8,128)(2,1)}, bf16[4,128,1024]{2,1,0:T(8,128)(2,1)S(1)}, u32[]{:S(2)}, u32[]{:S(2)}) collective-permute-start(bf16[4,128,1024]{2,1,0:T(8,128)(2,1)} %bitcast.127), channel_id=1, source_target_pairs={{0,16},{1,17},{2,18},{3,19},{4,20},{5,21},{6,22},{7,23},{8,9},{9,8... | collective-permute-start | bytes 3145736 | tf_op jit(solution)/shard_map/ppermute | solution.py:83
  127.3 35.4 %collective-permute-start.22 = (bf16[4,128,1024]{2,1,0:T(8,128)(2,1)}, bf16[4,128,1024]{2,1,0:T(8,128)(2,1)S(1)}, u32[]{:S(2)}, u32[]{:S(2)}) collective-permute-start(bf16[4,128,1024]{2,1,0:T(8,128)(2,1)} %bitcast.128), channel_id=1, source_target_pairs={{0,1},{1,0},{2,3},{3,2},{4,5},{5,4},{6,7},{7,6},{8,24},{9,25},{10,... | collective-permute-start | bytes 3145736 | tf_op jit(solution)/shard_map/ppermute | solution.py:83
  180.7 49.6 %collective-permute-start.30 = (bf16[2,4,128,1024]{3,2,1,0:T(8,128)(2,1)}, bf16[2,4,128,1024]{3,2,1,0:T(8,128)(2,1)S(1)}, u32[]{:S(2)}, u32[]{:S(2)}) collective-permute-start(bf16[2,4,128,1024]{3,2,1,0:T(8,128)(2,1)} %sum_pieces.10), channel_id=1, source_target_pairs={{0,1},{1,0},{2,3},{3,2},{4,5},{5,4},{6,7},{7,6},{8,24},{9,25},{10,... | collective-permute-start | bytes 6291464 | tf_op jit(solution)/shard_map/ppermute | solution.py:83
  244.5 29.8 %collective-permute-start.32 = (bf16[2,4,32,4096]{3,2,1,0:T(8,128)(2,1)}, bf16[2,4,32,4096]{3,2,1,0:T(8,128)(2,1)}, u32[]{:S(2)}, u32[]{:S(2)}) collective-permute-start(bf16[2,4,32,4096]{3,2,1,0:T(8,128)(2,1)} %sum_pieces.12), channel_id=1, source_target_pairs={{0,1},{1,0},{2,3},{3,2},{4,5},{5,4},{6,7},{7,6},{8,24},{9,25},{10,... | collective-permute-start | bytes 6291464 | tf_op jit(solution)/shard_map/ppermute | solution.py:83
  263.5 18.0 %collective-permute-start.33 = (bf16[4,128,1024]{2,1,0:T(8,128)(2,1)S(1)}, bf16[4,128,1024]{2,1,0:T(8,128)(2,1)}, u32[]{:S(2)}, u32[]{:S(2)}) collective-permute-start(bf16[4,128,1024]{2,1,0:T(8,128)(2,1)S(1)} %bitcast.144), channel_id=1, source_target_pairs={{0,16},{1,17},{2,18},{3,19},{4,20},{5,21},{6,22},{7,23},{8,9},{9,8... | collective-permute-start | bytes 3145736 | tf_op jit(solution)/shard_map/ppermute | solution.py:83
  274.3 22.2 %collective-permute-start.34 = (bf16[4,4,32,2048]{3,2,1,0:T(8,128)(2,1)}, bf16[4,4,32,2048]{3,2,1,0:T(8,128)(2,1)S(1)}, u32[]{:S(2)}, u32[]{:S(2)}) collective-permute-start(bf16[4,4,32,2048]{3,2,1,0:T(8,128)(2,1)} %get-tuple-element.233), channel_id=1, source_target_pairs={{0,8},{1,9},{2,10},{3,11},{4,12},{5,13},{6,14},{7,15},{8,0},{9,1},... | collective-permute-start | bytes 6291464 | tf_op jit(solution)/shard_map/ppermute | solution.py:83
  297.8 62.2 %all-gather.7.cloned.1.call-start = ((), (), s32[]{:S(2)}) async-start(), calls=%async_computation.3 | async-start | bytes 1310720 | tf_op jit(solution)/shard_map/all_gather | solution.py:108
  305.7 26.7 %collective-permute-start.44 = (bf16[2,4,32,2048]{3,2,1,0:T(8,128)(2,1)}, bf16[2,4,32,2048]{3,2,1,0:T(8,128)(2,1)S(1)}, u32[]{:S(2)}, u32[]{:S(2)}) collective-permute-start(bf16[2,4,32,2048]{3,2,1,0:T(8,128)(2,1)} %sum_pieces.16), channel_id=1, source_target_pairs={{0,1},{1,0},{2,3},{3,2},{4,5},{5,4},{6,7},{7,6},{8,24},{9,25},{10,... | collective-permute-start | bytes 3145736 | tf_op jit(solution)/shard_map/ppermute | solution.py:83
  306.1 27.1 %collective-permute-start.43 = (bf16[2,4,32,2048]{3,2,1,0:T(8,128)(2,1)S(1)}, bf16[2,4,32,2048]{3,2,1,0:T(8,128)(2,1)S(1)}, u32[]{:S(2)}, u32[]{:S(2)}) collective-permute-start(bf16[2,4,32,2048]{3,2,1,0:T(8,128)(2,1)S(1)} %copy-done.27), channel_id=1, source_target_pairs={{0,1},{1,0},{2,3},{3,2},{4,5},{5,4},{6,7},{7,6},{8,24},{9,25},{10,... | collective-permute-start | bytes 3145736 | tf_op jit(solution)/shard_map/ppermute | solution.py:83
  325.6 45.7 %reduce-scatter.5.cloned.1.call-start = ((), (), s32[]{:S(2)}) async-start(), calls=%async_computation.4 | async-start | bytes 1310720 | tf_op jit(solution)/shard_map/reduce_scatter | solution.py:105
  339.5 20.5 %collective-permute-start.46 = (bf16[4,32,2048]{2,1,0:T(8,128)(2,1)}, bf16[4,32,2048]{2,1,0:T(8,128)(2,1)}, u32[]{:S(2)}, u32[]{:S(2)}) collective-permute-start(bf16[4,32,2048]{2,1,0:T(8,128)(2,1)} %bitcast.38), channel_id=1, source_target_pairs={{0,16},{1,17},{2,18},{3,19},{4,20},{5,21},{6,22},{7,23},{8,9},{9,8... | collective-permute-start | bytes 1572872 | tf_op jit(solution)/shard_map/ppermute | solution.py:83
  339.5 20.5 %collective-permute-start.47 = (bf16[4,32,2048]{2,1,0:T(8,128)(2,1)}, bf16[4,32,2048]{2,1,0:T(8,128)(2,1)}, u32[]{:S(2)}, u32[]{:S(2)}) collective-permute-start(bf16[4,32,2048]{2,1,0:T(8,128)(2,1)} %bitcast.146), channel_id=1, source_target_pairs={{0,16},{1,17},{2,18},{3,19},{4,20},{5,21},{6,22},{7,23},{8,9},{9,8... | collective-permute-start | bytes 1572872 | tf_op jit(solution)/shard_map/ppermute | solution.py:83
  342.6 17.4 %collective-permute-start.48 = (bf16[16,8,2048]{2,1,0:T(8,128)(2,1)}, bf16[16,8,2048]{2,1,0:T(8,128)(2,1)}, u32[]{:S(2)}, u32[]{:S(2)}) collective-permute-start(bf16[16,8,2048]{2,1,0:T(8,128)(2,1)} %constant_dynamic-update-slice_fusion.15), channel_id=1, source_target_pairs={{0,8},{1,9},{2,10},{3,11},{4,12},{5,13},{6,14},{7,15},{8,0},{9,1},... | collective-permute-start | bytes 1572872 | tf_op jit(solution)/shard_map/ppermute | solution.py:83
  342.8 53.5 %all-gather.9.cloned.1.call-start = ((), (), s32[]{:S(2)}) async-start(), calls=%async_computation.5 | async-start | bytes 1310720 | tf_op jit(solution)/shard_map/all_gather | solution.py:108
  343.0 16.9 %collective-permute-start.49 = (f32[8,2,128]{2,0,1:T(8,128)S(1)}, f32[8,2,128]{2,0,1:T(8,128)S(1)}, u32[]{:S(2)}, u32[]{:S(2)}) collective-permute-start(f32[8,2,128]{2,0,1:T(8,128)S(1)} %add.296), channel_id=1, source_target_pairs={{0,16},{1,17},{2,18},{3,19},{4,20},{5,21},{6,22},{7,23},{8,24},{9,... | collective-permute-start | bytes 24584 | tf_op jit(solution)/shard_map/ppermute | solution.py:83
  372.3 19.4 %collective-permute-start.51 = (bf16[32,4224]{1,0:T(8,128)(2,1)S(1)}, bf16[32,4224]{1,0:T(8,128)(2,1)S(1)}, u32[]{:S(2)}, u32[]{:S(2)}) collective-permute-start(bf16[32,4224]{1,0:T(8,128)(2,1)S(1)} %pad_maximum_fusion.4), channel_id=1, source_target_pairs={{0,4},{1,5},{2,6},{3,7},{4,0},{5,1},{6,2},{7,3},{8,12},{9,13},{10,... | collective-permute-start | bytes 811016 | tf_op jit(solution)/shard_map/ppermute | solution.py:83
  375.3 21.0 %collective-permute-start.52 = (bf16[32,4224]{1,0:T(8,128)(2,1)S(1)}, bf16[32,4224]{1,0:T(8,128)(2,1)}, u32[]{:S(2)}, u32[]{:S(2)}) collective-permute-start(bf16[32,4224]{1,0:T(8,128)(2,1)S(1)} %pad_maximum_fusion.5), channel_id=1, source_target_pairs={{0,6},{1,7},{2,0},{3,1},{4,2},{5,3},{6,4},{7,5},{8,14},{9,15},{10,... | collective-permute-start | bytes 811016 | tf_op jit(solution)/shard_map/ppermute | solution.py:83
  (63 other events, 567.9 us)
Sparse Core Ops, SparseCore 0:
  43.3 26.8 all-gather.10
  86.6 25.6 all-gather.12
  297.9 24.8 reduce-scatter.2
  325.7 18.9 all-gather.6
  346.9 24.3 reduce-scatter.4
  372.7 18.6 all-gather.8

commit v5 on v4

--- a/solution.py
+++ b/solution.py
@@ -693,7 +693,11 @@
     gain_one, shift_one, gain_two, shift_two, bias_down = [vectors[:, i].reshape(1, -1).astype(F32) for i in range(5)]
     bias_up = vectors[:, 5:-1].reshape(1, -1).astype(F32)
 
-    near_1, near_2, own_down, partial, gain_one, shift_one = tie(near_1, near_2, own_down, partial, gain_one, shift_one)
+    down_total = jnp.sum(cotangent.astype(F32), axis=0)
+
+    near_1, near_2, own_down, partial, gain_one, shift_one, down_total = tie(
+        near_1, near_2, own_down, partial, gain_one, shift_one, down_total
+    )
     near_12, near_1c, near_2c, near_c = second(near_1), across(near_1), across(near_2), across(near_z)
     scales = 1.0 + plan.sum_x(partial)
     down_z = plan.along_z(own_down)
@@ -745,7 +749,7 @@
         low_theirs, grad_projected, grad_branch, up_got, grad_scale
     )
     low_sent = across(low_theirs)
-    sums = (grad_gain_two, grad_shift_two, jnp.sum(cotangent.astype(F32), axis=0), grad_up_bias)
+    sums = (grad_gain_two, grad_shift_two, down_total, grad_up_bias)
     rows = [grad_scale, jnp.broadcast_to(noise_index[:, None], (seqs, 128)).astype(F32)]
     everyone = jnp.concatenate(rows + [v.reshape(seqs, -1) for v in sums], axis=1).astype(BF16)[None]
     up_fold = sum_pieces(1, (up_keep, 1, 1), (up_sent, 2, 1), (up_got, 1, 1))[0]

time: 425 us -> 426 us (level)
    unnamed x80 -> x82, local copies, waits for them, and re-layouts: 11.5 us -> 12.9 us
  transfers between devices with their start and end apart: 62 -> 62, of which waited for: 24 -> 24; matrix products, arithmetic and copies ran while one was open for 7% -> 8% of each run, Pallas kernels for 47% -> 47%
where the time goes in v5:
time: 426 us; the launch traced here: 422 us
  Pallas kernels  203 us (48%)
  waiting for transfers between devices  109 us (26%)
  starting transfers between devices  44 us (10%)
  local copies, waits for them, and re-layouts  29.9 us (7%)
  other arithmetic  17.7 us (4%)
  between operations  15.1 us (4%)
    pallas_call x19, Pallas kernels, call(): pl.pallas_call(kernel, out_shape=[jax.ShapeDtypeStruct(shape, dtype) for...  203 us
    ppermute x56, waiting for transfers between devices, move(): return lax.ppermute(value, BOTH, pairs)  105 us
    ppermute x56, starting transfers between devices, move(): return lax.ppermute(value, BOTH, pairs)  43.8 us
    unnamed x82, local copies, waits for them, and re-layouts  12.9 us
  transfers between devices with their start and end apart: 62, of which 24 were waited for; matrix products, arithmetic and copies ran while one was open for 8% of the time, Pallas kernels for 47%

profile of v5, /device:TPU:9, one launch (start us, length us, event | category | flops | bytes accessed | tf_op | source)
XLA Modules:
  0.0 422.1 jit_solution(1458727385660442461)
XLA Ops:
  22.3 16.5 %collective-permute-done.2 = bf16[32,4224]{1,0:T(8,128)(2,1)S(1)} collective-permute-done((bf16[32,4224]{1,0:T(8,128)(2,1)S(1)}, bf16[32,4224]{1,0:T(8,128)(2,1)S(1)}, u32[]{:S(2)}, u32[]{:S(2)}) %collective-permute-start.2) | collective-permute-done | bytes 270368 | tf_op jit(solution)/shard_map/ppermute | solution.py:83
  38.7 3.2 collective-permute-done.1
  49.0 2.4 collective-permute-start.12
  51.4 14.2 %collective-permute-done.5.refs_2_ = bf16[4,32,4224]{2,1,0:T(8,128)(2,1)S(1)} collective-permute-done((bf16[4,32,4224]{2,1,0:T(8,128)(2,1)S(1)}, bf16[4,32,4224]{2,1,0:T(8,128)(2,1)S(1)}, u32[]{:S(2)}, u32[]{:S(2)}) %collective-permute-start.5) | collective-permute-done | bytes 1081376 | tf_op jit(solution)/shard_map/ppermute | solution.py:83
  70.3 13.8 %collective-permute-done.13 = f32[8,1024]{1,0:T(8,128)S(1)} collective-permute-done((f32[8,1024]{1,0:T(8,128)S(1)}, f32[8,1024]{1,0:T(8,128)S(1)}, u32[]{:S(2)}, u32[]{:S(2)}) %collective-permute-start.13) | collective-permute-done | bytes 32800 | tf_op jit(solution)/shard_map/ppermute | solution.py:83
  90.5 20.0 %attention.1 = (bf16[32,32,1024]{2,1,0:T(8,128)(2,1)}, bf16[1024,3072]{1,0:T(8,128)(2,1)}, bf16[1024,1024]{1,0:T(8,128)(2,1)}, bf16[32,32,1024]{2,1,0:T(8,128)(2,1)}) custom-call(s32[32]{0:T(128)} %get-tuple-element.324.places, s32[32]{0:T(128)} %get-tuple-element.323.slots.near_slots, bf16[1024,1024]{1,0:T(8,128)(2,1)} %tokens.5, f32[1,1024]{1,0:T(1,128)} %bitcast.157, ...), custom_call_target="tpu_custom_call" | custom-call | tf_op jit(solution)/shard_map/attention/pallas_call | solution.py:152
  112.7 9.3 %middle.1 = (f32[1024,1024]{1,0:T(8,128)}, bf16[1024,1024]{1,0:T(8,128)(2,1)}, bf16[32,32,1024]{2,1,0:T(8,128)(2,1)}) custom-call(s32[32]{0:T(128)} %get-tuple-element.324.places, s32[32]{0:T(128)} %get-tuple-element.323.slots.near_slots, s32[32]{0:T(128)} %fusion.51.slots, bf16[1024,1024]{1,0:T(8,128)(2,1)} %tokens.5, ...), custom_call_target="tpu_custom_call" | custom-call | tf_op jit(solution)/shard_map/middle/pallas_call | solution.py:152
  122.1 3.9 collective-permute-done.17.refs_3_.refs_11_
  131.3 32.0 %up.1 = (bf16[1024,4096]{1,0:T(8,128)(2,1)}, bf16[1024,4096]{1,0:T(8,128)(2,1)}, bf16[4,4,128,1024]{3,2,1,0:T(8,128)(2,1)}, bf16[2,4,128,1024]{3,2,1,0:T(8,128)(2,1)}, bf16[2,4,128,1024]{3,2,1,0:T(8,128)(2,1)}) custom-call(s32[32]{0:T(128)} %multiply_add_fusion.places, s32[32]{0:T(128)} %fusion.51.slots, bf16[1024,1024]{1,0:T(8,128)(2,1)} %get-tuple-element.173.act, ...), custom_call_target="tpu_custom_call" | custom-call | tf_op jit(solution)/shard_map/up/pallas_call | solution.py:152
  166.1 7.4 %collective-permute-done.27.refs_6_ = bf16[4,128,1024]{2,1,0:T(8,128)(2,1)S(1)} collective-permute-done((bf16[4,128,1024]{2,1,0:T(8,128)(2,1)}, bf16[4,128,1024]{2,1,0:T(8,128)(2,1)S(1)}, u32[]{:S(2)}, u32[]{:S(2)}) %collective-permute-start.27) | collective-permute-done | bytes 1048608 | tf_op jit(solution)/shard_map/ppermute | solution.py:83
  178.0 3.4 sum_pieces.10
  182.6 2.9 collective-permute-done.29.refs_7_
  186.5 44.6 %feed_back.1 = (bf16[4,4,32,4096]{3,2,1,0:T(8,128)(2,1)}, bf16[2,4,32,4096]{3,2,1,0:T(8,128)(2,1)}, bf16[2,4,32,4096]{3,2,1,0:T(8,128)(2,1)}, f32[1,4096]{1,0:T(...) custom-call(s32[32]{0:T(128)} %multiply_add_fusion.places, ...), custom_call_target="tpu_custom_call" | custom-call | tf_op jit(solution)/shard_map/feed_back/pallas_call | solution.py:152
  232.5 2.9 sum_pieces.11
  235.4 4.3 %collective-permute-done.31.refs_1_ = bf16[4,4,32,4096]{3,2,1,0:T(8,128)(2,1)S(1)} collective-permute-done((bf16[4,4,32,4096]{3,2,1,0:T(8,128)(2,1)}, bf16[4,4,32,4096]{3,2,1,0:T(8,128)(2,1)S(1)}, u32[]{:S(2)}, u32[]{:S(2)}) %collective-permute-start.31) | collective-permute-done | bytes 4194336 | tf_op jit(solution)/shard_map/ppermute | solution.py:83
  241.7 3.4 sum_pieces.12
  246.1 17.8 %attention_grad.1.grad_projected = bf16[1024,3072]{1,0:T(8,128)(2,1)} custom-call(s32[32]{0:T(128)} %get-tuple-element.324.places, bf16[1024,1024]{1,0:T(8,128)(2,1)} %get-tuple-element.231.grad_branch, bf16[1024,3072]{1,0:T(8,128)(2,1)} %get-tuple-element.208.qkv, f32[256,128]{1,0:T(8,128)} %bitcast.139, f32[256,128]{1,0:T(8,128)} %bitcast.141, ...), custom_call_target="tpu_custom_call" | custom-call | tf_op jit(solution)/shard_map/attention_grad/pallas_call | solution.py:152
  264.9 9.5 %near_grad.2 = (bf16[4,4,32,2048]{3,2,1,0:T(8,128)(2,1)}, bf16[2,4,32,2048]{3,2,1,0:T(8,128)(2,1)}, bf16[2,4,32,2048]{3,2,1,0:T(8,128)(2,1)}) custom-call(bf16[32,32,1024]{2,1,0:T(8,128)(2,1)} %get-tuple-element.183.act_one, bf16[1024,3072]{1,0:T(8,128)(2,1)} %attention_grad.1.grad_projected, bf16[32,32,1024]{2,1,0:T(8,128)(2,1)} %get-tuple-element.212.attended, ...), custom_call_target="tpu_custom_call" | custom-call | tf_op jit(solution)/shard_map/near_grad/pallas_call | solution.py:152
  277.1 2.9 sum_pieces.13
  284.3 3.2 sum_pieces.14
  287.4 9.5 %near_grad.3 = (bf16[4,4,32,2048]{3,2,1,0:T(8,128)(2,1)}, bf16[2,4,32,2048]{3,2,1,0:T(8,128)(2,1)}, bf16[2,4,32,2048]{3,2,1,0:T(8,128)(2,1)}) custom-call(bf16[32,32,1024]{2,1,0:T(8,128)(2,1)} %get-tuple-element.183.act_one, bf16[1024,3072]{1,0:T(8,128)(2,1)} %attention_grad.1.grad_projected, bf16[32,32,1024]{2,1,0:T(8,128)(2,1)} %get-tuple-element.212.attended, ...), custom_call_target="tpu_custom_call" | custom-call | tf_op jit(solution)/shard_map/near_grad/pallas_call | solution.py:152
  299.2 2.4 sum_pieces.15
  303.5 2.7 sum_pieces.16
  307.8 15.4 %token_grad.1 = (f32[1024,1024]{1,0:T(8,128)}, f32[1,1024]{1,0:T(1,128)}, f32[1,1024]{1,0:T(1,128)}) custom-call(s32[32]{0:T(128)} %get-tuple-element.324.places, bf16[1024,3072]{1,0:T(8,128)(2,1)} %attention_grad.1.grad_projected, bf16[1024,1024]{1,0:T(8,128)(2,1)} %tokens.5, f32[1024,1024]{1,0:T(8,128)} %get-tuple-element.248.grad_middle, ...), custom_call_target="tpu_custom_call" | custom-call | tf_op jit(solution)/shard_map/token_grad/pallas_call | solution.py:152
  326.8 3.2 sum_pieces.17
  344.3 16.1 %output.1 = bf16[1024,1024]{1,0:T(8,128)(2,1)} custom-call(s32[32]{0:T(128)} %multiply_add_fusion.places, bf16[1024,4096]{1,0:T(8,128)(2,1)} %get-tuple-element.182.hidden, f32[1024,1024]{1,0:T(8,128)} %get-tuple-element.262.middle, f32[1,1024]{1,0:T(1,128)} %bitcast.165, bf16[4,128,1024]{2,1,0:T(8,128)(2,1)} %bitcast.130, bf16[4,128,1024]{2,1,0:T(8,128)(2,1)} %copy-done.12, ...), custom_call_target="tpu_custom_call" | custom-call | tf_op jit(solution)/shard_map/output/pallas_call | solution.py:152
  361.2 2.4 fusion.4
  363.7 2.4 fusion.5
  367.3 4.5 %reduce-scatter.5.cloned.1.call-done = bf16[1,32,4096]{2,1,0:T(8,128)(2,1)} async-done(((bf16[4,32,4096]{2,1,0:T(8,128)(2,1)}), bf16[1,32,4096]{2,1,0:T(8,128)(2,1)}) %reduce-scatter.5.cloned.1.call-update) | async-done | bytes 262160 | tf_op jit(solution)/shard_map/reduce_scatter | solution.py:105
  378.6 13.6 %collective-permute-done.51 = bf16[32,4224]{1,0:T(8,128)(2,1)S(1)} collective-permute-done((bf16[32,4224]{1,0:T(8,128)(2,1)S(1)}, bf16[32,4224]{1,0:T(8,128)(2,1)S(1)}, u32[]{:S(2)}, u32[]{:S(2)}) %collective-permute-start.51) | collective-permute-done | bytes 270368 | tf_op jit(solution)/shard_map/ppermute | solution.py:83
  392.2 4.8 %collective-permute-done.52 = bf16[32,4224]{1,0:T(8,128)(2,1)} collective-permute-done((bf16[32,4224]{1,0:T(8,128)(2,1)S(1)}, bf16[32,4224]{1,0:T(8,128)(2,1)}, u32[]{:S(2)}, u32[]{:S(2)}) %collective-permute-start.52) | collective-permute-done | bytes 270368 | tf_op jit(solution)/shard_map/ppermute | solution.py:83
  402.1 3.6 collective-permute-done.54
  (282 shorter events, 108.7 us)
Async XLA Ops:
  7.2 77.5 %all-gather.11.cloned.1.call-start = ((), (), s32[]{:S(2)}) async-start(), calls=%async_computation.6 | async-start | bytes 1310720 | tf_op jit(solution)/shard_map/all_gather | solution.py:90
  16.5 22.2 %collective-permute-start.2 = (bf16[32,4224]{1,0:T(8,128)(2,1)S(1)}, bf16[32,4224]{1,0:T(8,128)(2,1)S(1)}, u32[]{:S(2)}, u32[]{:S(2)}) collective-permute-start(bf16[32,4224]{1,0:T(8,128)(2,1)S(1)} %fusion.3), channel_id=1, source_target_pairs={{0,4},{1,5},{2,6},{3,7},{4,0},{5,1},{6,2},{7,3},{8,12},{9,13},{10,... | collective-permute-start | bytes 811016 | tf_op jit(solution)/shard_map/ppermute | solution.py:83
  17.6 24.3 %collective-permute-start.1 = (bf16[32,4224]{1,0:T(8,128)(2,1)S(1)}, bf16[32,4224]{1,0:T(8,128)(2,1)S(1)}, u32[]{:S(2)}, u32[]{:S(2)}) collective-permute-start(bf16[32,4224]{1,0:T(8,128)(2,1)S(1)} %fusion.3), channel_id=1, source_target_pairs={{0,6},{1,7},{2,0},{3,1},{4,2},{5,3},{6,4},{7,5},{8,14},{9,15},{10,... | collective-permute-start | bytes 811016 | tf_op jit(solution)/shard_map/ppermute | solution.py:83
  42.1 23.5 %collective-permute-start.5 = (bf16[4,32,4224]{2,1,0:T(8,128)(2,1)S(1)}, bf16[4,32,4224]{2,1,0:T(8,128)(2,1)S(1)}, u32[]{:S(2)}, u32[]{:S(2)}) collective-permute-start(bf16[4,32,4224]{2,1,0:T(8,128)(2,1)S(1)} %pad_maximum_fusion.refs_0_), channel_id=1, source_target_pairs={{0,16},{1,17},{2,18},{3,19},{4,20},{5,21},{6,22},{7,23},{8,9},{9,8... | collective-permute-start | bytes 3244040 | tf_op jit(solution)/shard_map/ppermute | solution.py:83
  42.4 25.3 %collective-permute-start.4 = (bf16[4,32,4224]{2,1,0:T(8,128)(2,1)S(1)}, bf16[4,32,4224]{2,1,0:T(8,128)(2,1)}, u32[]{:S(2)}, u32[]{:S(2)}) collective-permute-start(bf16[4,32,4224]{2,1,0:T(8,128)(2,1)S(1)} %pad_maximum_fusion.refs_0_), channel_id=1, source_target_pairs={{0,1},{1,0},{2,3},{3,2},{4,5},{5,4},{6,7},{7,6},{8,24},{9,25},{10,... | collective-permute-start | bytes 3244040 | tf_op jit(solution)/shard_map/ppermute | solution.py:83
  43.7 78.4 %all-gather.13.cloned.1.call-start = ((), (), s32[]{:S(2)}) async-start(), calls=%async_computation.7 | async-start | bytes 1310720 | tf_op jit(solution)/shard_map/all_gather | solution.py:90
  49.0 35.7 %collective-permute-start.12 = (bf16[4,32,4224]{2,1,0:T(8,128)(2,1)S(1)}, bf16[4,32,4224]{2,1,0:T(8,128)(2,1)}, u32[]{:S(2)}, u32[]{:S(2)}) collective-permute-start(bf16[4,32,4224]{2,1,0:T(8,128)(2,1)S(1)} %pad_maximum_fusion.refs_0_), channel_id=1, source_target_pairs={{0,8},{1,9},{2,10},{3,11},{4,12},{5,13},{6,14},{7,15},{8,0},{9,1},... | collective-permute-start | bytes 3244040 | tf_op jit(solution)/shard_map/ppermute | solution.py:83
  67.8 17.0 %collective-permute-start.11 = (bf16[4,32,4224]{2,1,0:T(8,128)(2,1)S(1)}, bf16[4,32,4224]{2,1,0:T(8,128)(2,1)}, u32[]{:S(2)}, u32[]{:S(2)}) collective-permute-start(bf16[4,32,4224]{2,1,0:T(8,128)(2,1)S(1)} %collective-permute-done.5.refs_2_), channel_id=1, source_target_pairs={{0,8},{1,9},{2,10},{3,11},{4,12},{5,13},{6,14},{7,15},{8,0},{9,1},... | collective-permute-start | bytes 3244040 | tf_op jit(solution)/shard_map/ppermute | solution.py:83
  68.7 16.0 %collective-permute-start.10 = (bf16[4,32,4224]{2,1,0:T(8,128)(2,1)}, bf16[4,32,4224]{2,1,0:T(8,128)(2,1)}, u32[]{:S(2)}, u32[]{:S(2)}) collective-permute-start(bf16[4,32,4224]{2,1,0:T(8,128)(2,1)} %collective-permute-done.4.refs_1_), channel_id=1, source_target_pairs={{0,8},{1,9},{2,10},{3,11},{4,12},{5,13},{6,14},{7,15},{8,0},{9,1},... | collective-permute-start | bytes 3244040 | tf_op jit(solution)/shard_map/ppermute | solution.py:83
  68.8 16.0 %collective-permute-start.9 = (bf16[4,32,4224]{2,1,0:T(8,128)(2,1)}, bf16[4,32,4224]{2,1,0:T(8,128)(2,1)}, u32[]{:S(2)}, u32[]{:S(2)}) collective-permute-start(bf16[4,32,4224]{2,1,0:T(8,128)(2,1)} %collective-permute-done.4.refs_1_), channel_id=1, source_target_pairs={{0,16},{1,17},{2,18},{3,19},{4,20},{5,21},{6,22},{7,23},{8,9},{9,8... | collective-permute-start | bytes 3244040 | tf_op jit(solution)/shard_map/ppermute | solution.py:83
  84.8 25.7 %collective-permute-start.16 = (bf16[4,32,4096]{2,1,0:T(8,128)(2,1)}, bf16[4,32,4096]{2,1,0:T(8,128)(2,1)S(1)}, u32[]{:S(2)}, u32[]{:S(2)}) collective-permute-start(bf16[4,32,4096]{2,1,0:T(8,128)(2,1)} %bitcast.131), channel_id=1, source_target_pairs={{0,16},{1,17},{2,18},{3,19},{4,20},{5,21},{6,22},{7,23},{8,9},{9,8... | collective-permute-start | bytes 3145736 | tf_op jit(solution)/shard_map/ppermute | solution.py:83
  85.8 25.5 %collective-permute-start.15 = (bf16[4,32,4096]{2,1,0:T(8,128)(2,1)}, bf16[4,32,4096]{2,1,0:T(8,128)(2,1)}, u32[]{:S(2)}, u32[]{:S(2)}) collective-permute-start(bf16[4,32,4096]{2,1,0:T(8,128)(2,1)} %bitcast.132), channel_id=1, source_target_pairs={{0,1},{1,0},{2,3},{3,2},{4,5},{5,4},{6,7},{7,6},{8,24},{9,25},{10,... | collective-permute-start | bytes 3145736 | tf_op jit(solution)/shard_map/ppermute | solution.py:83
  87.0 238.1 %reduce-scatter.3.cloned.1.call-start = ((), (), s32[]{:S(2)}) async-start(), calls=%async_computation.2 | async-start | bytes 1310720 | tf_op jit(solution)/shard_map/reduce_scatter | solution.py:105
  88.1 34.0 %collective-permute-start.19 = (bf16[4,32,4096]{2,1,0:T(8,128)(2,1)}, bf16[4,32,4096]{2,1,0:T(8,128)(2,1)}, u32[]{:S(2)}, u32[]{:S(2)}) collective-permute-start(bf16[4,32,4096]{2,1,0:T(8,128)(2,1)} %bitcast.133), channel_id=1, source_target_pairs={{0,8},{1,9},{2,10},{3,11},{4,12},{5,13},{6,14},{7,15},{8,0},{9,1},... | collective-permute-start | bytes 3145736 | tf_op jit(solution)/shard_map/ppermute | solution.py:83
  127.2 36.1 %collective-permute-start.24 = (bf16[4,128,1024]{2,1,0:T(8,128)(2,1)}, bf16[4,128,1024]{2,1,0:T(8,128)(2,1)S(1)}, u32[]{:S(2)}, u32[]{:S(2)}) collective-permute-start(bf16[4,128,1024]{2,1,0:T(8,128)(2,1)} %bitcast.126), channel_id=1, source_target_pairs={{0,8},{1,9},{2,10},{3,11},{4,12},{5,13},{6,14},{7,15},{8,0},{9,1},... | collective-permute-start | bytes 3145736 | tf_op jit(solution)/shard_map/ppermute | solution.py:83
  127.2 36.1 %collective-permute-start.23 = (bf16[4,128,1024]{2,1,0:T(8,128)(2,1)}, bf16[4,128,1024]{2,1,0:T(8,128)(2,1)S(1)}, u32[]{:S(2)}, u32[]{:S(2)}) collective-permute-start(bf16[4,128,1024]{2,1,0:T(8,128)(2,1)} %bitcast.127), channel_id=1, source_target_pairs={{0,16},{1,17},{2,18},{3,19},{4,20},{5,21},{6,22},{7,23},{8,9},{9,8... | collective-permute-start | bytes 3145736 | tf_op jit(solution)/shard_map/ppermute | solution.py:83
  127.8 35.5 %collective-permute-start.22 = (bf16[4,128,1024]{2,1,0:T(8,128)(2,1)}, bf16[4,128,1024]{2,1,0:T(8,128)(2,1)S(1)}, u32[]{:S(2)}, u32[]{:S(2)}) collective-permute-start(bf16[4,128,1024]{2,1,0:T(8,128)(2,1)} %bitcast.128), channel_id=1, source_target_pairs={{0,1},{1,0},{2,3},{3,2},{4,5},{5,4},{6,7},{7,6},{8,24},{9,25},{10,... | collective-permute-start | bytes 3145736 | tf_op jit(solution)/shard_map/ppermute | solution.py:83
  181.4 49.7 %collective-permute-start.30 = (bf16[2,4,128,1024]{3,2,1,0:T(8,128)(2,1)}, bf16[2,4,128,1024]{3,2,1,0:T(8,128)(2,1)S(1)}, u32[]{:S(2)}, u32[]{:S(2)}) collective-permute-start(bf16[2,4,128,1024]{3,2,1,0:T(8,128)(2,1)} %sum_pieces.10), channel_id=1, source_target_pairs={{0,1},{1,0},{2,3},{3,2},{4,5},{5,4},{6,7},{7,6},{8,24},{9,25},{10,... | collective-permute-start | bytes 6291464 | tf_op jit(solution)/shard_map/ppermute | solution.py:83
  245.1 29.3 %collective-permute-start.32 = (bf16[2,4,32,4096]{3,2,1,0:T(8,128)(2,1)}, bf16[2,4,32,4096]{3,2,1,0:T(8,128)(2,1)S(1)}, u32[]{:S(2)}, u32[]{:S(2)}) collective-permute-start(bf16[2,4,32,4096]{3,2,1,0:T(8,128)(2,1)} %sum_pieces.12), channel_id=1, source_target_pairs={{0,1},{1,0},{2,3},{3,2},{4,5},{5,4},{6,7},{7,6},{8,24},{9,25},{10,... | collective-permute-start | bytes 6291464 | tf_op jit(solution)/shard_map/ppermute | solution.py:83
  264.0 18.1 %collective-permute-start.33 = (bf16[4,128,1024]{2,1,0:T(8,128)(2,1)S(1)}, bf16[4,128,1024]{2,1,0:T(8,128)(2,1)S(1)}, u32[]{:S(2)}, u32[]{:S(2)}) collective-permute-start(bf16[4,128,1024]{2,1,0:T(8,128)(2,1)S(1)} %bitcast.145), channel_id=1, source_target_pairs={{0,16},{1,17},{2,18},{3,19},{4,20},{5,21},{6,22},{7,23},{8,9},{9,8... | collective-permute-start | bytes 3145736 | tf_op jit(solution)/shard_map/ppermute | solution.py:83
  275.8 21.3 %collective-permute-start.34 = (bf16[4,4,32,2048]{3,2,1,0:T(8,128)(2,1)}, bf16[4,4,32,2048]{3,2,1,0:T(8,128)(2,1)S(1)}, u32[]{:S(2)}, u32[]{:S(2)}) collective-permute-start(bf16[4,4,32,2048]{3,2,1,0:T(8,128)(2,1)} %get-tuple-element.233), channel_id=1, source_target_pairs={{0,8},{1,9},{2,10},{3,11},{4,12},{5,13},{6,14},{7,15},{8,0},{9,1},... | collective-permute-start | bytes 6291464 | tf_op jit(solution)/shard_map/ppermute | solution.py:83
  298.3 62.2 %all-gather.7.cloned.1.call-start = ((), (), s32[]{:S(2)}) async-start(), calls=%async_computation.3 | async-start | bytes 1310720 | tf_op jit(solution)/shard_map/all_gather | solution.py:108
  306.2 26.8 %collective-permute-start.44 = (bf16[2,4,32,2048]{3,2,1,0:T(8,128)(2,1)}, bf16[2,4,32,2048]{3,2,1,0:T(8,128)(2,1)S(1)}, u32[]{:S(2)}, u32[]{:S(2)}) collective-permute-start(bf16[2,4,32,2048]{3,2,1,0:T(8,128)(2,1)} %sum_pieces.16), channel_id=1, source_target_pairs={{0,1},{1,0},{2,3},{3,2},{4,5},{5,4},{6,7},{7,6},{8,24},{9,25},{10,... | collective-permute-start | bytes 3145736 | tf_op jit(solution)/shard_map/ppermute | solution.py:83
  306.7 27.1 %collective-permute-start.43 = (bf16[2,4,32,2048]{3,2,1,0:T(8,128)(2,1)S(1)}, bf16[2,4,32,2048]{3,2,1,0:T(8,128)(2,1)S(1)}, u32[]{:S(2)}, u32[]{:S(2)}) collective-permute-start(bf16[2,4,32,2048]{3,2,1,0:T(8,128)(2,1)S(1)} %copy-done.29), channel_id=1, source_target_pairs={{0,1},{1,0},{2,3},{3,2},{4,5},{5,4},{6,7},{7,6},{8,24},{9,25},{10,... | collective-permute-start | bytes 3145736 | tf_op jit(solution)/shard_map/ppermute | solution.py:83
  326.0 45.8 %reduce-scatter.5.cloned.1.call-start = ((), (), s32[]{:S(2)}) async-start(), calls=%async_computation.4 | async-start | bytes 1310720 | tf_op jit(solution)/shard_map/reduce_scatter | solution.py:105
  340.1 20.4 %collective-permute-start.46 = (bf16[4,32,2048]{2,1,0:T(8,128)(2,1)}, bf16[4,32,2048]{2,1,0:T(8,128)(2,1)}, u32[]{:S(2)}, u32[]{:S(2)}) collective-permute-start(bf16[4,32,2048]{2,1,0:T(8,128)(2,1)} %bitcast.38), channel_id=1, source_target_pairs={{0,16},{1,17},{2,18},{3,19},{4,20},{5,21},{6,22},{7,23},{8,9},{9,8... | collective-permute-start | bytes 1572872 | tf_op jit(solution)/shard_map/ppermute | solution.py:83
  340.1 20.4 %collective-permute-start.47 = (bf16[4,32,2048]{2,1,0:T(8,128)(2,1)}, bf16[4,32,2048]{2,1,0:T(8,128)(2,1)}, u32[]{:S(2)}, u32[]{:S(2)}) collective-permute-start(bf16[4,32,2048]{2,1,0:T(8,128)(2,1)} %bitcast.147), channel_id=1, source_target_pairs={{0,16},{1,17},{2,18},{3,19},{4,20},{5,21},{6,22},{7,23},{8,9},{9,8... | collective-permute-start | bytes 1572872 | tf_op jit(solution)/shard_map/ppermute | solution.py:83
  343.2 17.3 %collective-permute-start.48 = (bf16[16,8,2048]{2,1,0:T(8,128)(2,1)}, bf16[16,8,2048]{2,1,0:T(8,128)(2,1)}, u32[]{:S(2)}, u32[]{:S(2)}) collective-permute-start(bf16[16,8,2048]{2,1,0:T(8,128)(2,1)} %constant_dynamic-update-slice_fusion.15), channel_id=1, source_target_pairs={{0,8},{1,9},{2,10},{3,11},{4,12},{5,13},{6,14},{7,15},{8,0},{9,1},... | collective-permute-start | bytes 1572872 | tf_op jit(solution)/shard_map/ppermute | solution.py:83
  343.3 53.6 %all-gather.9.cloned.1.call-start = ((), (), s32[]{:S(2)}) async-start(), calls=%async_computation.5 | async-start | bytes 1310720 | tf_op jit(solution)/shard_map/all_gather | solution.py:108
  343.4 17.0 %collective-permute-start.49 = (f32[8,2,128]{2,0,1:T(8,128)S(1)}, f32[8,2,128]{2,0,1:T(8,128)S(1)}, u32[]{:S(2)}, u32[]{:S(2)}) collective-permute-start(f32[8,2,128]{2,0,1:T(8,128)S(1)} %add.296), channel_id=1, source_target_pairs={{0,16},{1,17},{2,18},{3,19},{4,20},{5,21},{6,22},{7,23},{8,24},{9,... | collective-permute-start | bytes 24584 | tf_op jit(solution)/shard_map/ppermute | solution.py:83
  372.9 19.3 %collective-permute-start.51 = (bf16[32,4224]{1,0:T(8,128)(2,1)S(1)}, bf16[32,4224]{1,0:T(8,128)(2,1)S(1)}, u32[]{:S(2)}, u32[]{:S(2)}) collective-permute-start(bf16[32,4224]{1,0:T(8,128)(2,1)S(1)} %pad_maximum_fusion.4), channel_id=1, source_target_pairs={{0,4},{1,5},{2,6},{3,7},{4,0},{5,1},{6,2},{7,3},{8,12},{9,13},{10,... | collective-permute-start | bytes 811016 | tf_op jit(solution)/shard_map/ppermute | solution.py:83
  375.8 21.2 %collective-permute-start.52 = (bf16[32,4224]{1,0:T(8,128)(2,1)S(1)}, bf16[32,4224]{1,0:T(8,128)(2,1)}, u32[]{:S(2)}, u32[]{:S(2)}) collective-permute-start(bf16[32,4224]{1,0:T(8,128)(2,1)S(1)} %pad_maximum_fusion.5), channel_id=1, source_target_pairs={{0,6},{1,7},{2,0},{3,1},{4,2},{5,3},{6,4},{7,5},{8,14},{9,15},{10,... | collective-permute-start | bytes 811016 | tf_op jit(solution)/shard_map/ppermute | solution.py:83
  (64 other events, 532.6 us)
Sparse Core Ops, SparseCore 0:
  43.8 27.3 all-gather.10
  87.2 25.5 all-gather.12
  298.4 24.7 reduce-scatter.2
  326.2 18.3 all-gather.6
  346.8 24.9 reduce-scatter.4
  373.2 18.6 all-gather.8
